TPU v7x, 32 devices: a whole 2x2x4 slice. The times are simulated.
32 devices in a mesh: ctx: 8 (over y, x, core), dp: 4 (over z).
Axes of the slice: x: 2, y: 2, z: 4, core: 2. Of those that a mesh axis runs over, the one named last changes fastest.
Arguments:
- queries: bfloat16 [4, 1024, 1536], P('dp', 'ctx'), as said below
- keys: bfloat16 [4, 1024, 1536], P('dp', 'ctx'), as said below
- values: bfloat16 [4, 1024, 1536], P('dp', 'ctx'), may hold values from -6 to 6
- tangent_queries: bfloat16 [4, 1024, 1536], P('dp', 'ctx'), may hold values from -6 to 6
- tangent_keys: bfloat16 [4, 1024, 1536], P('dp', 'ctx'), may hold values from -6 to 6
- tangent_values: bfloat16 [4, 1024, 1536], P('dp', 'ctx'), may hold values from -6 to 6
- clip_ids: int32 [4, 1024], P('dp', 'ctx'), may hold values from 0 to 3, never falling along the last dimension, each value on 1 to 512 neighbouring positions
- block_order: int32 [8], replicated, may hold values from 0 to 7, each once
- out_weight: bfloat16 [1536, 3072], replicated, may hold values from -0.15625 to 0.15625
- layer_scale: float32 [3072], replicated, may hold values from 0.1 to 1.9
- cotangent: bfloat16 [4, 1024, 3072], P('dp', 'ctx'), as said below
Outputs:
- tangent_branch: bfloat16 [4, 1024, 3072], P('dp', 'ctx')
- scale_grad: float32 [3072], replicated
Inputs may be any that keep to these rules, and one draw needn't show every extreme that they name: `clip_ids`: ids never fall along a sample's rows; each of the 4 clips is a run of consecutive rows. `block_order`: each block number appears once. `queries`: real-valued. `keys`: real-valued. `cotangent`: real-valued.
All inputs are finite; a program needn't handle non-finite values.
Results may differ from a plain program's by a relative error of at most 0.02.
The roundings to bfloat16 on the way count: a program that leaves them out, or rounds other values in their place, can miss the bound.
Values may be sent and summed in bfloat16 or wider, within the bound.
No kernel may reach another device: no remote copies, remote signals or barrier semaphores. Data moves between devices by JAX's collectives and lax.ppermute only.
A program may use at most 192 MiB of HBM per device.

v0:
```python
import math

import jax
import jax.numpy as jnp
from jax import lax
from jax.sharding import PartitionSpec as P

HEADS = 12


def rotate(x, pos, half_dim):
    frequency = 10000.0 ** (-jnp.arange(half_dim, dtype=jnp.float32) / half_dim)
    angles = pos.astype(jnp.float32)[:, None] * frequency[None, :]
    cosine = jnp.cos(angles)[:, None, :]
    sine_part = jnp.sin(angles)[:, None, :]
    front_part = x[..., :half_dim]
    back_part = x[..., half_dim:]
    return jnp.concatenate(
        [front_part * cosine - back_part * sine_part, back_part * cosine + front_part * sine_part],
        axis=-1,
    )


def make_attend(query_rot, tquery_rot, query_ids, scale):

    def attend(carry, block):
        best, total, weighted, primal_acc, slope_acc, spread_acc = carry
        key_blk, value_blk, tkey_blk, tvalue_blk, key_ids = block
        scores = (
            jnp.einsum("hqd,hkd->hqk", query_rot, key_blk, preferred_element_type=jnp.float32)
            * scale
        )
        same_clip = query_ids[:, None] == key_ids[None, :]
        scores = jnp.where(same_clip[None], scores, -jnp.inf)
        slopes = (
            jnp.einsum("hqd,hkd->hqk", tquery_rot, key_blk, preferred_element_type=jnp.float32)
            + jnp.einsum("hqd,hkd->hqk", query_rot, tkey_blk, preferred_element_type=jnp.float32)
        ) * scale
        new_best = jnp.maximum(best, jnp.max(scores, axis=-1))
        factor = jnp.exp(best - new_best)
        weights = jnp.exp(scores - new_best[..., None])
        tilted = weights * slopes
        total = total * factor + jnp.sum(weights, axis=-1)
        weighted = weighted * factor + jnp.sum(tilted, axis=-1)
        weights_b = weights.astype(jnp.bfloat16)
        tilted_b = tilted.astype(jnp.bfloat16)
        primal_acc = primal_acc * factor[..., None] + jnp.einsum(
            "hqk,hkd->hqd", weights_b, value_blk, preferred_element_type=jnp.float32
        )
        slope_acc = slope_acc * factor[..., None] + jnp.einsum(
            "hqk,hkd->hqd", tilted_b, value_blk, preferred_element_type=jnp.float32
        )
        spread_acc = spread_acc * factor[..., None] + jnp.einsum(
            "hqk,hkd->hqd", weights_b, tvalue_blk, preferred_element_type=jnp.float32
        )
        return ((new_best, total, weighted, primal_acc, slope_acc, spread_acc), None)

    return attend


def start_states(heads, rows, head_dim):
    zeros_rows = jnp.zeros((heads, rows), jnp.float32)
    zeros_heads = jnp.zeros((heads, rows, head_dim), jnp.float32)
    return (
        jnp.full((heads, rows), -1e30, jnp.float32),
        zeros_rows,
        zeros_rows,
        zeros_heads,
        zeros_heads,
        zeros_heads,
    )


def local(
    queries,
    keys,
    values,
    tangent_queries,
    tangent_keys,
    tangent_values,
    clip_ids,
    block_order,
    out_weight,
    layer_scale,
    cotangent,
):
    tok_rows = queries.shape[1]
    heads = HEADS
    head_dim = queries.shape[2] // heads
    scale = head_dim ** (-0.5)
    cycle_index = lax.axis_index("ctx")
    positions = block_order[cycle_index] * tok_rows + jnp.arange(tok_rows, dtype=jnp.int32)

    def heads_first(x, turned):
        y = x[0].reshape(tok_rows, heads, head_dim)
        if turned:
            y = rotate(y.astype(jnp.float32), positions, head_dim // 2).astype(jnp.bfloat16)
        return jnp.transpose(y, (1, 0, 2))

    query_rot = heads_first(queries, True)
    key_rot = heads_first(keys, True)
    value_heads = heads_first(values, False)
    tquery_rot = heads_first(tangent_queries, True)
    tkey_rot = heads_first(tangent_keys, True)
    tvalue_heads = heads_first(tangent_values, False)
    all_ids = lax.all_gather(clip_ids, "ctx", axis=1, tiled=True)[0]
    own_ids = clip_ids[0]
    attend = make_attend(query_rot, tquery_rot, own_ids, scale)
    carry = start_states(heads, tok_rows, head_dim)
    key_part = lax.all_gather(key_rot, "ctx", axis=1, tiled=True)
    value_part = lax.all_gather(value_heads, "ctx", axis=1, tiled=True)
    tkey_part = lax.all_gather(tkey_rot, "ctx", axis=1, tiled=True)
    tvalue_part = lax.all_gather(tvalue_heads, "ctx", axis=1, tiled=True)
    count = key_part.shape[1]
    block_rows = math.gcd(count, tok_rows)
    blocks = count // block_rows

    def split_blocks(x):
        return jnp.transpose(x.reshape(heads, blocks, block_rows, head_dim), (1, 0, 2, 3))

    stacked = (
        split_blocks(key_part),
        split_blocks(value_part),
        split_blocks(tkey_part),
        split_blocks(tvalue_part),
        all_ids.reshape(blocks, block_rows),
    )
    carry, unused = lax.scan(attend, carry, stacked)
    best, total, weighted, primal_acc, slope_acc, spread_acc = carry
    mean_out = primal_acc / total[..., None]
    tangent_heads = (
        (slope_acc + spread_acc) / total[..., None] - (weighted / total)[..., None] * mean_out
    ).astype(jnp.bfloat16)
    tangent_rows = jnp.transpose(tangent_heads, (1, 0, 2)).reshape(tok_rows, heads * head_dim)
    projected = jnp.dot(tangent_rows, out_weight, preferred_element_type=jnp.float32)
    branch = (layer_scale * projected).astype(jnp.bfloat16)[None]
    partial_grad = jnp.sum(cotangent[0].astype(jnp.float32) * projected, axis=0)
    summed = lax.psum(partial_grad, ("ctx", "dp"))
    count_all = lax.axis_size("ctx") * lax.axis_size("dp") * tok_rows
    return (branch, summed / math.sqrt(count_all))


def solution(mesh):
    in_specs = (
        P("dp", "ctx", None),
        P("dp", "ctx", None),
        P("dp", "ctx", None),
        P("dp", "ctx", None),
        P("dp", "ctx", None),
        P("dp", "ctx", None),
        P("dp", "ctx"),
        P(),
        P(),
        P(),
        P("dp", "ctx", None),
    )
    out_specs = (P("dp", "ctx", None), P())
    return jax.shard_map(local, mesh=mesh, in_specs=in_specs, out_specs=out_specs, check_vma=False)
```

profile of v0, /device:TPU:0, one launch (start us, length us, event | category | flops | bytes accessed | tf_op | source)
XLA Modules:
  0.0 287.7 jit_solution(17658628092105028707)
XLA Ops:
  19.2 10.3 %all_gather.15 = s32[1,1024]{1,0:T(1,128)S(1)} all-gather(s32[1,128]{1,0:T(1,128)} %param.19), channel_id=1, replica_groups=mesh['ctx'=8,'dp'=4] {'ctx'}, dimensions={1}, use_global_device_ids=true | all-gather | bytes 4608 | tf_op jit(solution)/shard_map/all_gather | solution.py:106
  29.5 20.9 %all-gather.5.cloned.1.call-done = bf16[12,1024,128]{1,2,0:T(8,128)(2,1)} async-done(((bf16[12,128,128]{1,2,0:T(8,128)(2,1)}), bf16[12,1024,128]{1,2,0:T(8,128)(2,1)}) %all-gather.5.cloned.1.call-update) | async-done | bytes 3145744 | tf_op jit(solution)/shard_map/all_gather | solution.py:110
  50.4 4.4 %copy.44 = bf16[192,8,8,128]{3,2,1,0:T(8,128)(2,1)} copy(bf16[192,8,8,128]{3,1,2,0:T(8,128)(2,1)} %bitcast.120) | data formatting | bytes 6291456
  54.8 4.9 %copy.21 = bf16[12,8,128,128]{3,2,0,1:T(8,128)(2,1)} copy(bf16[12,8,128,128]{2,1,3,0:T(8,128)(2,1)} %bitcast.117) | data formatting | bytes 6291456 | tf_op jit(solution)/shard_map/reshape | solution.py:119
  59.7 25.4 %all-gather.9.cloned.1.call-done = bf16[12,1024,128]{1,2,0:T(8,128)(2,1)} async-done(((bf16[12,128,128]{1,2,0:T(8,128)(2,1)}), bf16[12,1024,128]{1,2,0:T(8,128)(2,1)}) %all-gather.9.cloned.1.call-update) | async-done | bytes 3145744 | tf_op jit(solution)/shard_map/all_gather | solution.py:111
  85.1 4.7 %copy.27 = bf16[12,1024,128]{2,1,0:T(8,128)(2,1)} copy(bf16[12,1024,128]{1,2,0:T(8,128)(2,1)} %all-gather.9.cloned.1.call-done) | data formatting | bytes 6291456 | tf_op jit(solution)/shard_map/all_gather | solution.py:111
  89.8 30.0 %all-gather.7.cloned.1.call-done = bf16[12,1024,128]{1,2,0:T(8,128)(2,1)} async-done(((bf16[12,128,128]{1,2,0:T(8,128)(2,1)}), bf16[12,1024,128]{1,2,0:T(8,128)(2,1)}) %all-gather.7.cloned.1.call-update) | async-done | bytes 3145744 | tf_op jit(solution)/shard_map/all_gather | solution.py:112
  119.8 4.7 %copy.25 = bf16[12,1024,128]{2,1,0:T(8,128)(2,1)} copy(bf16[12,1024,128]{1,2,0:T(8,128)(2,1)} %all-gather.7.cloned.1.call-done) | data formatting | bytes 6291456 | tf_op jit(solution)/shard_map/all_gather | solution.py:112
  124.5 29.9 %all-gather.11.cloned.1.call-done = bf16[12,1024,128]{1,2,0:T(8,128)(2,1)} async-done(((bf16[12,128,128]{1,2,0:T(8,128)(2,1)}), bf16[12,1024,128]{1,2,0:T(8,128)(2,1)}) %all-gather.11.cloned.1.call-update) | async-done | bytes 3145744 | tf_op jit(solution)/shard_map/all_gather | solution.py:113
  154.4 4.7 %copy.29 = bf16[12,1024,128]{2,1,0:T(8,128)(2,1)} copy(bf16[12,1024,128]{1,2,0:T(8,128)(2,1)} %all-gather.11.cloned.1.call-done) | data formatting | bytes 6291456 | tf_op jit(solution)/shard_map/all_gather | solution.py:113
  159.1 74.0 %while.21 = (s32[]{:T(128)}, f32[12,128]{1,0:T(8,128)S(1)}, f32[12,128]{1,0:T(8,128)S(1)}, f32[12,128]{1,0:T(8,128)S(1)}, f32[12,128,128]{2,1,0:T(8,128)S(1)}, /...) while((s32[]{:T(128)}, f32[12,128]{1,0:T(8,128)S(1)}, ...), condition=%wide.region_4.5_spmd.clone, body=%wide.region_0.4_spmd.clone.sunk | while | flops 306735616 | bytes 14737616 | solution.py:128
  163.6 1.6 convolution_add_fusion.8
  165.1 1.6 convolution_add_fusion.9
  166.7 1.6 convolution_add_fusion.7
  172.8 1.6 convolution_add_fusion.8
  174.4 1.6 convolution_add_fusion.9
  176.0 1.6 convolution_add_fusion.7
  182.1 1.6 convolution_add_fusion.8
  183.6 1.6 convolution_add_fusion.9
  185.2 1.6 convolution_add_fusion.7
  192.9 1.6 convolution_add_fusion.9
  194.5 1.6 convolution_add_fusion.7
  202.1 1.6 convolution_add_fusion.9
  203.7 1.6 convolution_add_fusion.7
  211.4 1.6 convolution_add_fusion.9
  213.0 1.6 convolution_add_fusion.7
  220.6 1.6 convolution_add_fusion.9
  222.2 1.6 convolution_add_fusion.7
  229.9 1.6 convolution_add_fusion.9
  231.4 1.6 convolution_add_fusion.7
  235.0 6.1 %fusion.32 = (f32[3072]{0:T(1024)S(1)}, bf16[1,128,3072]{2,1,0:T(8,128)(2,1)}) fusion(bf16[1,128,3072]{2,1,0:T(8,128)(2,1)S(1)} %copy-done, f32[3072]{0:T(1024)S(1)} %copy-done.7, bf16[128,1536]{0,1:T(8,128)(2,1)S(1)} %bitcast.121, bf16[1536,3072]{1,0:T(8,128)(2,1)} %param.21), kind=kOutput, calls=%fused_computation.46 | convolution fusion | flops 1209922560 | bytes 11427840 | tf_op jit(solution)/shard_map/dot_general | solution.py:135
  241.1 39.5 %psum.7 = f32[3072]{0:T(1024)S(1)} all-reduce(f32[3072]{0:T(1024)S(1)} %get-tuple-element.187), channel_id=1, replica_groups=mesh['ctx'=8,'dp'=4] {'ctx','dp'}, use_global_device_ids=true, to_apply=%region_6.7 | all-reduce | flops 3072 | bytes 24576 | tf_op jit(solution)/shard_map/psum | solution.py:138
  (141 shorter events, 57.0 us)
Async XLA Ops:
  7.2 4.6 %copy-start.1 = (bf16[1,128,1536]{2,1,0:T(8,128)(2,1)S(1)}, bf16[1,128,1536]{2,1,0:T(8,128)(2,1)}, u32[]{:S(2)}) copy-start(bf16[1,128,1536]{2,1,0:T(8,128)(2,1)} %param.16) | copy-start | bytes 1179652
  7.2 5.0 %copy-start.2 = (bf16[1,128,1536]{2,1,0:T(8,128)(2,1)S(1)}, bf16[1,128,1536]{2,1,0:T(8,128)(2,1)}, u32[]{:S(2)}) copy-start(bf16[1,128,1536]{2,1,0:T(8,128)(2,1)} %param.17) | copy-start | bytes 1179652
  7.2 43.2 %all-gather.5.cloned.1.call-start = ((), (), s32[]{:S(2)}) async-start(), calls=%async_computation | async-start | bytes 3538944 | tf_op jit(solution)/shard_map/all_gather | solution.py:110
  12.4 2.3 copy-start.3
  13.9 2.7 copy-start.4
  14.7 70.4 %all-gather.9.cloned.1.call-start = ((), (), s32[]{:S(2)}) async-start(), calls=%async_computation.2 | async-start | bytes 3538944 | tf_op jit(solution)/shard_map/all_gather | solution.py:111
  15.7 104.1 %all-gather.7.cloned.1.call-start = ((), (), s32[]{:S(2)}) async-start(), calls=%async_computation.1 | async-start | bytes 3538944 | tf_op jit(solution)/shard_map/all_gather | solution.py:112
  16.5 137.8 %all-gather.11.cloned.1.call-start = ((), (), s32[]{:S(2)}) async-start(), calls=%async_computation.3 | async-start | bytes 3538944 | tf_op jit(solution)/shard_map/all_gather | solution.py:113
  124.5 34.5 %copy-start.5 = (f32[12,128]{1,0:T(8,128)S(1)}, f32[12,128]{1,0:T(8,128)}, u32[]{:S(2)}) copy-start(f32[12,128]{1,0:T(8,128)} %custom-call.2) | copy-start | bytes 18436
  124.5 34.5 %copy-start.6 = (s32[1,128]{1,0:T(1,128)S(1)}, s32[1,128]{1,0:T(1,128)}, u32[]{:S(2)}) copy-start(s32[1,128]{1,0:T(1,128)} %param.19) | copy-start | bytes 1540
  233.3 0.8 copy-start.7
  233.9 1.1 copy-start
Sparse Core Ops, SparseCore 0:
  14.8 35.5 all-gather.4
  52.2 32.8 all-gather.8
  87.0 32.8 all-gather.6
  121.5 32.8 all-gather.10
where the time goes:
time: 290 us; the launch traced here: 288 us
  waiting for transfers between devices  106 us (37%)
  matrix products  77.3 us (27%)
  blocking collectives  49.8 us (17%)
  local copies, waits for them, and re-layouts  31.7 us (11%)
  between operations  14.7 us (5%)
  other arithmetic  7.07 us (2%)
    psum x1, blocking collectives, local(): summed = lax.psum(partial_grad, ('ctx', 'dp'))  39.5 us
    all_gather x1, waiting for transfers between devices, local(): tkey_part = lax.all_gather(tkey_rot, 'ctx', axis=1, tiled=True)  30 us
    all_gather x1, waiting for transfers between devices, local(): tvalue_part = lax.all_gather(tvalue_heads, 'ctx', axis=1, tiled=True)  29.9 us
    all_gather x1, waiting for transfers between devices, local(): value_part = lax.all_gather(value_heads, 'ctx', axis=1, tiled=True)  25.4 us
    all_gather x1, waiting for transfers between devices, local(): key_part = lax.all_gather(key_rot, 'ctx', axis=1, tiled=True)  20.9 us
    dot_general x8, matrix products, attend(): jnp.einsum('hqk,hkd->hqd', weights_b, tvalue_blk, preferred_element_type=...  12.5 us
    dot_general x8, matrix products, attend(): jnp.einsum('hqk,hkd->hqd', weights_b, value_blk, preferred_element_type=j...  12.5 us
    dot_general x8, matrix products, attend(): jnp.einsum('hqk,hkd->hqd', tilted_b, value_blk, preferred_element_type=jn...  12.5 us
  transfers between devices with their start and end apart: 4, of which 4 were waited for; matrix products, arithmetic and copies ran while one was open for 8% of the time, Pallas kernels for 0%

commit v1 on v0

v1 whole, which is shorter than its diff:
```python
import functools
import math

import jax
import jax.numpy as jnp
from jax import lax
from jax.experimental import pallas as pl
from jax.experimental.pallas import tpu as pltpu
from jax.sharding import PartitionSpec as P

HEADS = 12
ID_ROWS = 16
MASK = -3e38
MIB = 2**20


def frequencies(lane, half):
    index = lane % half
    low = 1 << (half.bit_length() // 2)

    def pick(part, count, step):
        factor = jnp.ones(lane.shape, jnp.float32)
        for k in range(1, count):
            factor = jnp.where(part == k, 10000.0 ** (-k * step / half), factor)
        return factor

    return pick(index // low, half // low, low) * pick(index % low, low, 1)


def rotation(order_ref, rows, head_dim):
    half = head_dim // 2
    lane = lax.broadcasted_iota(jnp.int32, (8, head_dim), 1)
    line = lax.broadcasted_iota(jnp.int32, (8, head_dim), 0)
    frequency = frequencies(lane, half)
    base = order_ref[lax.axis_index("ctx")] * rows
    steps = rows // 8
    angles = jnp.concatenate(
        [line.astype(jnp.float32) * frequency]
        + [(base + 8 * (line + 8 * k)).astype(jnp.float32) * frequency for k in range(steps // 8)],
        axis=0,
    )
    cosines, sines = jnp.cos(angles), jnp.sin(angles)
    cos_v, sin_v = cosines[:8], sines[:8]
    cos_rows, sin_rows = [], []
    for u in range(steps):
        cos_u, sin_u = cosines[8 + u : 9 + u], sines[8 + u : 9 + u]
        cos_rows.append(cos_u * cos_v - sin_u * sin_v)
        sin_rows.append(jnp.where(lane < half, -1.0, 1.0) * (sin_u * cos_v + cos_u * sin_v))
    return jnp.concatenate(cos_rows, axis=0), jnp.concatenate(sin_rows, axis=0)


def group_of(offsets, members):
    me = lax.axis_index("ctx")
    even, odd = offsets
    offset = even if even == odd else jnp.where(me % members % 2 == 0, even, odd)
    return (me // members) ^ offset


def pack_kernel(route, members, turns, with_ids, order_hbm, ids_hbm, *refs):
    n_in = 2 * len(turns)
    sources, outs, (scratch, in_sems, order_ref, ids_ref, small_sems) = refs[:n_in], refs[n_in:-5], refs[-5:]
    loads = [pltpu.make_async_copy(order_hbm, order_ref, small_sems.at[0]), pltpu.make_async_copy(ids_hbm, ids_ref, small_sems.at[1])]
    loads += [pltpu.make_async_copy(source.at[0], scratch.at[t], in_sems.at[t]) for t, source in enumerate(sources)]
    for load in loads:
        load.start()
    rows, features = scratch.shape[1:]
    per_group = HEADS // len(route)
    head_dim = features // HEADS
    places = [group_of(offsets, members) for offsets in route]
    loads[0].wait()
    cosine, sine = rotation(order_ref, rows, head_dim)

    def turned(x):
        x = x.astype(jnp.float32)
        return (x * cosine + pltpu.roll(x, head_dim // 2, 1) * sine).astype(jnp.bfloat16)

    loads[1].wait()
    if with_ids:
        ids = jnp.broadcast_to(ids_ref[...].astype(jnp.float32), (ID_ROWS, rows)).astype(jnp.bfloat16)
        for out in outs:
            out[per_group * len(turns) * rows :, :head_dim] = ids
            out[per_group * len(turns) * rows :, head_dim:] = ids
    for t in range(n_in):
        loads[2 + t].wait()
        for group, out in zip(places, outs):
            for i in range(per_group):
                column = pl.multiple_of((group * per_group + i) * head_dim, head_dim)
                x = scratch[t, :, pl.ds(column, head_dim)]
                at = (i * len(turns) + t // 2) * rows
                out[at : at + rows, t % 2 * head_dim : (t % 2 + 1) * head_dim] = turned(x) if turns[t // 2] else x


def arrived_kernel(*refs):
    refs[-1][...] = jnp.zeros(refs[-1].shape, refs[-1].dtype)


def stage_kernel(w_hbm, cot_hbm, after_ref, w_ref, cot_ref, done_ref, sems):
    copies = [pltpu.make_async_copy(w_hbm, w_ref, sems.at[0]), pltpu.make_async_copy(cot_hbm, cot_ref, sems.at[1])]
    for copy in copies:
        copy.start()
    done_ref[...] = jnp.zeros(done_ref.shape, done_ref.dtype)
    for copy in copies:
        copy.wait()


def merge_kernel(*refs):
    packs, (out, features) = refs[:-3], refs[-2:]
    places = len(packs)
    size, both = packs[0].shape
    head_dim = both // 2
    rows, keep = head_dim, size - ID_ROWS
    lane = lax.broadcasted_iota(jnp.int32, (rows, head_dim), 1).astype(jnp.float32)
    for p, pack in enumerate(packs):
        out[p * keep : (p + 1) * keep, :] = pack[:keep, :]
        ids = pack[keep:, :head_dim].astype(jnp.float32)[0:1]
        hit = jnp.transpose(jnp.broadcast_to(ids, (head_dim, rows))) == lane
        other = jnp.where(hit, 0.0, MASK).astype(jnp.bfloat16)
        features[p * rows : (p + 1) * rows, :head_dim] = other
        features[p * rows : (p + 1) * rows, head_dim:] = jnp.where(hit, 1.0, 0.0).astype(jnp.bfloat16)
        at = places * keep + p // 2 * rows
        out[at : at + rows, p % 2 * head_dim : (p % 2 + 1) * head_dim] = other


def attend_kernel(groups, members, places, scale, *refs):
    half = groups // 2
    packs, features, merged, refs = refs[:groups], refs[groups : groups + 2], refs[groups + 2 : groups + 2 * members], refs[groups + 2 * members :]
    queries, outs = refs[: len(places)], refs[-len(places) :]
    rows, part = outs[0].shape
    size, both = packs[0].shape
    head_dim = both // 2
    keep = size - ID_ROWS
    nt = (((1,), (1,)), ((), ()))
    blocks = [(pack, 0) for pack in packs] + [(other, p * keep) for other in merged for p in range(half)]
    other_clip = [(ref, p * rows, 0) for ref in features for p in range(half)]
    other_clip += [(other, half * keep + p // 2 * rows, p % 2 * head_dim) for other in merged for p in range(half)]
    same = jnp.concatenate([features[p // half][p % half * rows : (p % half + 1) * rows, head_dim:] for p in places], axis=0)

    def products(i):
        q = jnp.concatenate([query[i * rows : (i + 1) * rows, :] for query in queries], axis=0)
        q_masked = jnp.concatenate([q[:, head_dim:], same], axis=1)
        scores, slopes = [], []
        for b in range(0, len(blocks), 2):
            pair = [(ref, at + 2 * i * rows) for ref, at in blocks[b : b + 2]]
            masks = [ref[at : at + rows, col : col + head_dim] for ref, at, col in other_clip[b : b + 2]]
            keys = jnp.concatenate([ref[at : at + rows, :] for ref, at in pair], axis=0)
            masked = [jnp.concatenate([ref[at : at + rows, :head_dim], mask], axis=1) for (ref, at), mask in zip(pair, masks)]
            scores.append(lax.dot_general(q_masked, jnp.concatenate(masked, axis=0), nt, preferred_element_type=jnp.float32))
            slopes.append(lax.dot_general(q, keys, nt, preferred_element_type=jnp.float32))
        return scores, slopes

    def finish(i, scores, slopes):
        best = functools.reduce(jnp.maximum, scores)
        best = jnp.max(best, axis=1, keepdims=True)
        weights = [jnp.exp2((score - best) * (scale * math.log2(math.e))) for score in scores]
        tilted = [weight * slope for weight, slope in zip(weights, slopes)]
        total = 1.0 / jnp.sum(functools.reduce(lambda a, b: a + b, weights), axis=1, keepdims=True)
        weights = jnp.concatenate([weight.astype(jnp.bfloat16) for weight in weights], axis=1)
        tilted = jnp.concatenate([tilt.astype(jnp.bfloat16) for tilt in tilted], axis=1)
        vals = jnp.concatenate([ref[at + (2 * i + 1) * rows : at + (2 * i + 2) * rows, :] for ref, at in blocks], axis=0)
        ones = jnp.ones((vals.shape[0], head_dim), jnp.bfloat16)
        mixed = jnp.dot(weights, vals, preferred_element_type=jnp.float32)
        leaned = jnp.dot(tilted, jnp.concatenate([vals[:, :head_dim], ones], axis=1), preferred_element_type=jnp.float32)
        primal, spread = mixed[:, :head_dim], mixed[:, head_dim:]
        slope_part, weighted = leaned[:, :head_dim], leaned[:, head_dim:]
        out = ((slope_part - weighted * (primal * total)) * scale + spread) * total
        for k, ref in enumerate(outs):
            ref[:, i * head_dim : (i + 1) * head_dim] = out[k * rows : (k + 1) * rows].astype(jnp.bfloat16)

    ready = products(0)
    for i in range(part // head_dim):
        following = products(i + 1) if (i + 1) * head_dim < part else None
        finish(i, *ready)
        ready = following


def part_kernel(members, offsets, tile, ta_ref, w_ref, *refs):
    begun, out_ref = refs[:-1], refs[-1]
    group = group_of(offsets, members)
    width = ta_ref.shape[1]
    place = pl.ds(pl.multiple_of(group * width, width), width)
    for j in range(w_ref.shape[1] // tile):
        cols = slice(j * tile, (j + 1) * tile)
        part = jnp.dot(ta_ref[...], w_ref[place, cols], preferred_element_type=jnp.float32)
        out_ref[:, cols] = begun[0][:, cols] + part if begun else part


def project_kernel(members, offsets, tile, ta_ref, w_ref, begun_ref, cot_ref, projected_ref, grad_ref):
    group = group_of(offsets, members)
    width = ta_ref.shape[1]
    place = pl.ds(pl.multiple_of(group * width, width), width)
    for j in range(w_ref.shape[1] // tile):
        cols = slice(j * tile, (j + 1) * tile)
        projected = begun_ref[:, cols] + jnp.dot(ta_ref[...], w_ref[place, cols], preferred_element_type=jnp.float32)
        projected_ref[:, cols] = projected
        grad_ref[:, cols] = jnp.sum(cot_ref[0, :, cols].astype(jnp.float32) * projected, axis=0, keepdims=True)


def branch_kernel(projected_ref, scale_ref, branch_ref):
    branch_ref[0] = (scale_ref[...] * projected_ref[...]).astype(jnp.bfloat16)


def sum_kernel(factor, *refs):
    terms = [ref[...] for ref in refs[:-1]]
    while len(terms) > 1:
        terms = [terms[i] + terms[i + 1] for i in range(0, len(terms), 2)]
    refs[-1][...] = terms[0] * factor


def exchange_sum(x, partners, factor=1.0):
    n_ctx, n_dp = lax.axis_size("ctx"), lax.axis_size("dp")
    places = [(j, z) for j in range(n_ctx) for z in range(n_dp)]
    terms = [lax.ppermute(x, ("ctx", "dp"), [(j * n_dp + z, (j ^ own) * n_dp + (z ^ other)) for j, z in places]) for own, other in partners]
    return pl.pallas_call(
        functools.partial(sum_kernel, factor),
        out_shape=jax.ShapeDtypeStruct(x.shape, x.dtype),
        compiler_params=pltpu.CompilerParams(vmem_limit_bytes=16 * MIB),
        name="sum",
    )(*terms, x)


def local(queries, keys, values, tangent_queries, tangent_keys, tangent_values, clip_ids, block_order, out_weight, layer_scale, cotangent):
    n_ctx, n_dp = lax.axis_size("ctx"), lax.axis_size("dp")
    rows, features = queries.shape[1:]
    head_dim = features // HEADS
    width = out_weight.shape[1]
    groups = math.gcd(n_ctx, HEADS)
    members = n_ctx // groups
    per_group = HEADS // groups
    vmem = pl.BlockSpec(memory_space=pltpu.VMEM)
    hbm = pl.BlockSpec(memory_space=pltpu.HBM)
    bf16 = jnp.bfloat16

    cross = 1 if members > 1 else 0

    def swap(x, offset):
        return lax.ppermute(x, "ctx", [(j, j ^ offset) for j in range(n_ctx)])

    far = sorted((offset for offset in range(groups) if offset.bit_count() > 1), key=lambda offset: -offset.bit_count())
    near = [offset for offset in range(groups) if offset.bit_count() == 1]
    route = [(0, 0)] + [(offset, offset) for offset in far] + list(zip(near, reversed(near)))
    early, late = [*range(1 + len(far))], [*range(1 + len(far), groups)]

    def send(x, place):
        return lax.ppermute(x, "ctx", [(j, j ^ (route[place][j % members % 2] * members + cross)) for j in range(n_ctx)])

    def send_back(x, place):
        return lax.ppermute(x, "ctx", [(j ^ (route[place][j % members % 2] * members + cross), j) for j in range(n_ctx)])

    kv_pack = (2 * per_group * rows + ID_ROWS, 2 * head_dim)
    q_pack = (per_group * rows, 2 * head_dim)

    def in_hbm(x):
        return pltpu.with_memory_space_constraint(x, pltpu.HBM)

    def pack(name, shape, turns, with_ids, sources):
        return pl.pallas_call(
            functools.partial(pack_kernel, route, members, turns, with_ids),
            out_shape=[pltpu.VMEM(shape, bf16)] * groups,
            in_specs=[hbm] * (2 + len(sources)),
            out_specs=[vmem] * groups,
            scratch_shapes=[
                pltpu.VMEM((len(sources), rows, features), bf16),
                pltpu.SemaphoreType.DMA((len(sources),)),
                pltpu.SMEM(block_order.shape, jnp.int32),
                pltpu.VMEM(clip_ids.shape, jnp.int32),
                pltpu.SemaphoreType.DMA((2,)),
            ],
            compiler_params=pltpu.CompilerParams(vmem_limit_bytes=16 * MIB),
            name=name,
        )(*map(in_hbm, (block_order, clip_ids) + sources))

    kv = pack("pack_keys", kv_pack, (True, False), True, (keys, tangent_keys, values, tangent_values))
    q = list(pack("pack_queries", q_pack, (True,), False, (tangent_queries, queries)))
    weight, cot, staged = pl.pallas_call(
        stage_kernel,
        out_shape=[pltpu.VMEM(out_weight.shape, bf16), pltpu.VMEM(cotangent.shape, bf16), pltpu.VMEM((8, 128), jnp.float32)],
        in_specs=[hbm, hbm, vmem],
        out_specs=[vmem] * 3,
        scratch_shapes=[pltpu.SemaphoreType.DMA((2,))],
        compiler_params=pltpu.CompilerParams(vmem_limit_bytes=16 * MIB),
        name="stage",
    )(in_hbm(out_weight), in_hbm(cotangent), q[0])

    def exchange(sent):
        return [sent[0]] + [send(sent[place], place) for place in range(1, groups)]

    kv = exchange(kv)
    q = exchange(q)

    def merge(name, packs, after):
        places = len(packs)
        return pl.pallas_call(
            merge_kernel,
            out_shape=[
                jax.ShapeDtypeStruct((places * 2 * per_group * rows + places // 2 * rows, 2 * head_dim), bf16),
                jax.ShapeDtypeStruct((places * rows, 2 * head_dim), bf16),
            ],
            in_specs=[vmem] * (places + 1),
            out_specs=[vmem] * 2,
            compiler_params=pltpu.CompilerParams(vmem_limit_bytes=16 * MIB),
            name=name,
        )(*packs, after)

    merged_first, features_first = merge("merge_first", kv[: groups // 2], q[0])
    merged_last, features_last = merge("merge_last", kv[groups // 2 :], staged)
    others = [swap(merged, s) for s in range(1, members) for merged in (merged_first, merged_last)]
    arrived = pl.pallas_call(
        arrived_kernel,
        out_shape=jax.ShapeDtypeStruct((8, 128), jnp.float32),
        in_specs=[vmem] * len(early),
        out_specs=vmem,
        compiler_params=pltpu.CompilerParams(vmem_limit_bytes=16 * MIB),
        cost_estimate=pl.CostEstimate(flops=10**11, bytes_accessed=MIB, transcendentals=0),
        name="arrived",
    )(*(q[place] for place in early))

    def attend(name, places, *after):
        return pl.pallas_call(
            functools.partial(attend_kernel, groups, members, places, head_dim ** (-0.5)),
            out_shape=[jax.ShapeDtypeStruct((rows, per_group * head_dim), bf16)] * len(places),
            in_specs=[vmem] * (groups + 2 * members + len(places) + len(after)),
            out_specs=[vmem] * len(places),
            compiler_params=pltpu.CompilerParams(vmem_limit_bytes=24 * MIB),
            name=name,
        )(*kv, features_first, features_last, *others, *(q[place] for place in places), *after)

    done = dict(zip(early, attend("attend_early", early, arrived)))
    for place in early[1:]:
        done[place] = send_back(done[place], place)
    done.update(zip(late, attend("attend_late", late)))
    for place in late:
        done[place] = send_back(done[place], place)
    arrivals = [*early, *late]
    begun = None
    for place in arrivals[:-1]:
        begun = pl.pallas_call(
            functools.partial(part_kernel, members, route[place], 512),
            out_shape=jax.ShapeDtypeStruct((rows, width), jnp.float32),
            in_specs=[vmem] * (2 + (begun is not None)),
            out_specs=vmem,
            compiler_params=pltpu.CompilerParams(vmem_limit_bytes=16 * MIB),
            name=f"part{place}",
        )(done[place], weight, *([] if begun is None else [begun]))
    projected, grad = pl.pallas_call(
        functools.partial(project_kernel, members, route[arrivals[-1]], 512),
        out_shape=[jax.ShapeDtypeStruct((rows, width), jnp.float32), jax.ShapeDtypeStruct((1, width), jnp.float32)],
        in_specs=[vmem] * 4,
        out_specs=[vmem] * 2,
        compiler_params=pltpu.CompilerParams(vmem_limit_bytes=16 * MIB),
        name="project",
    )(done[arrivals[-1]], weight, begun, cot)
    branch = pl.pallas_call(
        branch_kernel,
        out_shape=jax.ShapeDtypeStruct((1, rows, width), bf16),
        in_specs=[vmem] * 2,
        out_specs=vmem,
        compiler_params=pltpu.CompilerParams(vmem_limit_bytes=16 * MIB),
        name="branch",
    )(projected, layer_scale[None, :])
    summed = exchange_sum(grad, [(s, 0) for s in reversed(range(1, members))])
    summed = exchange_sum(summed, [(offset + cross, 0) for offset in reversed(range(members, n_ctx, members))])
    factor = 1.0 / math.sqrt(n_ctx * n_dp * rows)
    offsets = [1 << k for k in range(n_dp.bit_length() - 1)]
    for offset in offsets:
        summed = exchange_sum(summed, [(cross, offset)], factor if offset == offsets[-1] else 1.0)
    return branch, summed[0]


def solution(mesh):
    tokens = P("dp", "ctx", None)
    in_specs = (tokens,) * 6 + (P("dp", "ctx"), P(), P(), P(), tokens)
    return jax.shard_map(local, mesh=mesh, in_specs=in_specs, out_specs=(tokens, P()), check_vma=False)
```

time: 290 us -> 58.8 us (0.20)
  waiting for transfers between devices: 106 us -> 17.4 us
  matrix products: 77.3 us -> 0 us
  blocking collectives: 49.8 us -> 0 us
  local copies, waits for them, and re-layouts: 31.7 us -> 0.01 us
  starting transfers between devices: 0.16 us -> 24.5 us
  Pallas kernels: 0 us -> 15.9 us
  between operations: 14.7 us -> 0.76 us
  other arithmetic: 7.07 us -> 0 us
    all_gather x4 -> x0, waiting for transfers between devices: 106 us -> none  [the longest x1 30 us: local(): tkey_part = lax.all_gather(tkey_rot, 'ctx', axis=1, tiled=True)]
    dot_general x49 -> x0, matrix products: 77.3 us -> none  [the longest x8 12.5 us: attend(): jnp.einsum('hqk,hkd->hqd', weights_b, tvalue_blk, preferred_element_type=...]
    psum x1 -> x0, blocking collectives: 39.5 us -> none  [local(): summed = lax.psum(partial_grad, ('ctx', 'dp'))]
    ppermute x0 -> x17, starting transfers between devices: none -> 24.5 us  [the longest x6 9.1 us: send(): lax.ppermute(x, 'ctx', [(j, j ^ route[place][j % members % 2] * members +...]
    ppermute x0 -> x17, waiting for transfers between devices: none -> 17.4 us  [the longest x6 10.8 us: send(): lax.ppermute(x, 'ctx', [(j, j ^ route[place][j % members % 2] * members +...]
    pallas_call x0 -> x17, Pallas kernels: none -> 15.9 us  [the longest x2 4.73 us: attend(): pl.pallas_call(functools.partial(attend_kernel, groups, members, places,...]
    all_gather x3 -> x0, local copies, waits for them, and re-layouts: 14.1 us -> none  [the longest x1 4.74 us: local(): value_part = lax.all_gather(value_heads, 'ctx', axis=1, tiled=True)]
    unnamed x25 -> x2, local copies, waits for them, and re-layouts: 10.5 us -> 0.01 us
  transfers between devices with their start and end apart: 4 -> 17, of which waited for: 4 -> 10; matrix products, arithmetic and copies ran while one was open for 8% -> 0% of each run, Pallas kernels for 0% -> 22%
where the time goes in v1:
time: 58.8 us; the launch traced here: 58.6 us
  starting transfers between devices  24.5 us (42%)
  waiting for transfers between devices  17.4 us (30%)
  Pallas kernels  15.9 us (27%)
  between operations  0.76 us (1%)
    ppermute x6, waiting for transfers between devices, send(): lax.ppermute(x, 'ctx', [(j, j ^ route[place][j % members % 2] * members +...  10.8 us
    ppermute x6, starting transfers between devices, send(): lax.ppermute(x, 'ctx', [(j, j ^ route[place][j % members % 2] * members +...  9.1 us
    ppermute x3, starting transfers between devices, send_back(): lax.ppermute(x, 'ctx', [(j ^ route[place][j % members % 2] * members + cr...  7.51 us
    ppermute x6, starting transfers between devices, exchange_sum(): lax.ppermute(x, ('ctx', 'dp'), [(j * n_dp + z, (j ^ own) * n_dp + (z ^ ot...  7.35 us
    pallas_call x2, Pallas kernels, attend(): pl.pallas_call(functools.partial(attend_kernel, groups, members, places,...  4.73 us
    ppermute x6, waiting for transfers between devices, exchange_sum(): lax.ppermute(x, ('ctx', 'dp'), [(j * n_dp + z, (j ^ own) * n_dp + (z ^ ot...  4.73 us
    pallas_call x1, Pallas kernels, local(): pl.pallas_call(stage_kernel, out_shape=[pltpu.VMEM(out_weight.shape, bf16...  3.84 us
    pallas_call x2, Pallas kernels, pack(): pl.pallas_call(functools.partial(pack_kernel, route, members, turns, with...  3.02 us
  transfers between devices with their start and end apart: 17, of which 10 were waited for; matrix products, arithmetic and copies ran while one was open for 0% of the time, Pallas kernels for 22%

profile of v1, /device:TPU:0, one launch (start us, length us, event | category | flops | bytes accessed | tf_op | source)
XLA Modules:
  0.0 58.6 jit_solution(6436943845360636977)
XLA Ops:
  0.6 1.6 %pack_keys.1 = (bf16[784,256]{1,0:T(8,128)(2,1)S(1)}, bf16[784,256]{1,0:T(8,128)(2,1)S(1)}, bf16[784,256]{1,0:T(8,128)(2,1)S(1)}, bf16[784,256]{1,0:T(8,128)(2,1)S(1)}) custom-call(s32[8]{0:T(128)} %order_hbm.3, s32[1,128]{1,0:T(1,128)} %ids_hbm.3, bf16[1,128,1536]{2,1,0:T(8,128)(2,1)} %refs_0_.2, bf16[1,128,1536]{2,1,0:T(8,128)(2,1)} %refs_1_.2, ...), custom_call_target="tpu_custom_call" | custom-call | tf_op jit(solution)/shard_map/pack_keys/pallas_call | solution.py:256
  2.2 3.4 %collective-permute-start = (bf16[784,256]{1,0:T(8,128)(2,1)S(1)}, bf16[784,256]{1,0:T(8,128)(2,1)S(1)}, u32[]{:S(2)}, u32[]{:S(2)}) collective-permute-start(bf16[784,256]{1,0:T(8,128)(2,1)S(1)} %get-tuple-element.24), channel_id=1, source_target_pairs={{0,28},{4,24},{8,20},{12,16},{16,12},{20,8},{24,4},{28,0},{1,29},{... | collective-permute-start | bytes 1204232 | tf_op jit(solution)/shard_map/ppermute | solution.py:244
  5.6 0.8 %collective-permute-start.1 = (bf16[784,256]{1,0:T(8,128)(2,1)S(1)}, bf16[784,256]{1,0:T(8,128)(2,1)S(1)}, u32[]{:S(2)}, u32[]{:S(2)}) collective-permute-start(bf16[784,256]{1,0:T(8,128)(2,1)S(1)} %get-tuple-element.25), channel_id=1, source_target_pairs={{0,12},{4,16},{8,4},{12,24},{16,28},{20,0},{24,20},{28,8},{1,13},{... | collective-permute-start | bytes 1204232 | tf_op jit(solution)/shard_map/ppermute | solution.py:244
  6.5 0.9 %collective-permute-start.2 = (bf16[784,256]{1,0:T(8,128)(2,1)S(1)}, bf16[784,256]{1,0:T(8,128)(2,1)S(1)}, u32[]{:S(2)}, u32[]{:S(2)}) collective-permute-start(bf16[784,256]{1,0:T(8,128)(2,1)S(1)} %get-tuple-element.26), channel_id=1, source_target_pairs={{0,20},{4,8},{8,28},{12,0},{16,4},{20,24},{24,12},{28,16},{1,21},{... | collective-permute-start | bytes 1204232 | tf_op jit(solution)/shard_map/ppermute | solution.py:244
  7.4 1.4 %pack_queries.1 = (bf16[384,256]{1,0:T(8,128)(2,1)S(1)}, bf16[384,256]{1,0:T(8,128)(2,1)S(1)}, bf16[384,256]{1,0:T(8,128)(2,1)S(1)}, bf16[384,256]{1,0:T(8,128)(2,1)S(1)}) custom-call(s32[8]{0:T(128)} %order_hbm.3, s32[1,128]{1,0:T(1,128)} %ids_hbm.3, bf16[1,128,1536]{2,1,0:T(8,128)(2,1)} %refs_0_.3, bf16[1,128,1536]{2,1,0:T(8,128)(2,1)} %refs_1_.3), custom_call_target="tpu_custom_call" | custom-call | tf_op jit(solution)/shard_map/pack_queries/pallas_call | solution.py:256
  8.9 1.7 %collective-permute-start.5 = (bf16[384,256]{1,0:T(8,128)(2,1)S(1)}, bf16[384,256]{1,0:T(8,128)(2,1)S(1)}, u32[]{:S(2)}, u32[]{:S(2)}) collective-permute-start(bf16[384,256]{1,0:T(8,128)(2,1)S(1)} %get-tuple-element.33), channel_id=1, source_target_pairs={{0,12},{4,16},{8,4},{12,24},{16,28},{20,0},{24,20},{28,8},{1,13},{... | collective-permute-start | bytes 589832 | tf_op jit(solution)/shard_map/ppermute | solution.py:244
  10.6 3.8 %stage.1 = (bf16[1536,3072]{1,0:T(8,128)(2,1)S(1)}, bf16[1,128,3072]{2,1,0:T(8,128)(2,1)S(1)}, f32[8,128]{1,0:T(8,128)S(1)}) custom-call(bf16[1536,3072]{1,0:T(8,128)(2,1)} %w_hbm.1, bf16[1,128,3072]{2,1,0:T(8,128)(2,1)} %cot_hbm.1, bf16[384,256]{1,0:T(8,128)(2,1)S(1)} %get-tuple-element.27.refs_2_.after_ref.refs_0_.refs_8_), custom_call_target="tpu_custom_call" | custom-call | tf_op jit(solution)/shard_map/stage/pallas_call | solution.py:274
  14.5 0.9 %collective-permute-done.refs_1_ = bf16[784,256]{1,0:T(8,128)(2,1)S(1)} collective-permute-done((bf16[784,256]{1,0:T(8,128)(2,1)S(1)}, bf16[784,256]{1,0:T(8,128)(2,1)S(1)}, u32[]{:S(2)}, u32[]{:S(2)}) %collective-permute-start) | collective-permute-done | bytes 401440 | tf_op jit(solution)/shard_map/ppermute | solution.py:244
  15.4 2.1 %collective-permute-start.6 = (bf16[384,256]{1,0:T(8,128)(2,1)S(1)}, bf16[384,256]{1,0:T(8,128)(2,1)S(1)}, u32[]{:S(2)}, u32[]{:S(2)}) collective-permute-start(bf16[384,256]{1,0:T(8,128)(2,1)S(1)} %get-tuple-element.34), channel_id=1, source_target_pairs={{0,20},{4,8},{8,28},{12,0},{16,4},{20,24},{24,12},{28,16},{1,21},{... | collective-permute-start | bytes 589832 | tf_op jit(solution)/shard_map/ppermute | solution.py:244
  17.6 7.1 %collective-permute-done.1.refs_0_.refs_2_ = bf16[784,256]{1,0:T(8,128)(2,1)S(1)} collective-permute-done((bf16[784,256]{1,0:T(8,128)(2,1)S(1)}, bf16[784,256]{1,0:T(8,128)(2,1)S(1)}, u32[]{:S(2)}, u32[]{:S(2)}) %collective-permute-start.1) | collective-permute-done | bytes 401440 | tf_op jit(solution)/shard_map/ppermute | solution.py:244
  24.7 0.4 collective-permute-start.3
  25.4 2.8 %collective-permute-done.9.refs_1_.refs_9_ = bf16[384,256]{1,0:T(8,128)(2,1)S(1)} collective-permute-done((bf16[384,256]{1,0:T(8,128)(2,1)S(1)}, bf16[384,256]{1,0:T(8,128)(2,1)S(1)}, u32[]{:S(2)}, u32[]{:S(2)}) %collective-permute-start.9) | collective-permute-done | bytes 196640 | tf_op jit(solution)/shard_map/ppermute | solution.py:244
  28.3 2.4 %attend_early.1 = (bf16[128,384]{1,0:T(8,128)(2,1)S(1)}, bf16[128,384]{1,0:T(8,128)(2,1)S(1)}) custom-call(bf16[784,256]{1,0:T(8,128)(2,1)S(1)} %get-tuple-element.23.refs_0_, bf16[784,256]{1,0:T(8,128)(2,1)S(1)} %collective-permute-done.refs_1_, bf16[784,256]{1,0:T(8,128)(2,1)S(1)} %collective-permute-done.1.refs_0_.refs_2_, ...), custom_call_target="tpu_custom_call" | custom-call | tf_op jit(solution)/shard_map/attend_early/pallas_call | solution.py:318
  30.7 5.7 %collective-permute-start.10 = (bf16[128,384]{1,0:T(8,128)(2,1)S(1)}, bf16[128,384]{1,0:T(8,128)(2,1)S(1)}, u32[]{:S(2)}, u32[]{:S(2)}) collective-permute-start(bf16[128,384]{1,0:T(8,128)(2,1)S(1)} %get-tuple-element.39), channel_id=1, source_target_pairs={{28,0},{24,4},{20,8},{16,12},{12,16},{8,20},{4,24},{0,28},{29,1},{... | collective-permute-start | bytes 294920 | tf_op jit(solution)/shard_map/ppermute | solution.py:247
  36.4 2.4 %attend_late.1 = (bf16[128,384]{1,0:T(8,128)(2,1)S(1)}, bf16[128,384]{1,0:T(8,128)(2,1)S(1)}) custom-call(bf16[784,256]{1,0:T(8,128)(2,1)S(1)} %get-tuple-element.23.refs_0_, bf16[784,256]{1,0:T(8,128)(2,1)S(1)} %collective-permute-done.refs_1_, bf16[784,256]{1,0:T(8,128)(2,1)S(1)} %collective-permute-done.1.refs_0_.refs_2_, ...), custom_call_target="tpu_custom_call" | custom-call | tf_op jit(solution)/shard_map/attend_late/pallas_call | solution.py:318
  38.8 1.7 %collective-permute-start.7 = (bf16[128,384]{1,0:T(8,128)(2,1)S(1)}, bf16[128,384]{1,0:T(8,128)(2,1)S(1)}, u32[]{:S(2)}, u32[]{:S(2)}) collective-permute-start(bf16[128,384]{1,0:T(8,128)(2,1)S(1)} %get-tuple-element.35), channel_id=1, source_target_pairs={{20,0},{8,4},{28,8},{0,12},{4,16},{24,20},{12,24},{16,28},{21,1},{... | collective-permute-start | bytes 294920 | tf_op jit(solution)/shard_map/ppermute | solution.py:247
  40.6 0.6 part0.1.refs_0_
  41.2 0.6 %part1.1.refs_0_ = f32[128,3072]{1,0:T(8,128)S(1)} custom-call(bf16[128,384]{1,0:T(8,128)(2,1)S(1)} %collective-permute-done.10.ta_ref, bf16[1536,3072]{1,0:T(8,128)(2,1)S(1)} %get-tuple-element.36.w_ref, f32[128,3072]{1,0:T(8,128)S(1)} %part0.1.refs_0_), custom_call_target="tpu_custom_call" | custom-call | tf_op jit(solution)/shard_map/part1/pallas_call | solution.py:336
  41.8 1.8 %collective-permute-done.8.ta_ref = bf16[128,384]{1,0:T(8,128)(2,1)S(1)} collective-permute-done((bf16[128,384]{1,0:T(8,128)(2,1)S(1)}, bf16[128,384]{1,0:T(8,128)(2,1)S(1)}, u32[]{:S(2)}, u32[]{:S(2)}) %collective-permute-start.8) | collective-permute-done | bytes 98336 | tf_op jit(solution)/shard_map/ppermute | solution.py:247
  43.6 0.6 %part2.1.begun_ref = f32[128,3072]{1,0:T(8,128)S(1)} custom-call(bf16[128,384]{1,0:T(8,128)(2,1)S(1)} %collective-permute-done.8.ta_ref, bf16[1536,3072]{1,0:T(8,128)(2,1)S(1)} %get-tuple-element.36.w_ref, f32[128,3072]{1,0:T(8,128)S(1)} %part1.1.refs_0_), custom_call_target="tpu_custom_call" | custom-call | tf_op jit(solution)/shard_map/part2/pallas_call | solution.py:336
  44.3 0.7 %project.1 = (f32[128,3072]{1,0:T(8,128)S(1)}, f32[1,3072]{1,0:T(1,128)S(1)}) custom-call(bf16[128,384]{1,0:T(8,128)(2,1)S(1)} %collective-permute-done.7.ta_ref, bf16[1536,3072]{1,0:T(8,128)(2,1)S(1)} %get-tuple-element.36.w_ref, f32[128,3072]{1,0:T(8,128)S(1)} %part2.1.begun_ref, bf16[1,128,3072]{2,1,0:T(8,128)(2,1)S(1)} %get-tuple-element.41.cot_ref), custom_call_target="tpu_custom_call" | custom-call | tf_op jit(solution)/shard_map/project/pallas_call | solution.py:344
  45.2 1.0 %collective-permute-done.11.refs_0_ = f32[1,3072]{1,0:T(1,128)S(1)} collective-permute-done((f32[1,3072]{1,0:T(1,128)S(1)}, f32[1,3072]{1,0:T(1,128)S(1)}, u32[]{:S(2)}, u32[]{:S(2)}) %collective-permute-start.11) | collective-permute-done | bytes 12320 | tf_op jit(solution)/shard_map/ppermute | solution.py:212
  46.2 1.5 %collective-permute-start.13 = (f32[1,3072]{1,0:T(1,128)S(1)}, f32[1,3072]{1,0:T(1,128)S(1)}, u32[]{:S(2)}, u32[]{:S(2)}) collective-permute-start(f32[1,3072]{1,0:T(1,128)S(1)} %sum.4.refs_3_), channel_id=1, source_target_pairs={{0,20},{1,21},{2,22},{3,23},{4,16},{5,17},{6,18},{7,19},{8,28},{9,... | collective-permute-start | bytes 36872 | tf_op jit(solution)/shard_map/ppermute | solution.py:212
  47.8 1.5 %collective-permute-start.14 = (f32[1,3072]{1,0:T(1,128)S(1)}, f32[1,3072]{1,0:T(1,128)S(1)}, u32[]{:S(2)}, u32[]{:S(2)}) collective-permute-start(f32[1,3072]{1,0:T(1,128)S(1)} %sum.4.refs_3_), channel_id=1, source_target_pairs={{0,12},{1,13},{2,14},{3,15},{4,8},{5,9},{6,10},{7,11},{8,4},{9,5},... | collective-permute-start | bytes 36872 | tf_op jit(solution)/shard_map/ppermute | solution.py:212
  49.2 1.0 %collective-permute-done.12.refs_0_ = f32[1,3072]{1,0:T(1,128)S(1)} collective-permute-done((f32[1,3072]{1,0:T(1,128)S(1)}, f32[1,3072]{1,0:T(1,128)S(1)}, u32[]{:S(2)}, u32[]{:S(2)}) %collective-permute-start.12) | collective-permute-done | bytes 12320 | tf_op jit(solution)/shard_map/ppermute | solution.py:212
  50.2 0.7 %collective-permute-done.14.refs_2_ = f32[1,3072]{1,0:T(1,128)S(1)} collective-permute-done((f32[1,3072]{1,0:T(1,128)S(1)}, f32[1,3072]{1,0:T(1,128)S(1)}, u32[]{:S(2)}, u32[]{:S(2)}) %collective-permute-start.14) | collective-permute-done | bytes 12320 | tf_op jit(solution)/shard_map/ppermute | solution.py:212
  50.9 1.5 %collective-permute-start.15 = (f32[1,3072]{1,0:T(1,128)S(1)}, f32[1,3072]{1,0:T(1,128)S(1)}, u32[]{:S(2)}, u32[]{:S(2)}) collective-permute-start(f32[1,3072]{1,0:T(1,128)S(1)} %sum.5.refs_1_), channel_id=1, source_target_pairs={{0,5},{1,4},{2,7},{3,6},{4,1},{5,0},{6,3},{7,2},{8,13},{9,12},{10,... | collective-permute-start | bytes 36872 | tf_op jit(solution)/shard_map/ppermute | solution.py:212
  52.4 1.6 %collective-permute-done.15.refs_0_ = f32[1,3072]{1,0:T(1,128)S(1)} collective-permute-done((f32[1,3072]{1,0:T(1,128)S(1)}, f32[1,3072]{1,0:T(1,128)S(1)}, u32[]{:S(2)}, u32[]{:S(2)}) %collective-permute-start.15) | collective-permute-done | bytes 12320 | tf_op jit(solution)/shard_map/ppermute | solution.py:212
  54.0 2.5 %collective-permute-start.16 = (f32[1,3072]{1,0:T(1,128)S(1)}, f32[1,3072]{1,0:T(1,128)S(1)}, u32[]{:S(2)}, u32[]{:S(2)}) collective-permute-start(f32[1,3072]{1,0:T(1,128)S(1)} %sum.6.refs_1_), channel_id=1, source_target_pairs={{0,6},{1,7},{2,4},{3,5},{4,2},{5,3},{6,0},{7,1},{8,14},{9,15},{10,... | collective-permute-start | bytes 36872 | tf_op jit(solution)/shard_map/ppermute | solution.py:212
  56.5 1.0 %branch.1 = bf16[1,128,3072]{2,1,0:T(8,128)(2,1)} custom-call(f32[128,3072]{1,0:T(8,128)S(1)} %get-tuple-element.42.projected_ref, f32[1,3072]{1,0:T(1,128)S(1)} %bitcast.2), custom_call_target="tpu_custom_call" | custom-call | tf_op jit(solution)/shard_map/branch/pallas_call | solution.py:352
  57.5 0.5 collective-permute-done.16.refs_0_
  58.0 0.6 %sum.7 = f32[1,3072]{1,0:T(1,128)} custom-call(f32[1,3072]{1,0:T(1,128)S(1)} %collective-permute-done.16.refs_0_, f32[1,3072]{1,0:T(1,128)S(1)} %sum.6.refs_1_), custom_call_target="tpu_custom_call" | custom-call | tf_op jit(solution)/shard_map/sum/pallas_call | solution.py:213
  (21 shorter events, 1.1 us)
Async XLA Ops:
  2.2 13.1 %collective-permute-start = (bf16[784,256]{1,0:T(8,128)(2,1)S(1)}, bf16[784,256]{1,0:T(8,128)(2,1)S(1)}, u32[]{:S(2)}, u32[]{:S(2)}) collective-permute-start(bf16[784,256]{1,0:T(8,128)(2,1)S(1)} %get-tuple-element.24), channel_id=1, source_target_pairs={{0,28},{4,24},{8,20},{12,16},{16,12},{20,8},{24,4},{28,0},{1,29},{... | collective-permute-start | bytes 1204232 | tf_op jit(solution)/shard_map/ppermute | solution.py:244
  5.6 19.1 %collective-permute-start.1 = (bf16[784,256]{1,0:T(8,128)(2,1)S(1)}, bf16[784,256]{1,0:T(8,128)(2,1)S(1)}, u32[]{:S(2)}, u32[]{:S(2)}) collective-permute-start(bf16[784,256]{1,0:T(8,128)(2,1)S(1)} %get-tuple-element.25), channel_id=1, source_target_pairs={{0,12},{4,16},{8,4},{12,24},{16,28},{20,0},{24,20},{28,8},{1,13},{... | collective-permute-start | bytes 1204232 | tf_op jit(solution)/shard_map/ppermute | solution.py:244
  6.5 18.6 %collective-permute-start.2 = (bf16[784,256]{1,0:T(8,128)(2,1)S(1)}, bf16[784,256]{1,0:T(8,128)(2,1)S(1)}, u32[]{:S(2)}, u32[]{:S(2)}) collective-permute-start(bf16[784,256]{1,0:T(8,128)(2,1)S(1)} %get-tuple-element.26), channel_id=1, source_target_pairs={{0,20},{4,8},{8,28},{12,0},{16,4},{20,24},{24,12},{28,16},{1,21},{... | collective-permute-start | bytes 1204232 | tf_op jit(solution)/shard_map/ppermute | solution.py:244
  8.8 19.4 %collective-permute-start.9 = (bf16[384,256]{1,0:T(8,128)(2,1)S(1)}, bf16[384,256]{1,0:T(8,128)(2,1)S(1)}, u32[]{:S(2)}, u32[]{:S(2)}) collective-permute-start(bf16[384,256]{1,0:T(8,128)(2,1)S(1)} %get-tuple-element.38), channel_id=1, source_target_pairs={{0,28},{4,24},{8,20},{12,16},{16,12},{20,8},{24,4},{28,0},{1,29},{... | collective-permute-start | bytes 589832 | tf_op jit(solution)/shard_map/ppermute | solution.py:244
  8.9 27.5 %collective-permute-start.5 = (bf16[384,256]{1,0:T(8,128)(2,1)S(1)}, bf16[384,256]{1,0:T(8,128)(2,1)S(1)}, u32[]{:S(2)}, u32[]{:S(2)}) collective-permute-start(bf16[384,256]{1,0:T(8,128)(2,1)S(1)} %get-tuple-element.33), channel_id=1, source_target_pairs={{0,12},{4,16},{8,4},{12,24},{16,28},{20,0},{24,20},{28,8},{1,13},{... | collective-permute-start | bytes 589832 | tf_op jit(solution)/shard_map/ppermute | solution.py:244
  15.4 21.0 %collective-permute-start.6 = (bf16[384,256]{1,0:T(8,128)(2,1)S(1)}, bf16[384,256]{1,0:T(8,128)(2,1)S(1)}, u32[]{:S(2)}, u32[]{:S(2)}) collective-permute-start(bf16[384,256]{1,0:T(8,128)(2,1)S(1)} %get-tuple-element.34), channel_id=1, source_target_pairs={{0,20},{4,8},{8,28},{12,0},{16,4},{20,24},{24,12},{28,16},{1,21},{... | collective-permute-start | bytes 589832 | tf_op jit(solution)/shard_map/ppermute | solution.py:244
  24.7 3.5 %collective-permute-start.3 = (bf16[1664,256]{1,0:T(8,128)(2,1)S(1)}, bf16[1664,256]{1,0:T(8,128)(2,1)S(1)}, u32[]{:S(2)}, u32[]{:S(2)}) collective-permute-start(bf16[1664,256]{1,0:T(8,128)(2,1)S(1)} %get-tuple-element.31), channel_id=1, source_target_pairs={{0,4},{4,0},{8,12},{12,8},{16,20},{20,16},{24,28},{28,24},{1,5},{5... | collective-permute-start | bytes 2555912 | tf_op jit(solution)/shard_map/ppermute | solution.py:236
  25.2 3.1 %collective-permute-start.4 = (bf16[1664,256]{1,0:T(8,128)(2,1)S(1)}, bf16[1664,256]{1,0:T(8,128)(2,1)S(1)}, u32[]{:S(2)}, u32[]{:S(2)}) collective-permute-start(bf16[1664,256]{1,0:T(8,128)(2,1)S(1)} %get-tuple-element.32), channel_id=1, source_target_pairs={{0,4},{4,0},{8,12},{12,8},{16,20},{20,16},{24,28},{28,24},{1,5},{5... | collective-permute-start | bytes 2555912 | tf_op jit(solution)/shard_map/ppermute | solution.py:236
  30.7 10.5 %collective-permute-start.10 = (bf16[128,384]{1,0:T(8,128)(2,1)S(1)}, bf16[128,384]{1,0:T(8,128)(2,1)S(1)}, u32[]{:S(2)}, u32[]{:S(2)}) collective-permute-start(bf16[128,384]{1,0:T(8,128)(2,1)S(1)} %get-tuple-element.39), channel_id=1, source_target_pairs={{28,0},{24,4},{20,8},{16,12},{12,16},{8,20},{4,24},{0,28},{29,1},{... | collective-permute-start | bytes 294920 | tf_op jit(solution)/shard_map/ppermute | solution.py:247
  38.8 4.8 %collective-permute-start.8 = (bf16[128,384]{1,0:T(8,128)(2,1)S(1)}, bf16[128,384]{1,0:T(8,128)(2,1)S(1)}, u32[]{:S(2)}, u32[]{:S(2)}) collective-permute-start(bf16[128,384]{1,0:T(8,128)(2,1)S(1)} %get-tuple-element.37), channel_id=1, source_target_pairs={{12,0},{16,4},{4,8},{24,12},{28,16},{0,20},{20,24},{8,28},{13,1},{... | collective-permute-start | bytes 294920 | tf_op jit(solution)/shard_map/ppermute | solution.py:247
  38.8 5.4 %collective-permute-start.7 = (bf16[128,384]{1,0:T(8,128)(2,1)S(1)}, bf16[128,384]{1,0:T(8,128)(2,1)S(1)}, u32[]{:S(2)}, u32[]{:S(2)}) collective-permute-start(bf16[128,384]{1,0:T(8,128)(2,1)S(1)} %get-tuple-element.35), channel_id=1, source_target_pairs={{20,0},{8,4},{28,8},{0,12},{4,16},{24,20},{12,24},{16,28},{21,1},{... | collective-permute-start | bytes 294920 | tf_op jit(solution)/shard_map/ppermute | solution.py:247
  44.3 12.3 %copy-start = (f32[3072]{0:T(1024)S(1)}, f32[3072]{0:T(1024)}, u32[]{:S(2)}) copy-start(f32[3072]{0:T(1024)} %param.20) | copy-start | bytes 36868
  45.0 1.2 %collective-permute-start.11 = (f32[1,3072]{1,0:T(1,128)S(1)}, f32[1,3072]{1,0:T(1,128)S(1)}, u32[]{:S(2)}, u32[]{:S(2)}) collective-permute-start(f32[1,3072]{1,0:T(1,128)S(1)} %get-tuple-element.43.refs_1_), channel_id=1, source_target_pairs={{0,4},{1,5},{2,6},{3,7},{4,0},{5,1},{6,2},{7,3},{8,12},{9,13},{10,... | collective-permute-start | bytes 36872 | tf_op jit(solution)/shard_map/ppermute | solution.py:212
  46.2 4.0 %collective-permute-start.12 = (f32[1,3072]{1,0:T(1,128)S(1)}, f32[1,3072]{1,0:T(1,128)S(1)}, u32[]{:S(2)}, u32[]{:S(2)}) collective-permute-start(f32[1,3072]{1,0:T(1,128)S(1)} %sum.4.refs_3_), channel_id=1, source_target_pairs={{0,28},{1,29},{2,30},{3,31},{4,24},{5,25},{6,26},{7,27},{8,20},{9,... | collective-permute-start | bytes 36872 | tf_op jit(solution)/shard_map/ppermute | solution.py:212
  46.2 4.0 %collective-permute-start.13 = (f32[1,3072]{1,0:T(1,128)S(1)}, f32[1,3072]{1,0:T(1,128)S(1)}, u32[]{:S(2)}, u32[]{:S(2)}) collective-permute-start(f32[1,3072]{1,0:T(1,128)S(1)} %sum.4.refs_3_), channel_id=1, source_target_pairs={{0,20},{1,21},{2,22},{3,23},{4,16},{5,17},{6,18},{7,19},{8,28},{9,... | collective-permute-start | bytes 36872 | tf_op jit(solution)/shard_map/ppermute | solution.py:212
  47.8 3.1 %collective-permute-start.14 = (f32[1,3072]{1,0:T(1,128)S(1)}, f32[1,3072]{1,0:T(1,128)S(1)}, u32[]{:S(2)}, u32[]{:S(2)}) collective-permute-start(f32[1,3072]{1,0:T(1,128)S(1)} %sum.4.refs_3_), channel_id=1, source_target_pairs={{0,12},{1,13},{2,14},{3,15},{4,8},{5,9},{6,10},{7,11},{8,4},{9,5},... | collective-permute-start | bytes 36872 | tf_op jit(solution)/shard_map/ppermute | solution.py:212
  50.9 3.1 %collective-permute-start.15 = (f32[1,3072]{1,0:T(1,128)S(1)}, f32[1,3072]{1,0:T(1,128)S(1)}, u32[]{:S(2)}, u32[]{:S(2)}) collective-permute-start(f32[1,3072]{1,0:T(1,128)S(1)} %sum.5.refs_1_), channel_id=1, source_target_pairs={{0,5},{1,4},{2,7},{3,6},{4,1},{5,0},{6,3},{7,2},{8,13},{9,12},{10,... | collective-permute-start | bytes 36872 | tf_op jit(solution)/shard_map/ppermute | solution.py:212
  54.0 4.0 %collective-permute-start.16 = (f32[1,3072]{1,0:T(1,128)S(1)}, f32[1,3072]{1,0:T(1,128)S(1)}, u32[]{:S(2)}, u32[]{:S(2)}) collective-permute-start(f32[1,3072]{1,0:T(1,128)S(1)} %sum.6.refs_1_), channel_id=1, source_target_pairs={{0,6},{1,7},{2,4},{3,5},{4,2},{5,3},{6,0},{7,1},{8,14},{9,15},{10,... | collective-permute-start | bytes 36872 | tf_op jit(solution)/shard_map/ppermute | solution.py:212

commit v2 on v1

--- a/solution.py
+++ b/solution.py
@@ -49,43 +49,53 @@
     return jnp.concatenate(cos_rows, axis=0), jnp.concatenate(sin_rows, axis=0)
 
 
+def odd_one(group, place):
+    bits = group
+    for shift in (4, 2, 1):
+        bits = bits ^ (bits >> shift)
+    return ((bits & 1) + place) % 2
+
+
 def group_of(offsets, members):
     me = lax.axis_index("ctx")
+    group = me // members
     even, odd = offsets
-    offset = even if even == odd else jnp.where(me % members % 2 == 0, even, odd)
-    return (me // members) ^ offset
-
-
-def pack_kernel(route, members, turns, with_ids, order_hbm, ids_hbm, *refs):
+    return group ^ (even if even == odd else jnp.where(odd_one(group, me % members) == 0, even, odd))
+
+
+def pack_kernel(offsets, members, turns, with_ids, order_hbm, ids_hbm, *refs):
     n_in = 2 * len(turns)
     sources, outs, (scratch, in_sems, order_ref, ids_ref, small_sems) = refs[:n_in], refs[n_in:-5], refs[-5:]
-    loads = [pltpu.make_async_copy(order_hbm, order_ref, small_sems.at[0]), pltpu.make_async_copy(ids_hbm, ids_ref, small_sems.at[1])]
-    loads += [pltpu.make_async_copy(source.at[0], scratch.at[t], in_sems.at[t]) for t, source in enumerate(sources)]
-    for load in loads:
+    rows, part = scratch.shape[2:]
+    head_dim = outs[0].shape[1] // 2
+    per_group = part // head_dim
+    small = [pltpu.make_async_copy(order_hbm, order_ref, small_sems.at[0]), pltpu.make_async_copy(ids_hbm, ids_ref, small_sems.at[1])]
+    for load in small:
         load.start()
-    rows, features = scratch.shape[1:]
-    per_group = HEADS // len(route)
-    head_dim = features // HEADS
-    places = [group_of(offsets, members) for offsets in route]
-    loads[0].wait()
+    loads = {}
+    for t, source in enumerate(sources):
+        for p, pair in enumerate(offsets):
+            column = pl.multiple_of(group_of(pair, members) * part, part)
+            loads[t, p] = pltpu.make_async_copy(source.at[0, :, pl.ds(column, part)], scratch.at[t, p], in_sems.at[t, p])
+            loads[t, p].start()
+    small[0].wait()
     cosine, sine = rotation(order_ref, rows, head_dim)
 
     def turned(x):
         x = x.astype(jnp.float32)
         return (x * cosine + pltpu.roll(x, head_dim // 2, 1) * sine).astype(jnp.bfloat16)
 
-    loads[1].wait()
+    small[1].wait()
     if with_ids:
         ids = jnp.broadcast_to(ids_ref[...].astype(jnp.float32), (ID_ROWS, rows)).astype(jnp.bfloat16)
         for out in outs:
             out[per_group * len(turns) * rows :, :head_dim] = ids
             out[per_group * len(turns) * rows :, head_dim:] = ids
     for t in range(n_in):
-        loads[2 + t].wait()
-        for group, out in zip(places, outs):
+        for p, out in enumerate(outs):
+            loads[t, p].wait()
             for i in range(per_group):
-                column = pl.multiple_of((group * per_group + i) * head_dim, head_dim)
-                x = scratch[t, :, pl.ds(column, head_dim)]
+                x = scratch[t, p, :, i * head_dim : (i + 1) * head_dim]
                 at = (i * len(turns) + t // 2) * rows
                 out[at : at + rows, t % 2 * head_dim : (t % 2 + 1) * head_dim] = turned(x) if turns[t // 2] else x
 
@@ -241,10 +251,8 @@
     early, late = [*range(1 + len(far))], [*range(1 + len(far), groups)]
 
     def send(x, place):
-        return lax.ppermute(x, "ctx", [(j, j ^ (route[place][j % members % 2] * members + cross)) for j in range(n_ctx)])
-
-    def send_back(x, place):
-        return lax.ppermute(x, "ctx", [(j ^ (route[place][j % members % 2] * members + cross), j) for j in range(n_ctx)])
+        offset = [route[place][odd_one(j // members, j % members)] for j in range(n_ctx)]
+        return lax.ppermute(x, "ctx", [(j, j ^ (offset[j] * members + cross)) for j in range(n_ctx)])
 
     kv_pack = (2 * per_group * rows + ID_ROWS, 2 * head_dim)
     q_pack = (per_group * rows, 2 * head_dim)
@@ -252,15 +260,15 @@
     def in_hbm(x):
         return pltpu.with_memory_space_constraint(x, pltpu.HBM)
 
-    def pack(name, shape, turns, with_ids, sources):
+    def pack(name, places, shape, turns, with_ids, sources):
         return pl.pallas_call(
-            functools.partial(pack_kernel, route, members, turns, with_ids),
-            out_shape=[pltpu.VMEM(shape, bf16)] * groups,
+            functools.partial(pack_kernel, [route[place] for place in places], members, turns, with_ids),
+            out_shape=[pltpu.VMEM(shape, bf16)] * len(places),
             in_specs=[hbm] * (2 + len(sources)),
-            out_specs=[vmem] * groups,
+            out_specs=[vmem] * len(places),
             scratch_shapes=[
-                pltpu.VMEM((len(sources), rows, features), bf16),
-                pltpu.SemaphoreType.DMA((len(sources),)),
+                pltpu.VMEM((len(sources), len(places), rows, per_group * head_dim), bf16),
+                pltpu.SemaphoreType.DMA((len(sources), len(places))),
                 pltpu.SMEM(block_order.shape, jnp.int32),
                 pltpu.VMEM(clip_ids.shape, jnp.int32),
                 pltpu.SemaphoreType.DMA((2,)),
@@ -269,8 +277,12 @@
             name=name,
         )(*map(in_hbm, (block_order, clip_ids) + sources))
 
-    kv = pack("pack_keys", kv_pack, (True, False), True, (keys, tangent_keys, values, tangent_values))
-    q = list(pack("pack_queries", q_pack, (True,), False, (tangent_queries, queries)))
+    key_sources = (keys, tangent_keys, values, tangent_values)
+    far_kv = pack("pack_far", early[1:], kv_pack, (True, False), True, key_sources)
+    near_kv = pack("pack_near", [0, *late], kv_pack, (True, False), True, key_sources)
+    kv = [near_kv[0], *far_kv, *near_kv[1:]]
+    q = list(pack("pack_queries", range(groups), q_pack, (True,), False, (tangent_queries, queries)))
+
     weight, cot, staged = pl.pallas_call(
         stage_kernel,
         out_shape=[pltpu.VMEM(out_weight.shape, bf16), pltpu.VMEM(cotangent.shape, bf16), pltpu.VMEM((8, 128), jnp.float32)],
@@ -326,10 +338,10 @@
 
     done = dict(zip(early, attend("attend_early", early, arrived)))
     for place in early[1:]:
-        done[place] = send_back(done[place], place)
+        done[place] = send(done[place], place)
     done.update(zip(late, attend("attend_late", late)))
     for place in late:
-        done[place] = send_back(done[place], place)
+        done[place] = send(done[place], place)
     arrivals = [*early, *late]
     begun = None
     for place in arrivals[:-1]:
@@ -359,10 +371,7 @@
     )(projected, layer_scale[None, :])
     summed = exchange_sum(grad, [(s, 0) for s in reversed(range(1, members))])
     summed = exchange_sum(summed, [(offset + cross, 0) for offset in reversed(range(members, n_ctx, members))])
-    factor = 1.0 / math.sqrt(n_ctx * n_dp * rows)
-    offsets = [1 << k for k in range(n_dp.bit_length() - 1)]
-    for offset in offsets:
-        summed = exchange_sum(summed, [(cross, offset)], factor if offset == offsets[-1] else 1.0)
+    summed = exchange_sum(summed, [(cross, offset) for offset in reversed(range(1, n_dp))], 1.0 / math.sqrt(n_ctx * n_dp * rows))
     return branch, summed[0]
 
 

time: 58.8 us -> 56.7 us (0.964)
  starting transfers between devices: 24.5 us -> 21.1 us
  Pallas kernels: 15.9 us -> 17.7 us
    ppermute x9, starting transfers between devices: 16.6 us -> 12.9 us  [send(): lax.ppermute(x, 'ctx', [(j, j ^ offset[j] * members + cross) for j in ran...]
    pallas_call x2 -> x3, Pallas kernels: 3.02 us -> 4.91 us  [pack(): pl.pallas_call(functools.partial(pack_kernel, [route[place] for place in...]
    ppermute x9, waiting for transfers between devices: 12.6 us -> 11.4 us  [send(): lax.ppermute(x, 'ctx', [(j, j ^ offset[j] * members + cross) for j in ran...]
    ppermute x6 -> x7, waiting for transfers between devices: 4.73 us -> 5.18 us  [exchange_sum(): lax.ppermute(x, ('ctx', 'dp'), [(j * n_dp + z, (j ^ own) * n_dp + (z ^ ot...]
    ppermute x6 -> x7, starting transfers between devices: 7.35 us -> 7.66 us  [exchange_sum(): lax.ppermute(x, ('ctx', 'dp'), [(j * n_dp + z, (j ^ own) * n_dp + (z ^ ot...]
  transfers between devices with their start and end apart: 17 -> 18, of which waited for: 10 -> 10; matrix products, arithmetic and copies ran while one was open for 0% -> 0% of each run, Pallas kernels for 22% -> 27%
where the time goes in v2:
time: 56.7 us; the launch traced here: 56.5 us
  starting transfers between devices  21.1 us (37%)
  Pallas kernels  17.7 us (31%)
  waiting for transfers between devices  16.9 us (30%)
  between operations  0.75 us (1%)
    ppermute x9, starting transfers between devices, send(): lax.ppermute(x, 'ctx', [(j, j ^ offset[j] * members + cross) for j in ran...  12.9 us
    ppermute x9, waiting for transfers between devices, send(): lax.ppermute(x, 'ctx', [(j, j ^ offset[j] * members + cross) for j in ran...  11.4 us
    ppermute x7, starting transfers between devices, exchange_sum(): lax.ppermute(x, ('ctx', 'dp'), [(j * n_dp + z, (j ^ own) * n_dp + (z ^ ot...  7.66 us
    ppermute x7, waiting for transfers between devices, exchange_sum(): lax.ppermute(x, ('ctx', 'dp'), [(j * n_dp + z, (j ^ own) * n_dp + (z ^ ot...  5.18 us
    pallas_call x3, Pallas kernels, pack(): pl.pallas_call(functools.partial(pack_kernel, [route[place] for place in...  4.91 us
    pallas_call x2, Pallas kernels, attend(): pl.pallas_call(functools.partial(attend_kernel, groups, members, places,...  4.63 us
    pallas_call x1, Pallas kernels, local(): pl.pallas_call(stage_kernel, out_shape=[pltpu.VMEM(out_weight.shape, bf16...  3.84 us
    pallas_call x3, Pallas kernels, local(): pl.pallas_call(functools.partial(part_kernel, members, route[place], 512)...  1.85 us
  transfers between devices with their start and end apart: 18, of which 10 were waited for; matrix products, arithmetic and copies ran while one was open for 0% of the time, Pallas kernels for 27%

profile of v2, /device:TPU:0, one launch (start us, length us, event | category | flops | bytes accessed | tf_op | source)
XLA Modules:
  0.0 56.5 jit_solution(13917920754680896422)
XLA Ops:
  0.6 1.2 %pack_far.1 = bf16[784,256]{1,0:T(8,128)(2,1)S(1)} custom-call(s32[8]{0:T(128)} %order_hbm.5, s32[1,128]{1,0:T(1,128)} %ids_hbm.5, bf16[1,128,1536]{2,1,0:T(8,128)(2,1)} %refs_0_.4, bf16[1,128,1536]{2,1,0:T(8,128)(2,1)} %refs_1_.4, bf16[1,128,1536]{2,1,0:T(8,128)(2,1)} %refs_2_.3, bf16[1,128,1536]{2,1,0:T(8,128)(2,1)} %refs_3_.3), custom_call_target="tpu_custom_call" | custom-call | tf_op jit(solution)/shard_map/pack_far/pallas_call | solution.py:264
  1.8 3.4 %collective-permute-start = (bf16[784,256]{1,0:T(8,128)(2,1)S(1)}, bf16[784,256]{1,0:T(8,128)(2,1)S(1)}, u32[]{:S(2)}, u32[]{:S(2)}) collective-permute-start(bf16[784,256]{1,0:T(8,128)(2,1)S(1)} %pack_far.1), channel_id=1, source_target_pairs={{0,28},{4,24},{8,20},{12,16},{16,12},{20,8},{24,4},{28,0},{1,29},{... | collective-permute-start | bytes 1204232 | tf_op jit(solution)/shard_map/ppermute | solution.py:255
  5.2 1.9 %pack_near.1 = (bf16[784,256]{1,0:T(8,128)(2,1)S(1)}, bf16[784,256]{1,0:T(8,128)(2,1)S(1)}, bf16[784,256]{1,0:T(8,128)(2,1)S(1)}) custom-call(s32[8]{0:T(128)} %order_hbm.5, s32[1,128]{1,0:T(1,128)} %ids_hbm.5, bf16[1,128,1536]{2,1,0:T(8,128)(2,1)} %refs_0_.4, bf16[1,128,1536]{2,1,0:T(8,128)(2,1)} %refs_1_.4, bf16[1,128,1536]{2,1,0:T(8,128)(2,1)} %refs_2_.3, ...), custom_call_target="tpu_custom_call" | custom-call | tf_op jit(solution)/shard_map/pack_near/pallas_call | solution.py:264
  7.2 0.9 %collective-permute-start.1 = (bf16[784,256]{1,0:T(8,128)(2,1)S(1)}, bf16[784,256]{1,0:T(8,128)(2,1)S(1)}, u32[]{:S(2)}, u32[]{:S(2)}) collective-permute-start(bf16[784,256]{1,0:T(8,128)(2,1)S(1)} %get-tuple-element.23), channel_id=1, source_target_pairs={{0,12},{4,16},{8,28},{12,0},{16,4},{20,24},{24,20},{28,8},{1,13},{... | collective-permute-start | bytes 1204232 | tf_op jit(solution)/shard_map/ppermute | solution.py:255
  8.1 1.8 %pack_queries.1 = (bf16[384,256]{1,0:T(8,128)(2,1)S(1)}, bf16[384,256]{1,0:T(8,128)(2,1)S(1)}, bf16[384,256]{1,0:T(8,128)(2,1)S(1)}, bf16[384,256]{1,0:T(8,128)(2,1)S(1)}) custom-call(s32[8]{0:T(128)} %order_hbm.5, s32[1,128]{1,0:T(1,128)} %ids_hbm.5, bf16[1,128,1536]{2,1,0:T(8,128)(2,1)} %refs_0_.5, bf16[1,128,1536]{2,1,0:T(8,128)(2,1)} %refs_1_.5), custom_call_target="tpu_custom_call" | custom-call | tf_op jit(solution)/shard_map/pack_queries/pallas_call | solution.py:264
  9.9 2.7 %collective-permute-start.9 = (bf16[384,256]{1,0:T(8,128)(2,1)S(1)}, bf16[384,256]{1,0:T(8,128)(2,1)S(1)}, u32[]{:S(2)}, u32[]{:S(2)}) collective-permute-start(bf16[384,256]{1,0:T(8,128)(2,1)S(1)} %get-tuple-element.36), channel_id=1, source_target_pairs={{0,28},{4,24},{8,20},{12,16},{16,12},{20,8},{24,4},{28,0},{1,29},{... | collective-permute-start | bytes 589832 | tf_op jit(solution)/shard_map/ppermute | solution.py:255
  12.6 3.8 %stage.1 = (bf16[1536,3072]{1,0:T(8,128)(2,1)S(1)}, bf16[1,128,3072]{2,1,0:T(8,128)(2,1)S(1)}, f32[8,128]{1,0:T(8,128)S(1)}) custom-call(bf16[1536,3072]{1,0:T(8,128)(2,1)} %w_hbm.1, bf16[1,128,3072]{2,1,0:T(8,128)(2,1)} %cot_hbm.1, bf16[384,256]{1,0:T(8,128)(2,1)S(1)} %get-tuple-element.25.refs_2_.after_ref.refs_0_.refs_8_), custom_call_target="tpu_custom_call" | custom-call | tf_op jit(solution)/shard_map/stage/pallas_call | solution.py:286
  16.4 0.7 %collective-permute-start.6 = (bf16[384,256]{1,0:T(8,128)(2,1)S(1)}, bf16[384,256]{1,0:T(8,128)(2,1)S(1)}, u32[]{:S(2)}, u32[]{:S(2)}) collective-permute-start(bf16[384,256]{1,0:T(8,128)(2,1)S(1)} %get-tuple-element.32), channel_id=1, source_target_pairs={{0,20},{4,8},{8,4},{12,24},{16,28},{20,0},{24,12},{28,16},{1,21},{... | collective-permute-start | bytes 589832 | tf_op jit(solution)/shard_map/ppermute | solution.py:255
  17.2 7.3 %collective-permute-done.1.refs_0_.refs_2_ = bf16[784,256]{1,0:T(8,128)(2,1)S(1)} collective-permute-done((bf16[784,256]{1,0:T(8,128)(2,1)S(1)}, bf16[784,256]{1,0:T(8,128)(2,1)S(1)}, u32[]{:S(2)}, u32[]{:S(2)}) %collective-permute-start.1) | collective-permute-done | bytes 401440 | tf_op jit(solution)/shard_map/ppermute | solution.py:255
  24.7 0.5 collective-permute-start.4
  25.2 2.6 %collective-permute-done.9.refs_1_.refs_9_ = bf16[384,256]{1,0:T(8,128)(2,1)S(1)} collective-permute-done((bf16[384,256]{1,0:T(8,128)(2,1)S(1)}, bf16[384,256]{1,0:T(8,128)(2,1)S(1)}, u32[]{:S(2)}, u32[]{:S(2)}) %collective-permute-start.9) | collective-permute-done | bytes 196640 | tf_op jit(solution)/shard_map/ppermute | solution.py:255
  28.1 2.3 %attend_early.1 = (bf16[128,384]{1,0:T(8,128)(2,1)S(1)}, bf16[128,384]{1,0:T(8,128)(2,1)S(1)}) custom-call(bf16[784,256]{1,0:T(8,128)(2,1)S(1)} %get-tuple-element.22.refs_0_, bf16[784,256]{1,0:T(8,128)(2,1)S(1)} %collective-permute-done.refs_1_, bf16[784,256]{1,0:T(8,128)(2,1)S(1)} %collective-permute-done.1.refs_0_.refs_2_, ...), custom_call_target="tpu_custom_call" | custom-call | tf_op jit(solution)/shard_map/attend_early/pallas_call | solution.py:330
  30.4 2.9 %collective-permute-start.10 = (bf16[128,384]{1,0:T(8,128)(2,1)S(1)}, bf16[128,384]{1,0:T(8,128)(2,1)S(1)}, u32[]{:S(2)}, u32[]{:S(2)}) collective-permute-start(bf16[128,384]{1,0:T(8,128)(2,1)S(1)} %get-tuple-element.37), channel_id=1, source_target_pairs={{0,28},{4,24},{8,20},{12,16},{16,12},{20,8},{24,4},{28,0},{1,29},{... | collective-permute-start | bytes 294920 | tf_op jit(solution)/shard_map/ppermute | solution.py:255
  33.3 2.3 %attend_late.1 = (bf16[128,384]{1,0:T(8,128)(2,1)S(1)}, bf16[128,384]{1,0:T(8,128)(2,1)S(1)}) custom-call(bf16[784,256]{1,0:T(8,128)(2,1)S(1)} %get-tuple-element.22.refs_0_, bf16[784,256]{1,0:T(8,128)(2,1)S(1)} %collective-permute-done.refs_1_, bf16[784,256]{1,0:T(8,128)(2,1)S(1)} %collective-permute-done.1.refs_0_.refs_2_, ...), custom_call_target="tpu_custom_call" | custom-call | tf_op jit(solution)/shard_map/attend_late/pallas_call | solution.py:330
  35.6 1.0 %collective-permute-start.8 = (bf16[128,384]{1,0:T(8,128)(2,1)S(1)}, bf16[128,384]{1,0:T(8,128)(2,1)S(1)}, u32[]{:S(2)}, u32[]{:S(2)}) collective-permute-start(bf16[128,384]{1,0:T(8,128)(2,1)S(1)} %get-tuple-element.35), channel_id=1, source_target_pairs={{0,12},{4,16},{8,28},{12,0},{16,4},{20,24},{24,20},{28,8},{1,13},{... | collective-permute-start | bytes 294920 | tf_op jit(solution)/shard_map/ppermute | solution.py:255
  36.6 1.4 %collective-permute-start.7 = (bf16[128,384]{1,0:T(8,128)(2,1)S(1)}, bf16[128,384]{1,0:T(8,128)(2,1)S(1)}, u32[]{:S(2)}, u32[]{:S(2)}) collective-permute-start(bf16[128,384]{1,0:T(8,128)(2,1)S(1)} %get-tuple-element.33), channel_id=1, source_target_pairs={{0,20},{4,8},{8,4},{12,24},{16,28},{20,0},{24,12},{28,16},{1,21},{... | collective-permute-start | bytes 294920 | tf_op jit(solution)/shard_map/ppermute | solution.py:255
  38.0 0.6 %part0.1.refs_0_ = f32[128,3072]{1,0:T(8,128)S(1)} custom-call(bf16[128,384]{1,0:T(8,128)(2,1)S(1)} %get-tuple-element.38.ta_ref, bf16[1536,3072]{1,0:T(8,128)(2,1)S(1)} %get-tuple-element.34.w_ref), custom_call_target="tpu_custom_call" | custom-call | tf_op jit(solution)/shard_map/part0/pallas_call | solution.py:348
  38.6 0.6 %part1.1.refs_0_ = f32[128,3072]{1,0:T(8,128)S(1)} custom-call(bf16[128,384]{1,0:T(8,128)(2,1)S(1)} %collective-permute-done.10.ta_ref, bf16[1536,3072]{1,0:T(8,128)(2,1)S(1)} %get-tuple-element.34.w_ref, f32[128,3072]{1,0:T(8,128)S(1)} %part0.1.refs_0_), custom_call_target="tpu_custom_call" | custom-call | tf_op jit(solution)/shard_map/part1/pallas_call | solution.py:348
  39.7 0.6 %part2.1.begun_ref = f32[128,3072]{1,0:T(8,128)S(1)} custom-call(bf16[128,384]{1,0:T(8,128)(2,1)S(1)} %collective-permute-done.8.ta_ref, bf16[1536,3072]{1,0:T(8,128)(2,1)S(1)} %get-tuple-element.34.w_ref, f32[128,3072]{1,0:T(8,128)S(1)} %part1.1.refs_0_), custom_call_target="tpu_custom_call" | custom-call | tf_op jit(solution)/shard_map/part2/pallas_call | solution.py:348
  40.4 1.1 %collective-permute-done.7.ta_ref = bf16[128,384]{1,0:T(8,128)(2,1)S(1)} collective-permute-done((bf16[128,384]{1,0:T(8,128)(2,1)S(1)}, bf16[128,384]{1,0:T(8,128)(2,1)S(1)}, u32[]{:S(2)}, u32[]{:S(2)}) %collective-permute-start.7) | collective-permute-done | bytes 98336 | tf_op jit(solution)/shard_map/ppermute | solution.py:255
  41.4 0.6 %project.1 = (f32[128,3072]{1,0:T(8,128)S(1)}, f32[1,3072]{1,0:T(1,128)S(1)}) custom-call(bf16[128,384]{1,0:T(8,128)(2,1)S(1)} %collective-permute-done.7.ta_ref, bf16[1536,3072]{1,0:T(8,128)(2,1)S(1)} %get-tuple-element.34.w_ref, f32[128,3072]{1,0:T(8,128)S(1)} %part2.1.begun_ref, bf16[1,128,3072]{2,1,0:T(8,128)(2,1)S(1)} %get-tuple-element.39.cot_ref), custom_call_target="tpu_custom_call" | custom-call | tf_op jit(solution)/shard_map/project/pallas_call | solution.py:356
  42.1 0.5 collective-permute-start.11
  42.6 0.8 %collective-permute-done.11.refs_0_ = f32[1,3072]{1,0:T(1,128)S(1)} collective-permute-done((f32[1,3072]{1,0:T(1,128)S(1)}, f32[1,3072]{1,0:T(1,128)S(1)}, u32[]{:S(2)}, u32[]{:S(2)}) %collective-permute-start.11) | collective-permute-done | bytes 12320 | tf_op jit(solution)/shard_map/ppermute | solution.py:222
  43.5 1.7 %collective-permute-start.12 = (f32[1,3072]{1,0:T(1,128)S(1)}, f32[1,3072]{1,0:T(1,128)S(1)}, u32[]{:S(2)}, u32[]{:S(2)}) collective-permute-start(f32[1,3072]{1,0:T(1,128)S(1)} %sum.3.refs_3_), channel_id=1, source_target_pairs={{0,28},{1,29},{2,30},{3,31},{4,24},{5,25},{6,26},{7,27},{8,20},{9,... | collective-permute-start | bytes 36872 | tf_op jit(solution)/shard_map/ppermute | solution.py:222
  45.4 1.3 %collective-permute-start.14 = (f32[1,3072]{1,0:T(1,128)S(1)}, f32[1,3072]{1,0:T(1,128)S(1)}, u32[]{:S(2)}, u32[]{:S(2)}) collective-permute-start(f32[1,3072]{1,0:T(1,128)S(1)} %sum.3.refs_3_), channel_id=1, source_target_pairs={{0,12},{1,13},{2,14},{3,15},{4,8},{5,9},{6,10},{7,11},{8,4},{9,5},... | collective-permute-start | bytes 36872 | tf_op jit(solution)/shard_map/ppermute | solution.py:222
  46.6 0.9 %collective-permute-done.12.refs_0_ = f32[1,3072]{1,0:T(1,128)S(1)} collective-permute-done((f32[1,3072]{1,0:T(1,128)S(1)}, f32[1,3072]{1,0:T(1,128)S(1)}, u32[]{:S(2)}, u32[]{:S(2)}) %collective-permute-start.12) | collective-permute-done | bytes 12320 | tf_op jit(solution)/shard_map/ppermute | solution.py:222
  47.5 0.8 %collective-permute-done.13.refs_1_ = f32[1,3072]{1,0:T(1,128)S(1)} collective-permute-done((f32[1,3072]{1,0:T(1,128)S(1)}, f32[1,3072]{1,0:T(1,128)S(1)}, u32[]{:S(2)}, u32[]{:S(2)}) %collective-permute-start.13) | collective-permute-done | bytes 12320 | tf_op jit(solution)/shard_map/ppermute | solution.py:222
  48.5 3.4 %collective-permute-start.15 = (f32[1,3072]{1,0:T(1,128)S(1)}, f32[1,3072]{1,0:T(1,128)S(1)}, u32[]{:S(2)}, u32[]{:S(2)}) collective-permute-start(f32[1,3072]{1,0:T(1,128)S(1)} %sum.4.refs_3_), channel_id=1, source_target_pairs={{0,7},{1,6},{2,5},{3,4},{4,3},{5,2},{6,1},{7,0},{8,15},{9,14},{10,... | collective-permute-start | bytes 36872 | tf_op jit(solution)/shard_map/ppermute | solution.py:222
  51.9 0.6 collective-permute-start.17
  52.4 1.0 %branch.1 = bf16[1,128,3072]{2,1,0:T(8,128)(2,1)} custom-call(f32[128,3072]{1,0:T(8,128)S(1)} %get-tuple-element.40.projected_ref, f32[1,3072]{1,0:T(1,128)S(1)} %bitcast.2), custom_call_target="tpu_custom_call" | custom-call | tf_op jit(solution)/shard_map/branch/pallas_call | solution.py:364
  53.4 2.5 %collective-permute-done.16.refs_1_ = f32[1,3072]{1,0:T(1,128)S(1)} collective-permute-done((f32[1,3072]{1,0:T(1,128)S(1)}, f32[1,3072]{1,0:T(1,128)S(1)}, u32[]{:S(2)}, u32[]{:S(2)}) %collective-permute-start.16) | collective-permute-done | bytes 12320 | tf_op jit(solution)/shard_map/ppermute | solution.py:222
  55.9 0.6 %sum.5 = f32[1,3072]{1,0:T(1,128)} custom-call(f32[1,3072]{1,0:T(1,128)S(1)} %collective-permute-done.15.refs_0_, f32[1,3072]{1,0:T(1,128)S(1)} %collective-permute-done.16.refs_1_, f32[1,3072]{1,0:T(1,128)S(1)} %collective-permute-done.17.refs_2_, f32[1,3072]{1,0:T(1,128)S(1)} %sum.4.refs_3_), custom_call_target="tpu_custom_call" | custom-call | tf_op jit(solution)/shard_map/sum/pallas_call | solution.py:223
  (23 shorter events, 1.5 us)
Async XLA Ops:
  1.8 14.6 %collective-permute-start = (bf16[784,256]{1,0:T(8,128)(2,1)S(1)}, bf16[784,256]{1,0:T(8,128)(2,1)S(1)}, u32[]{:S(2)}, u32[]{:S(2)}) collective-permute-start(bf16[784,256]{1,0:T(8,128)(2,1)S(1)} %pack_far.1), channel_id=1, source_target_pairs={{0,28},{4,24},{8,20},{12,16},{16,12},{20,8},{24,4},{28,0},{1,29},{... | collective-permute-start | bytes 1204232 | tf_op jit(solution)/shard_map/ppermute | solution.py:255
  7.2 17.4 %collective-permute-start.1 = (bf16[784,256]{1,0:T(8,128)(2,1)S(1)}, bf16[784,256]{1,0:T(8,128)(2,1)S(1)}, u32[]{:S(2)}, u32[]{:S(2)}) collective-permute-start(bf16[784,256]{1,0:T(8,128)(2,1)S(1)} %get-tuple-element.23), channel_id=1, source_target_pairs={{0,12},{4,16},{8,28},{12,0},{16,4},{20,24},{24,20},{28,8},{1,13},{... | collective-permute-start | bytes 1204232 | tf_op jit(solution)/shard_map/ppermute | solution.py:255
  8.1 16.5 %collective-permute-start.2 = (bf16[784,256]{1,0:T(8,128)(2,1)S(1)}, bf16[784,256]{1,0:T(8,128)(2,1)S(1)}, u32[]{:S(2)}, u32[]{:S(2)}) collective-permute-start(bf16[784,256]{1,0:T(8,128)(2,1)S(1)} %get-tuple-element.24), channel_id=1, source_target_pairs={{0,20},{4,8},{8,4},{12,24},{16,28},{20,0},{24,12},{28,16},{1,21},{... | collective-permute-start | bytes 1204232 | tf_op jit(solution)/shard_map/ppermute | solution.py:255
  9.9 17.9 %collective-permute-start.9 = (bf16[384,256]{1,0:T(8,128)(2,1)S(1)}, bf16[384,256]{1,0:T(8,128)(2,1)S(1)}, u32[]{:S(2)}, u32[]{:S(2)}) collective-permute-start(bf16[384,256]{1,0:T(8,128)(2,1)S(1)} %get-tuple-element.36), channel_id=1, source_target_pairs={{0,28},{4,24},{8,20},{12,16},{16,12},{20,8},{24,4},{28,0},{1,29},{... | collective-permute-start | bytes 589832 | tf_op jit(solution)/shard_map/ppermute | solution.py:255
  12.6 20.7 %collective-permute-start.5 = (bf16[384,256]{1,0:T(8,128)(2,1)S(1)}, bf16[384,256]{1,0:T(8,128)(2,1)S(1)}, u32[]{:S(2)}, u32[]{:S(2)}) collective-permute-start(bf16[384,256]{1,0:T(8,128)(2,1)S(1)} %get-tuple-element.31), channel_id=1, source_target_pairs={{0,12},{4,16},{8,28},{12,0},{16,4},{20,24},{24,20},{28,8},{1,13},{... | collective-permute-start | bytes 589832 | tf_op jit(solution)/shard_map/ppermute | solution.py:255
  16.4 16.9 %collective-permute-start.6 = (bf16[384,256]{1,0:T(8,128)(2,1)S(1)}, bf16[384,256]{1,0:T(8,128)(2,1)S(1)}, u32[]{:S(2)}, u32[]{:S(2)}) collective-permute-start(bf16[384,256]{1,0:T(8,128)(2,1)S(1)} %get-tuple-element.32), channel_id=1, source_target_pairs={{0,20},{4,8},{8,4},{12,24},{16,28},{20,0},{24,12},{28,16},{1,21},{... | collective-permute-start | bytes 589832 | tf_op jit(solution)/shard_map/ppermute | solution.py:255
  24.5 3.3 %collective-permute-start.3 = (bf16[1664,256]{1,0:T(8,128)(2,1)S(1)}, bf16[1664,256]{1,0:T(8,128)(2,1)S(1)}, u32[]{:S(2)}, u32[]{:S(2)}) collective-permute-start(bf16[1664,256]{1,0:T(8,128)(2,1)S(1)} %get-tuple-element.29), channel_id=1, source_target_pairs={{0,4},{4,0},{8,12},{12,8},{16,20},{20,16},{24,28},{28,24},{1,5},{5... | collective-permute-start | bytes 2555912 | tf_op jit(solution)/shard_map/ppermute | solution.py:246
  24.7 3.4 %collective-permute-start.4 = (bf16[1664,256]{1,0:T(8,128)(2,1)S(1)}, bf16[1664,256]{1,0:T(8,128)(2,1)S(1)}, u32[]{:S(2)}, u32[]{:S(2)}) collective-permute-start(bf16[1664,256]{1,0:T(8,128)(2,1)S(1)} %get-tuple-element.30), channel_id=1, source_target_pairs={{0,4},{4,0},{8,12},{12,8},{16,20},{20,16},{24,28},{28,24},{1,5},{5... | collective-permute-start | bytes 2555912 | tf_op jit(solution)/shard_map/ppermute | solution.py:246
  30.4 8.1 %collective-permute-start.10 = (bf16[128,384]{1,0:T(8,128)(2,1)S(1)}, bf16[128,384]{1,0:T(8,128)(2,1)S(1)}, u32[]{:S(2)}, u32[]{:S(2)}) collective-permute-start(bf16[128,384]{1,0:T(8,128)(2,1)S(1)} %get-tuple-element.37), channel_id=1, source_target_pairs={{0,28},{4,24},{8,20},{12,16},{16,12},{20,8},{24,4},{28,0},{1,29},{... | collective-permute-start | bytes 294920 | tf_op jit(solution)/shard_map/ppermute | solution.py:255
  35.6 4.1 %collective-permute-start.8 = (bf16[128,384]{1,0:T(8,128)(2,1)S(1)}, bf16[128,384]{1,0:T(8,128)(2,1)S(1)}, u32[]{:S(2)}, u32[]{:S(2)}) collective-permute-start(bf16[128,384]{1,0:T(8,128)(2,1)S(1)} %get-tuple-element.35), channel_id=1, source_target_pairs={{0,12},{4,16},{8,28},{12,0},{16,4},{20,24},{24,20},{28,8},{1,13},{... | collective-permute-start | bytes 294920 | tf_op jit(solution)/shard_map/ppermute | solution.py:255
  36.6 4.8 %collective-permute-start.7 = (bf16[128,384]{1,0:T(8,128)(2,1)S(1)}, bf16[128,384]{1,0:T(8,128)(2,1)S(1)}, u32[]{:S(2)}, u32[]{:S(2)}) collective-permute-start(bf16[128,384]{1,0:T(8,128)(2,1)S(1)} %get-tuple-element.33), channel_id=1, source_target_pairs={{0,20},{4,8},{8,4},{12,24},{16,28},{20,0},{24,12},{28,16},{1,21},{... | collective-permute-start | bytes 294920 | tf_op jit(solution)/shard_map/ppermute | solution.py:255
  41.4 11.0 %copy-start = (f32[3072]{0:T(1024)S(1)}, f32[3072]{0:T(1024)}, u32[]{:S(2)}) copy-start(f32[3072]{0:T(1024)} %param.20) | copy-start | bytes 36868
  42.1 1.4 %collective-permute-start.11 = (f32[1,3072]{1,0:T(1,128)S(1)}, f32[1,3072]{1,0:T(1,128)S(1)}, u32[]{:S(2)}, u32[]{:S(2)}) collective-permute-start(f32[1,3072]{1,0:T(1,128)S(1)} %get-tuple-element.41.refs_1_), channel_id=1, source_target_pairs={{0,4},{1,5},{2,6},{3,7},{4,0},{5,1},{6,2},{7,3},{8,12},{9,13},{10,... | collective-permute-start | bytes 36872 | tf_op jit(solution)/shard_map/ppermute | solution.py:222
  43.5 4.0 %collective-permute-start.12 = (f32[1,3072]{1,0:T(1,128)S(1)}, f32[1,3072]{1,0:T(1,128)S(1)}, u32[]{:S(2)}, u32[]{:S(2)}) collective-permute-start(f32[1,3072]{1,0:T(1,128)S(1)} %sum.3.refs_3_), channel_id=1, source_target_pairs={{0,28},{1,29},{2,30},{3,31},{4,24},{5,25},{6,26},{7,27},{8,20},{9,... | collective-permute-start | bytes 36872 | tf_op jit(solution)/shard_map/ppermute | solution.py:222
  45.2 3.1 %collective-permute-start.13 = (f32[1,3072]{1,0:T(1,128)S(1)}, f32[1,3072]{1,0:T(1,128)S(1)}, u32[]{:S(2)}, u32[]{:S(2)}) collective-permute-start(f32[1,3072]{1,0:T(1,128)S(1)} %sum.3.refs_3_), channel_id=1, source_target_pairs={{0,20},{1,21},{2,22},{3,23},{4,16},{5,17},{6,18},{7,19},{8,28},{9,... | collective-permute-start | bytes 36872 | tf_op jit(solution)/shard_map/ppermute | solution.py:222
  45.4 3.1 %collective-permute-start.14 = (f32[1,3072]{1,0:T(1,128)S(1)}, f32[1,3072]{1,0:T(1,128)S(1)}, u32[]{:S(2)}, u32[]{:S(2)}) collective-permute-start(f32[1,3072]{1,0:T(1,128)S(1)} %sum.3.refs_3_), channel_id=1, source_target_pairs={{0,12},{1,13},{2,14},{3,15},{4,8},{5,9},{6,10},{7,11},{8,4},{9,5},... | collective-permute-start | bytes 36872 | tf_op jit(solution)/shard_map/ppermute | solution.py:222
  48.5 4.9 %collective-permute-start.15 = (f32[1,3072]{1,0:T(1,128)S(1)}, f32[1,3072]{1,0:T(1,128)S(1)}, u32[]{:S(2)}, u32[]{:S(2)}) collective-permute-start(f32[1,3072]{1,0:T(1,128)S(1)} %sum.4.refs_3_), channel_id=1, source_target_pairs={{0,7},{1,6},{2,5},{3,4},{4,3},{5,2},{6,1},{7,0},{8,15},{9,14},{10,... | collective-permute-start | bytes 36872 | tf_op jit(solution)/shard_map/ppermute | solution.py:222
  51.9 4.0 %collective-permute-start.16 = (f32[1,3072]{1,0:T(1,128)S(1)}, f32[1,3072]{1,0:T(1,128)S(1)}, u32[]{:S(2)}, u32[]{:S(2)}) collective-permute-start(f32[1,3072]{1,0:T(1,128)S(1)} %sum.4.refs_3_), channel_id=1, source_target_pairs={{0,6},{1,7},{2,4},{3,5},{4,2},{5,3},{6,0},{7,1},{8,14},{9,15},{10,... | collective-permute-start | bytes 36872 | tf_op jit(solution)/shard_map/ppermute | solution.py:222
  51.9 4.0 %collective-permute-start.17 = (f32[1,3072]{1,0:T(1,128)S(1)}, f32[1,3072]{1,0:T(1,128)S(1)}, u32[]{:S(2)}, u32[]{:S(2)}) collective-permute-start(f32[1,3072]{1,0:T(1,128)S(1)} %sum.4.refs_3_), channel_id=1, source_target_pairs={{0,5},{1,4},{2,7},{3,6},{4,1},{5,0},{6,3},{7,2},{8,13},{9,12},{10,... | collective-permute-start | bytes 36872 | tf_op jit(solution)/shard_map/ppermute | solution.py:222

commit v3 on v2

--- a/solution.py
+++ b/solution.py
@@ -371,7 +371,10 @@
     )(projected, layer_scale[None, :])
     summed = exchange_sum(grad, [(s, 0) for s in reversed(range(1, members))])
     summed = exchange_sum(summed, [(offset + cross, 0) for offset in reversed(range(members, n_ctx, members))])
-    summed = exchange_sum(summed, [(cross, offset) for offset in reversed(range(1, n_dp))], 1.0 / math.sqrt(n_ctx * n_dp * rows))
+    factor = 1.0 / math.sqrt(n_ctx * n_dp * rows)
+    offsets = [1 << k for k in range(n_dp.bit_length() - 1)]
+    for offset in offsets:
+        summed = exchange_sum(summed, [(cross, offset)], factor if offset == offsets[-1] else 1.0)
     return branch, summed[0]
 
 

time: 56.7 us -> 56.5 us (level)
    ppermute x7 -> x6, starting transfers between devices: 7.66 us -> 7.43 us  [exchange_sum(): lax.ppermute(x, ('ctx', 'dp'), [(j * n_dp + z, (j ^ own) * n_dp + (z ^ ot...]
    ppermute x7 -> x6, waiting for transfers between devices: 5.18 us -> 5.13 us  [exchange_sum(): lax.ppermute(x, ('ctx', 'dp'), [(j * n_dp + z, (j ^ own) * n_dp + (z ^ ot...]
  transfers between devices with their start and end apart: 18 -> 17, of which waited for: 10 -> 11; matrix products, arithmetic and copies ran while one was open for 0% -> 0% of each run, Pallas kernels for 27% -> 27%
where the time goes in v3:
time: 56.5 us; the launch traced here: 56.2 us
  starting transfers between devices  20.9 us (37%)
  Pallas kernels  17.7 us (31%)
  waiting for transfers between devices  16.9 us (30%)
  between operations  0.75 us (1%)
    ppermute x9, starting transfers between devices, send(): lax.ppermute(x, 'ctx', [(j, j ^ offset[j] * members + cross) for j in ran...  12.9 us
    ppermute x9, waiting for transfers between devices, send(): lax.ppermute(x, 'ctx', [(j, j ^ offset[j] * members + cross) for j in ran...  11.4 us
    ppermute x6, starting transfers between devices, exchange_sum(): lax.ppermute(x, ('ctx', 'dp'), [(j * n_dp + z, (j ^ own) * n_dp + (z ^ ot...  7.43 us
    ppermute x6, waiting for transfers between devices, exchange_sum(): lax.ppermute(x, ('ctx', 'dp'), [(j * n_dp + z, (j ^ own) * n_dp + (z ^ ot...  5.13 us
    pallas_call x3, Pallas kernels, pack(): pl.pallas_call(functools.partial(pack_kernel, [route[place] for place in...  4.91 us
    pallas_call x2, Pallas kernels, attend(): pl.pallas_call(functools.partial(attend_kernel, groups, members, places,...  4.63 us
    pallas_call x1, Pallas kernels, local(): pl.pallas_call(stage_kernel, out_shape=[pltpu.VMEM(out_weight.shape, bf16...  3.84 us
    pallas_call x3, Pallas kernels, local(): pl.pallas_call(functools.partial(part_kernel, members, route[place], 512)...  1.85 us
  transfers between devices with their start and end apart: 17, of which 11 were waited for; matrix products, arithmetic and copies ran while one was open for 0% of the time, Pallas kernels for 27%

profile of v3, /device:TPU:0, one launch (start us, length us, event | category | flops | bytes accessed | tf_op | source)
XLA Modules:
  0.0 56.2 jit_solution(4293646873192040359)
XLA Ops:
  0.6 1.2 %pack_far.1 = bf16[784,256]{1,0:T(8,128)(2,1)S(1)} custom-call(s32[8]{0:T(128)} %order_hbm.5, s32[1,128]{1,0:T(1,128)} %ids_hbm.5, bf16[1,128,1536]{2,1,0:T(8,128)(2,1)} %refs_0_.4, bf16[1,128,1536]{2,1,0:T(8,128)(2,1)} %refs_1_.4, bf16[1,128,1536]{2,1,0:T(8,128)(2,1)} %refs_2_.3, bf16[1,128,1536]{2,1,0:T(8,128)(2,1)} %refs_3_.3), custom_call_target="tpu_custom_call" | custom-call | tf_op jit(solution)/shard_map/pack_far/pallas_call | solution.py:264
  1.8 3.4 %collective-permute-start = (bf16[784,256]{1,0:T(8,128)(2,1)S(1)}, bf16[784,256]{1,0:T(8,128)(2,1)S(1)}, u32[]{:S(2)}, u32[]{:S(2)}) collective-permute-start(bf16[784,256]{1,0:T(8,128)(2,1)S(1)} %pack_far.1), channel_id=1, source_target_pairs={{0,28},{4,24},{8,20},{12,16},{16,12},{20,8},{24,4},{28,0},{1,29},{... | collective-permute-start | bytes 1204232 | tf_op jit(solution)/shard_map/ppermute | solution.py:255
  5.2 1.9 %pack_near.1 = (bf16[784,256]{1,0:T(8,128)(2,1)S(1)}, bf16[784,256]{1,0:T(8,128)(2,1)S(1)}, bf16[784,256]{1,0:T(8,128)(2,1)S(1)}) custom-call(s32[8]{0:T(128)} %order_hbm.5, s32[1,128]{1,0:T(1,128)} %ids_hbm.5, bf16[1,128,1536]{2,1,0:T(8,128)(2,1)} %refs_0_.4, bf16[1,128,1536]{2,1,0:T(8,128)(2,1)} %refs_1_.4, bf16[1,128,1536]{2,1,0:T(8,128)(2,1)} %refs_2_.3, ...), custom_call_target="tpu_custom_call" | custom-call | tf_op jit(solution)/shard_map/pack_near/pallas_call | solution.py:264
  7.2 0.9 %collective-permute-start.1 = (bf16[784,256]{1,0:T(8,128)(2,1)S(1)}, bf16[784,256]{1,0:T(8,128)(2,1)S(1)}, u32[]{:S(2)}, u32[]{:S(2)}) collective-permute-start(bf16[784,256]{1,0:T(8,128)(2,1)S(1)} %get-tuple-element.23), channel_id=1, source_target_pairs={{0,12},{4,16},{8,28},{12,0},{16,4},{20,24},{24,20},{28,8},{1,13},{... | collective-permute-start | bytes 1204232 | tf_op jit(solution)/shard_map/ppermute | solution.py:255
  8.1 1.8 %pack_queries.1 = (bf16[384,256]{1,0:T(8,128)(2,1)S(1)}, bf16[384,256]{1,0:T(8,128)(2,1)S(1)}, bf16[384,256]{1,0:T(8,128)(2,1)S(1)}, bf16[384,256]{1,0:T(8,128)(2,1)S(1)}) custom-call(s32[8]{0:T(128)} %order_hbm.5, s32[1,128]{1,0:T(1,128)} %ids_hbm.5, bf16[1,128,1536]{2,1,0:T(8,128)(2,1)} %refs_0_.5, bf16[1,128,1536]{2,1,0:T(8,128)(2,1)} %refs_1_.5), custom_call_target="tpu_custom_call" | custom-call | tf_op jit(solution)/shard_map/pack_queries/pallas_call | solution.py:264
  9.9 2.7 %collective-permute-start.9 = (bf16[384,256]{1,0:T(8,128)(2,1)S(1)}, bf16[384,256]{1,0:T(8,128)(2,1)S(1)}, u32[]{:S(2)}, u32[]{:S(2)}) collective-permute-start(bf16[384,256]{1,0:T(8,128)(2,1)S(1)} %get-tuple-element.36), channel_id=1, source_target_pairs={{0,28},{4,24},{8,20},{12,16},{16,12},{20,8},{24,4},{28,0},{1,29},{... | collective-permute-start | bytes 589832 | tf_op jit(solution)/shard_map/ppermute | solution.py:255
  12.6 3.8 %stage.1 = (bf16[1536,3072]{1,0:T(8,128)(2,1)S(1)}, bf16[1,128,3072]{2,1,0:T(8,128)(2,1)S(1)}, f32[8,128]{1,0:T(8,128)S(1)}) custom-call(bf16[1536,3072]{1,0:T(8,128)(2,1)} %w_hbm.1, bf16[1,128,3072]{2,1,0:T(8,128)(2,1)} %cot_hbm.1, bf16[384,256]{1,0:T(8,128)(2,1)S(1)} %get-tuple-element.25.refs_2_.after_ref.refs_0_.refs_8_), custom_call_target="tpu_custom_call" | custom-call | tf_op jit(solution)/shard_map/stage/pallas_call | solution.py:286
  16.4 0.7 %collective-permute-start.6 = (bf16[384,256]{1,0:T(8,128)(2,1)S(1)}, bf16[384,256]{1,0:T(8,128)(2,1)S(1)}, u32[]{:S(2)}, u32[]{:S(2)}) collective-permute-start(bf16[384,256]{1,0:T(8,128)(2,1)S(1)} %get-tuple-element.32), channel_id=1, source_target_pairs={{0,20},{4,8},{8,4},{12,24},{16,28},{20,0},{24,12},{28,16},{1,21},{... | collective-permute-start | bytes 589832 | tf_op jit(solution)/shard_map/ppermute | solution.py:255
  17.2 7.3 %collective-permute-done.1.refs_0_.refs_2_ = bf16[784,256]{1,0:T(8,128)(2,1)S(1)} collective-permute-done((bf16[784,256]{1,0:T(8,128)(2,1)S(1)}, bf16[784,256]{1,0:T(8,128)(2,1)S(1)}, u32[]{:S(2)}, u32[]{:S(2)}) %collective-permute-start.1) | collective-permute-done | bytes 401440 | tf_op jit(solution)/shard_map/ppermute | solution.py:255
  25.2 2.6 %collective-permute-done.9.refs_1_.refs_9_ = bf16[384,256]{1,0:T(8,128)(2,1)S(1)} collective-permute-done((bf16[384,256]{1,0:T(8,128)(2,1)S(1)}, bf16[384,256]{1,0:T(8,128)(2,1)S(1)}, u32[]{:S(2)}, u32[]{:S(2)}) %collective-permute-start.9) | collective-permute-done | bytes 196640 | tf_op jit(solution)/shard_map/ppermute | solution.py:255
  28.1 2.3 %attend_early.1 = (bf16[128,384]{1,0:T(8,128)(2,1)S(1)}, bf16[128,384]{1,0:T(8,128)(2,1)S(1)}) custom-call(bf16[784,256]{1,0:T(8,128)(2,1)S(1)} %get-tuple-element.22.refs_0_, bf16[784,256]{1,0:T(8,128)(2,1)S(1)} %collective-permute-done.refs_1_, bf16[784,256]{1,0:T(8,128)(2,1)S(1)} %collective-permute-done.1.refs_0_.refs_2_, ...), custom_call_target="tpu_custom_call" | custom-call | tf_op jit(solution)/shard_map/attend_early/pallas_call | solution.py:330
  30.4 2.9 %collective-permute-start.10 = (bf16[128,384]{1,0:T(8,128)(2,1)S(1)}, bf16[128,384]{1,0:T(8,128)(2,1)S(1)}, u32[]{:S(2)}, u32[]{:S(2)}) collective-permute-start(bf16[128,384]{1,0:T(8,128)(2,1)S(1)} %get-tuple-element.37), channel_id=1, source_target_pairs={{0,28},{4,24},{8,20},{12,16},{16,12},{20,8},{24,4},{28,0},{1,29},{... | collective-permute-start | bytes 294920 | tf_op jit(solution)/shard_map/ppermute | solution.py:255
  33.3 2.3 %attend_late.1 = (bf16[128,384]{1,0:T(8,128)(2,1)S(1)}, bf16[128,384]{1,0:T(8,128)(2,1)S(1)}) custom-call(bf16[784,256]{1,0:T(8,128)(2,1)S(1)} %get-tuple-element.22.refs_0_, bf16[784,256]{1,0:T(8,128)(2,1)S(1)} %collective-permute-done.refs_1_, bf16[784,256]{1,0:T(8,128)(2,1)S(1)} %collective-permute-done.1.refs_0_.refs_2_, ...), custom_call_target="tpu_custom_call" | custom-call | tf_op jit(solution)/shard_map/attend_late/pallas_call | solution.py:330
  35.6 1.0 %collective-permute-start.8 = (bf16[128,384]{1,0:T(8,128)(2,1)S(1)}, bf16[128,384]{1,0:T(8,128)(2,1)S(1)}, u32[]{:S(2)}, u32[]{:S(2)}) collective-permute-start(bf16[128,384]{1,0:T(8,128)(2,1)S(1)} %get-tuple-element.35), channel_id=1, source_target_pairs={{0,12},{4,16},{8,28},{12,0},{16,4},{20,24},{24,20},{28,8},{1,13},{... | collective-permute-start | bytes 294920 | tf_op jit(solution)/shard_map/ppermute | solution.py:255
  36.6 1.4 %collective-permute-start.7 = (bf16[128,384]{1,0:T(8,128)(2,1)S(1)}, bf16[128,384]{1,0:T(8,128)(2,1)S(1)}, u32[]{:S(2)}, u32[]{:S(2)}) collective-permute-start(bf16[128,384]{1,0:T(8,128)(2,1)S(1)} %get-tuple-element.33), channel_id=1, source_target_pairs={{0,20},{4,8},{8,4},{12,24},{16,28},{20,0},{24,12},{28,16},{1,21},{... | collective-permute-start | bytes 294920 | tf_op jit(solution)/shard_map/ppermute | solution.py:255
  38.0 0.6 %part0.1.refs_0_ = f32[128,3072]{1,0:T(8,128)S(1)} custom-call(bf16[128,384]{1,0:T(8,128)(2,1)S(1)} %get-tuple-element.38.ta_ref, bf16[1536,3072]{1,0:T(8,128)(2,1)S(1)} %get-tuple-element.34.w_ref), custom_call_target="tpu_custom_call" | custom-call | tf_op jit(solution)/shard_map/part0/pallas_call | solution.py:348
  38.6 0.6 %part1.1.refs_0_ = f32[128,3072]{1,0:T(8,128)S(1)} custom-call(bf16[128,384]{1,0:T(8,128)(2,1)S(1)} %collective-permute-done.10.ta_ref, bf16[1536,3072]{1,0:T(8,128)(2,1)S(1)} %get-tuple-element.34.w_ref, f32[128,3072]{1,0:T(8,128)S(1)} %part0.1.refs_0_), custom_call_target="tpu_custom_call" | custom-call | tf_op jit(solution)/shard_map/part1/pallas_call | solution.py:348
  39.7 0.6 %part2.1.begun_ref = f32[128,3072]{1,0:T(8,128)S(1)} custom-call(bf16[128,384]{1,0:T(8,128)(2,1)S(1)} %collective-permute-done.8.ta_ref, bf16[1536,3072]{1,0:T(8,128)(2,1)S(1)} %get-tuple-element.34.w_ref, f32[128,3072]{1,0:T(8,128)S(1)} %part1.1.refs_0_), custom_call_target="tpu_custom_call" | custom-call | tf_op jit(solution)/shard_map/part2/pallas_call | solution.py:348
  40.4 1.1 %collective-permute-done.7.ta_ref = bf16[128,384]{1,0:T(8,128)(2,1)S(1)} collective-permute-done((bf16[128,384]{1,0:T(8,128)(2,1)S(1)}, bf16[128,384]{1,0:T(8,128)(2,1)S(1)}, u32[]{:S(2)}, u32[]{:S(2)}) %collective-permute-start.7) | collective-permute-done | bytes 98336 | tf_op jit(solution)/shard_map/ppermute | solution.py:255
  41.4 0.6 %project.1 = (f32[128,3072]{1,0:T(8,128)S(1)}, f32[1,3072]{1,0:T(1,128)S(1)}) custom-call(bf16[128,384]{1,0:T(8,128)(2,1)S(1)} %collective-permute-done.7.ta_ref, bf16[1536,3072]{1,0:T(8,128)(2,1)S(1)} %get-tuple-element.34.w_ref, f32[128,3072]{1,0:T(8,128)S(1)} %part2.1.begun_ref, bf16[1,128,3072]{2,1,0:T(8,128)(2,1)S(1)} %get-tuple-element.39.cot_ref), custom_call_target="tpu_custom_call" | custom-call | tf_op jit(solution)/shard_map/project/pallas_call | solution.py:356
  42.1 0.5 collective-permute-start.11
  42.6 0.8 %collective-permute-done.11.refs_0_ = f32[1,3072]{1,0:T(1,128)S(1)} collective-permute-done((f32[1,3072]{1,0:T(1,128)S(1)}, f32[1,3072]{1,0:T(1,128)S(1)}, u32[]{:S(2)}, u32[]{:S(2)}) %collective-permute-start.11) | collective-permute-done | bytes 12320 | tf_op jit(solution)/shard_map/ppermute | solution.py:222
  43.5 1.7 %collective-permute-start.12 = (f32[1,3072]{1,0:T(1,128)S(1)}, f32[1,3072]{1,0:T(1,128)S(1)}, u32[]{:S(2)}, u32[]{:S(2)}) collective-permute-start(f32[1,3072]{1,0:T(1,128)S(1)} %sum.4.refs_3_), channel_id=1, source_target_pairs={{0,28},{1,29},{2,30},{3,31},{4,24},{5,25},{6,26},{7,27},{8,20},{9,... | collective-permute-start | bytes 36872 | tf_op jit(solution)/shard_map/ppermute | solution.py:222
  45.4 1.3 %collective-permute-start.14 = (f32[1,3072]{1,0:T(1,128)S(1)}, f32[1,3072]{1,0:T(1,128)S(1)}, u32[]{:S(2)}, u32[]{:S(2)}) collective-permute-start(f32[1,3072]{1,0:T(1,128)S(1)} %sum.4.refs_3_), channel_id=1, source_target_pairs={{0,12},{1,13},{2,14},{3,15},{4,8},{5,9},{6,10},{7,11},{8,4},{9,5},... | collective-permute-start | bytes 36872 | tf_op jit(solution)/shard_map/ppermute | solution.py:222
  46.6 0.9 %collective-permute-done.12.refs_0_ = f32[1,3072]{1,0:T(1,128)S(1)} collective-permute-done((f32[1,3072]{1,0:T(1,128)S(1)}, f32[1,3072]{1,0:T(1,128)S(1)}, u32[]{:S(2)}, u32[]{:S(2)}) %collective-permute-start.12) | collective-permute-done | bytes 12320 | tf_op jit(solution)/shard_map/ppermute | solution.py:222
  47.5 0.8 %collective-permute-done.13.refs_1_ = f32[1,3072]{1,0:T(1,128)S(1)} collective-permute-done((f32[1,3072]{1,0:T(1,128)S(1)}, f32[1,3072]{1,0:T(1,128)S(1)}, u32[]{:S(2)}, u32[]{:S(2)}) %collective-permute-start.13) | collective-permute-done | bytes 12320 | tf_op jit(solution)/shard_map/ppermute | solution.py:222
  48.5 1.4 %collective-permute-start.15 = (f32[1,3072]{1,0:T(1,128)S(1)}, f32[1,3072]{1,0:T(1,128)S(1)}, u32[]{:S(2)}, u32[]{:S(2)}) collective-permute-start(f32[1,3072]{1,0:T(1,128)S(1)} %sum.5.refs_1_), channel_id=1, source_target_pairs={{0,5},{1,4},{2,7},{3,6},{4,1},{5,0},{6,3},{7,2},{8,13},{9,12},{10,... | collective-permute-start | bytes 36872 | tf_op jit(solution)/shard_map/ppermute | solution.py:222
  49.8 1.8 %collective-permute-done.15.refs_0_ = f32[1,3072]{1,0:T(1,128)S(1)} collective-permute-done((f32[1,3072]{1,0:T(1,128)S(1)}, f32[1,3072]{1,0:T(1,128)S(1)}, u32[]{:S(2)}, u32[]{:S(2)}) %collective-permute-start.15) | collective-permute-done | bytes 12320 | tf_op jit(solution)/shard_map/ppermute | solution.py:222
  51.6 2.4 %collective-permute-start.16 = (f32[1,3072]{1,0:T(1,128)S(1)}, f32[1,3072]{1,0:T(1,128)S(1)}, u32[]{:S(2)}, u32[]{:S(2)}) collective-permute-start(f32[1,3072]{1,0:T(1,128)S(1)} %sum.6.refs_1_), channel_id=1, source_target_pairs={{0,6},{1,7},{2,4},{3,5},{4,2},{5,3},{6,0},{7,1},{8,14},{9,15},{10,... | collective-permute-start | bytes 36872 | tf_op jit(solution)/shard_map/ppermute | solution.py:222
  54.0 1.0 %branch.1 = bf16[1,128,3072]{2,1,0:T(8,128)(2,1)} custom-call(f32[128,3072]{1,0:T(8,128)S(1)} %get-tuple-element.40.projected_ref, f32[1,3072]{1,0:T(1,128)S(1)} %bitcast.2), custom_call_target="tpu_custom_call" | custom-call | tf_op jit(solution)/shard_map/branch/pallas_call | solution.py:364
  55.0 0.7 %collective-permute-done.16.refs_0_ = f32[1,3072]{1,0:T(1,128)S(1)} collective-permute-done((f32[1,3072]{1,0:T(1,128)S(1)}, f32[1,3072]{1,0:T(1,128)S(1)}, u32[]{:S(2)}, u32[]{:S(2)}) %collective-permute-start.16) | collective-permute-done | bytes 12320 | tf_op jit(solution)/shard_map/ppermute | solution.py:222
  55.6 0.6 %sum.7 = f32[1,3072]{1,0:T(1,128)} custom-call(f32[1,3072]{1,0:T(1,128)S(1)} %collective-permute-done.16.refs_0_, f32[1,3072]{1,0:T(1,128)S(1)} %sum.6.refs_1_), custom_call_target="tpu_custom_call" | custom-call | tf_op jit(solution)/shard_map/sum/pallas_call | solution.py:223
  (22 shorter events, 2.0 us)
Async XLA Ops:
  1.8 14.6 %collective-permute-start = (bf16[784,256]{1,0:T(8,128)(2,1)S(1)}, bf16[784,256]{1,0:T(8,128)(2,1)S(1)}, u32[]{:S(2)}, u32[]{:S(2)}) collective-permute-start(bf16[784,256]{1,0:T(8,128)(2,1)S(1)} %pack_far.1), channel_id=1, source_target_pairs={{0,28},{4,24},{8,20},{12,16},{16,12},{20,8},{24,4},{28,0},{1,29},{... | collective-permute-start | bytes 1204232 | tf_op jit(solution)/shard_map/ppermute | solution.py:255
  7.2 17.4 %collective-permute-start.1 = (bf16[784,256]{1,0:T(8,128)(2,1)S(1)}, bf16[784,256]{1,0:T(8,128)(2,1)S(1)}, u32[]{:S(2)}, u32[]{:S(2)}) collective-permute-start(bf16[784,256]{1,0:T(8,128)(2,1)S(1)} %get-tuple-element.23), channel_id=1, source_target_pairs={{0,12},{4,16},{8,28},{12,0},{16,4},{20,24},{24,20},{28,8},{1,13},{... | collective-permute-start | bytes 1204232 | tf_op jit(solution)/shard_map/ppermute | solution.py:255
  8.1 16.5 %collective-permute-start.2 = (bf16[784,256]{1,0:T(8,128)(2,1)S(1)}, bf16[784,256]{1,0:T(8,128)(2,1)S(1)}, u32[]{:S(2)}, u32[]{:S(2)}) collective-permute-start(bf16[784,256]{1,0:T(8,128)(2,1)S(1)} %get-tuple-element.24), channel_id=1, source_target_pairs={{0,20},{4,8},{8,4},{12,24},{16,28},{20,0},{24,12},{28,16},{1,21},{... | collective-permute-start | bytes 1204232 | tf_op jit(solution)/shard_map/ppermute | solution.py:255
  9.9 17.9 %collective-permute-start.9 = (bf16[384,256]{1,0:T(8,128)(2,1)S(1)}, bf16[384,256]{1,0:T(8,128)(2,1)S(1)}, u32[]{:S(2)}, u32[]{:S(2)}) collective-permute-start(bf16[384,256]{1,0:T(8,128)(2,1)S(1)} %get-tuple-element.36), channel_id=1, source_target_pairs={{0,28},{4,24},{8,20},{12,16},{16,12},{20,8},{24,4},{28,0},{1,29},{... | collective-permute-start | bytes 589832 | tf_op jit(solution)/shard_map/ppermute | solution.py:255
  12.6 20.7 %collective-permute-start.5 = (bf16[384,256]{1,0:T(8,128)(2,1)S(1)}, bf16[384,256]{1,0:T(8,128)(2,1)S(1)}, u32[]{:S(2)}, u32[]{:S(2)}) collective-permute-start(bf16[384,256]{1,0:T(8,128)(2,1)S(1)} %get-tuple-element.31), channel_id=1, source_target_pairs={{0,12},{4,16},{8,28},{12,0},{16,4},{20,24},{24,20},{28,8},{1,13},{... | collective-permute-start | bytes 589832 | tf_op jit(solution)/shard_map/ppermute | solution.py:255
  16.4 16.9 %collective-permute-start.6 = (bf16[384,256]{1,0:T(8,128)(2,1)S(1)}, bf16[384,256]{1,0:T(8,128)(2,1)S(1)}, u32[]{:S(2)}, u32[]{:S(2)}) collective-permute-start(bf16[384,256]{1,0:T(8,128)(2,1)S(1)} %get-tuple-element.32), channel_id=1, source_target_pairs={{0,20},{4,8},{8,4},{12,24},{16,28},{20,0},{24,12},{28,16},{1,21},{... | collective-permute-start | bytes 589832 | tf_op jit(solution)/shard_map/ppermute | solution.py:255
  24.5 3.3 %collective-permute-start.3 = (bf16[1664,256]{1,0:T(8,128)(2,1)S(1)}, bf16[1664,256]{1,0:T(8,128)(2,1)S(1)}, u32[]{:S(2)}, u32[]{:S(2)}) collective-permute-start(bf16[1664,256]{1,0:T(8,128)(2,1)S(1)} %get-tuple-element.29), channel_id=1, source_target_pairs={{0,4},{4,0},{8,12},{12,8},{16,20},{20,16},{24,28},{28,24},{1,5},{5... | collective-permute-start | bytes 2555912 | tf_op jit(solution)/shard_map/ppermute | solution.py:246
  24.7 3.4 %collective-permute-start.4 = (bf16[1664,256]{1,0:T(8,128)(2,1)S(1)}, bf16[1664,256]{1,0:T(8,128)(2,1)S(1)}, u32[]{:S(2)}, u32[]{:S(2)}) collective-permute-start(bf16[1664,256]{1,0:T(8,128)(2,1)S(1)} %get-tuple-element.30), channel_id=1, source_target_pairs={{0,4},{4,0},{8,12},{12,8},{16,20},{20,16},{24,28},{28,24},{1,5},{5... | collective-permute-start | bytes 2555912 | tf_op jit(solution)/shard_map/ppermute | solution.py:246
  30.4 8.1 %collective-permute-start.10 = (bf16[128,384]{1,0:T(8,128)(2,1)S(1)}, bf16[128,384]{1,0:T(8,128)(2,1)S(1)}, u32[]{:S(2)}, u32[]{:S(2)}) collective-permute-start(bf16[128,384]{1,0:T(8,128)(2,1)S(1)} %get-tuple-element.37), channel_id=1, source_target_pairs={{0,28},{4,24},{8,20},{12,16},{16,12},{20,8},{24,4},{28,0},{1,29},{... | collective-permute-start | bytes 294920 | tf_op jit(solution)/shard_map/ppermute | solution.py:255
  35.6 4.1 %collective-permute-start.8 = (bf16[128,384]{1,0:T(8,128)(2,1)S(1)}, bf16[128,384]{1,0:T(8,128)(2,1)S(1)}, u32[]{:S(2)}, u32[]{:S(2)}) collective-permute-start(bf16[128,384]{1,0:T(8,128)(2,1)S(1)} %get-tuple-element.35), channel_id=1, source_target_pairs={{0,12},{4,16},{8,28},{12,0},{16,4},{20,24},{24,20},{28,8},{1,13},{... | collective-permute-start | bytes 294920 | tf_op jit(solution)/shard_map/ppermute | solution.py:255
  36.6 4.8 %collective-permute-start.7 = (bf16[128,384]{1,0:T(8,128)(2,1)S(1)}, bf16[128,384]{1,0:T(8,128)(2,1)S(1)}, u32[]{:S(2)}, u32[]{:S(2)}) collective-permute-start(bf16[128,384]{1,0:T(8,128)(2,1)S(1)} %get-tuple-element.33), channel_id=1, source_target_pairs={{0,20},{4,8},{8,4},{12,24},{16,28},{20,0},{24,12},{28,16},{1,21},{... | collective-permute-start | bytes 294920 | tf_op jit(solution)/shard_map/ppermute | solution.py:255
  41.4 12.6 %copy-start = (f32[3072]{0:T(1024)S(1)}, f32[3072]{0:T(1024)}, u32[]{:S(2)}) copy-start(f32[3072]{0:T(1024)} %param.20) | copy-start | bytes 36868
  42.1 1.4 %collective-permute-start.11 = (f32[1,3072]{1,0:T(1,128)S(1)}, f32[1,3072]{1,0:T(1,128)S(1)}, u32[]{:S(2)}, u32[]{:S(2)}) collective-permute-start(f32[1,3072]{1,0:T(1,128)S(1)} %get-tuple-element.41.refs_1_), channel_id=1, source_target_pairs={{0,4},{1,5},{2,6},{3,7},{4,0},{5,1},{6,2},{7,3},{8,12},{9,13},{10,... | collective-permute-start | bytes 36872 | tf_op jit(solution)/shard_map/ppermute | solution.py:222
  43.5 4.0 %collective-permute-start.12 = (f32[1,3072]{1,0:T(1,128)S(1)}, f32[1,3072]{1,0:T(1,128)S(1)}, u32[]{:S(2)}, u32[]{:S(2)}) collective-permute-start(f32[1,3072]{1,0:T(1,128)S(1)} %sum.4.refs_3_), channel_id=1, source_target_pairs={{0,28},{1,29},{2,30},{3,31},{4,24},{5,25},{6,26},{7,27},{8,20},{9,... | collective-permute-start | bytes 36872 | tf_op jit(solution)/shard_map/ppermute | solution.py:222
  45.2 3.1 %collective-permute-start.13 = (f32[1,3072]{1,0:T(1,128)S(1)}, f32[1,3072]{1,0:T(1,128)S(1)}, u32[]{:S(2)}, u32[]{:S(2)}) collective-permute-start(f32[1,3072]{1,0:T(1,128)S(1)} %sum.4.refs_3_), channel_id=1, source_target_pairs={{0,20},{1,21},{2,22},{3,23},{4,16},{5,17},{6,18},{7,19},{8,28},{9,... | collective-permute-start | bytes 36872 | tf_op jit(solution)/shard_map/ppermute | solution.py:222
  45.4 3.1 %collective-permute-start.14 = (f32[1,3072]{1,0:T(1,128)S(1)}, f32[1,3072]{1,0:T(1,128)S(1)}, u32[]{:S(2)}, u32[]{:S(2)}) collective-permute-start(f32[1,3072]{1,0:T(1,128)S(1)} %sum.4.refs_3_), channel_id=1, source_target_pairs={{0,12},{1,13},{2,14},{3,15},{4,8},{5,9},{6,10},{7,11},{8,4},{9,5},... | collective-permute-start | bytes 36872 | tf_op jit(solution)/shard_map/ppermute | solution.py:222
  48.5 3.1 %collective-permute-start.15 = (f32[1,3072]{1,0:T(1,128)S(1)}, f32[1,3072]{1,0:T(1,128)S(1)}, u32[]{:S(2)}, u32[]{:S(2)}) collective-permute-start(f32[1,3072]{1,0:T(1,128)S(1)} %sum.5.refs_1_), channel_id=1, source_target_pairs={{0,5},{1,4},{2,7},{3,6},{4,1},{5,0},{6,3},{7,2},{8,13},{9,12},{10,... | collective-permute-start | bytes 36872 | tf_op jit(solution)/shard_map/ppermute | solution.py:222
  51.6 4.0 %collective-permute-start.16 = (f32[1,3072]{1,0:T(1,128)S(1)}, f32[1,3072]{1,0:T(1,128)S(1)}, u32[]{:S(2)}, u32[]{:S(2)}) collective-permute-start(f32[1,3072]{1,0:T(1,128)S(1)} %sum.6.refs_1_), channel_id=1, source_target_pairs={{0,6},{1,7},{2,4},{3,5},{4,2},{5,3},{6,0},{7,1},{8,14},{9,15},{10,... | collective-permute-start | bytes 36872 | tf_op jit(solution)/shard_map/ppermute | solution.py:222

commit v4 on v3

--- a/solution.py
+++ b/solution.py
@@ -27,23 +27,30 @@
     return pick(index // low, half // low, low) * pick(index % low, low, 1)
 
 
-def rotation(order_ref, rows, head_dim):
-    half = head_dim // 2
+def tables(blocks, rows, head_dim):
     lane = lax.broadcasted_iota(jnp.int32, (8, head_dim), 1)
     line = lax.broadcasted_iota(jnp.int32, (8, head_dim), 0)
-    frequency = frequencies(lane, half)
-    base = order_ref[lax.axis_index("ctx")] * rows
+    frequency = frequencies(lane, head_dim // 2)
     steps = rows // 8
-    angles = jnp.concatenate(
-        [line.astype(jnp.float32) * frequency]
-        + [(base + 8 * (line + 8 * k)).astype(jnp.float32) * frequency for k in range(steps // 8)],
-        axis=0,
-    )
-    cosines, sines = jnp.cos(angles), jnp.sin(angles)
+    positions = [line] + [8 * (line + 8 * k) for k in range(steps // 8)] + [rows * (line + 8 * k) for k in range(blocks // 8)]
+    angles = jnp.concatenate([position.astype(jnp.float32) * frequency for position in positions], axis=0)
+    return jnp.cos(angles), jnp.sin(angles)
+
+
+def rotation(block, rows, head_dim, cosines, sines):
+    half = head_dim // 2
+    steps = rows // 8
+    lane = lax.broadcasted_iota(jnp.int32, (8, head_dim), 1)
+    firsts = cosines.shape[0] - 8 - steps
+    here = lax.broadcasted_iota(jnp.int32, (firsts, head_dim), 0) == block
+    cos_first = jnp.sum(jnp.where(here, cosines[8 + steps :], 0.0), axis=0, keepdims=True)
+    sin_first = jnp.sum(jnp.where(here, sines[8 + steps :], 0.0), axis=0, keepdims=True)
     cos_v, sin_v = cosines[:8], sines[:8]
+    cos_8u = cos_first * cosines[8 : 8 + steps] - sin_first * sines[8 : 8 + steps]
+    sin_8u = sin_first * cosines[8 : 8 + steps] + cos_first * sines[8 : 8 + steps]
     cos_rows, sin_rows = [], []
     for u in range(steps):
-        cos_u, sin_u = cosines[8 + u : 9 + u], sines[8 + u : 9 + u]
+        cos_u, sin_u = cos_8u[u : u + 1], sin_8u[u : u + 1]
         cos_rows.append(cos_u * cos_v - sin_u * sin_v)
         sin_rows.append(jnp.where(lane < half, -1.0, 1.0) * (sin_u * cos_v + cos_u * sin_v))
     return jnp.concatenate(cos_rows, axis=0), jnp.concatenate(sin_rows, axis=0)
@@ -78,8 +85,9 @@
             column = pl.multiple_of(group_of(pair, members) * part, part)
             loads[t, p] = pltpu.make_async_copy(source.at[0, :, pl.ds(column, part)], scratch.at[t, p], in_sems.at[t, p])
             loads[t, p].start()
+    cosines, sines = tables(order_ref.shape[0], rows, head_dim)
     small[0].wait()
-    cosine, sine = rotation(order_ref, rows, head_dim)
+    cosine, sine = rotation(order_ref[lax.axis_index("ctx")], rows, head_dim, cosines, sines)
 
     def turned(x):
         x = x.astype(jnp.float32)

time: 56.5 us -> 56.5 us (level)
  no operation moved by 1% of the time
where the time goes in v4:
time: 56.5 us; the launch traced here: 56.2 us
  starting transfers between devices  20.9 us (37%)
  Pallas kernels  17.7 us (31%)
  waiting for transfers between devices  16.9 us (30%)
  between operations  0.75 us (1%)
    ppermute x9, starting transfers between devices, send(): lax.ppermute(x, 'ctx', [(j, j ^ offset[j] * members + cross) for j in ran...  12.9 us
    ppermute x9, waiting for transfers between devices, send(): lax.ppermute(x, 'ctx', [(j, j ^ offset[j] * members + cross) for j in ran...  11.4 us
    ppermute x6, starting transfers between devices, exchange_sum(): lax.ppermute(x, ('ctx', 'dp'), [(j * n_dp + z, (j ^ own) * n_dp + (z ^ ot...  7.43 us
    ppermute x6, waiting for transfers between devices, exchange_sum(): lax.ppermute(x, ('ctx', 'dp'), [(j * n_dp + z, (j ^ own) * n_dp + (z ^ ot...  5.13 us
    pallas_call x3, Pallas kernels, pack(): pl.pallas_call(functools.partial(pack_kernel, [route[place] for place in...  4.95 us
    pallas_call x2, Pallas kernels, attend(): pl.pallas_call(functools.partial(attend_kernel, groups, members, places,...  4.63 us
    pallas_call x1, Pallas kernels, local(): pl.pallas_call(stage_kernel, out_shape=[pltpu.VMEM(out_weight.shape, bf16...  3.84 us
    pallas_call x3, Pallas kernels, local(): pl.pallas_call(functools.partial(part_kernel, members, route[place], 512)...  1.85 us
  transfers between devices with their start and end apart: 17, of which 11 were waited for; matrix products, arithmetic and copies ran while one was open for 0% of the time, Pallas kernels for 27%

profile of v4, /device:TPU:0, one launch (start us, length us, event | category | flops | bytes accessed | tf_op | source)
XLA Modules:
  0.0 56.2 jit_solution(11819937424070899502)
XLA Ops:
  0.6 1.2 %pack_far.1 = bf16[784,256]{1,0:T(8,128)(2,1)S(1)} custom-call(s32[8]{0:T(128)} %order_hbm.5, s32[1,128]{1,0:T(1,128)} %ids_hbm.5, bf16[1,128,1536]{2,1,0:T(8,128)(2,1)} %refs_0_.4, bf16[1,128,1536]{2,1,0:T(8,128)(2,1)} %refs_1_.4, bf16[1,128,1536]{2,1,0:T(8,128)(2,1)} %refs_2_.3, bf16[1,128,1536]{2,1,0:T(8,128)(2,1)} %refs_3_.3), custom_call_target="tpu_custom_call" | custom-call | tf_op jit(solution)/shard_map/pack_far/pallas_call | solution.py:272
  1.8 3.4 %collective-permute-start = (bf16[784,256]{1,0:T(8,128)(2,1)S(1)}, bf16[784,256]{1,0:T(8,128)(2,1)S(1)}, u32[]{:S(2)}, u32[]{:S(2)}) collective-permute-start(bf16[784,256]{1,0:T(8,128)(2,1)S(1)} %pack_far.1), channel_id=1, source_target_pairs={{0,28},{4,24},{8,20},{12,16},{16,12},{20,8},{24,4},{28,0},{1,29},{... | collective-permute-start | bytes 1204232 | tf_op jit(solution)/shard_map/ppermute | solution.py:263
  5.2 1.9 %pack_near.1 = (bf16[784,256]{1,0:T(8,128)(2,1)S(1)}, bf16[784,256]{1,0:T(8,128)(2,1)S(1)}, bf16[784,256]{1,0:T(8,128)(2,1)S(1)}) custom-call(s32[8]{0:T(128)} %order_hbm.5, s32[1,128]{1,0:T(1,128)} %ids_hbm.5, bf16[1,128,1536]{2,1,0:T(8,128)(2,1)} %refs_0_.4, bf16[1,128,1536]{2,1,0:T(8,128)(2,1)} %refs_1_.4, bf16[1,128,1536]{2,1,0:T(8,128)(2,1)} %refs_2_.3, ...), custom_call_target="tpu_custom_call" | custom-call | tf_op jit(solution)/shard_map/pack_near/pallas_call | solution.py:272
  7.2 0.9 %collective-permute-start.1 = (bf16[784,256]{1,0:T(8,128)(2,1)S(1)}, bf16[784,256]{1,0:T(8,128)(2,1)S(1)}, u32[]{:S(2)}, u32[]{:S(2)}) collective-permute-start(bf16[784,256]{1,0:T(8,128)(2,1)S(1)} %get-tuple-element.23), channel_id=1, source_target_pairs={{0,12},{4,16},{8,28},{12,0},{16,4},{20,24},{24,20},{28,8},{1,13},{... | collective-permute-start | bytes 1204232 | tf_op jit(solution)/shard_map/ppermute | solution.py:263
  8.1 1.8 %pack_queries.1 = (bf16[384,256]{1,0:T(8,128)(2,1)S(1)}, bf16[384,256]{1,0:T(8,128)(2,1)S(1)}, bf16[384,256]{1,0:T(8,128)(2,1)S(1)}, bf16[384,256]{1,0:T(8,128)(2,1)S(1)}) custom-call(s32[8]{0:T(128)} %order_hbm.5, s32[1,128]{1,0:T(1,128)} %ids_hbm.5, bf16[1,128,1536]{2,1,0:T(8,128)(2,1)} %refs_0_.5, bf16[1,128,1536]{2,1,0:T(8,128)(2,1)} %refs_1_.5), custom_call_target="tpu_custom_call" | custom-call | tf_op jit(solution)/shard_map/pack_queries/pallas_call | solution.py:272
  9.9 2.7 %collective-permute-start.9 = (bf16[384,256]{1,0:T(8,128)(2,1)S(1)}, bf16[384,256]{1,0:T(8,128)(2,1)S(1)}, u32[]{:S(2)}, u32[]{:S(2)}) collective-permute-start(bf16[384,256]{1,0:T(8,128)(2,1)S(1)} %get-tuple-element.36), channel_id=1, source_target_pairs={{0,28},{4,24},{8,20},{12,16},{16,12},{20,8},{24,4},{28,0},{1,29},{... | collective-permute-start | bytes 589832 | tf_op jit(solution)/shard_map/ppermute | solution.py:263
  12.6 3.8 %stage.1 = (bf16[1536,3072]{1,0:T(8,128)(2,1)S(1)}, bf16[1,128,3072]{2,1,0:T(8,128)(2,1)S(1)}, f32[8,128]{1,0:T(8,128)S(1)}) custom-call(bf16[1536,3072]{1,0:T(8,128)(2,1)} %w_hbm.1, bf16[1,128,3072]{2,1,0:T(8,128)(2,1)} %cot_hbm.1, bf16[384,256]{1,0:T(8,128)(2,1)S(1)} %get-tuple-element.25.refs_2_.after_ref.refs_0_.refs_8_), custom_call_target="tpu_custom_call" | custom-call | tf_op jit(solution)/shard_map/stage/pallas_call | solution.py:294
  16.5 0.6 %collective-permute-start.6 = (bf16[384,256]{1,0:T(8,128)(2,1)S(1)}, bf16[384,256]{1,0:T(8,128)(2,1)S(1)}, u32[]{:S(2)}, u32[]{:S(2)}) collective-permute-start(bf16[384,256]{1,0:T(8,128)(2,1)S(1)} %get-tuple-element.32), channel_id=1, source_target_pairs={{0,20},{4,8},{8,4},{12,24},{16,28},{20,0},{24,12},{28,16},{1,21},{... | collective-permute-start | bytes 589832 | tf_op jit(solution)/shard_map/ppermute | solution.py:263
  17.2 7.3 %collective-permute-done.1.refs_0_.refs_2_ = bf16[784,256]{1,0:T(8,128)(2,1)S(1)} collective-permute-done((bf16[784,256]{1,0:T(8,128)(2,1)S(1)}, bf16[784,256]{1,0:T(8,128)(2,1)S(1)}, u32[]{:S(2)}, u32[]{:S(2)}) %collective-permute-start.1) | collective-permute-done | bytes 401440 | tf_op jit(solution)/shard_map/ppermute | solution.py:263
  25.2 2.6 %collective-permute-done.9.refs_1_.refs_9_ = bf16[384,256]{1,0:T(8,128)(2,1)S(1)} collective-permute-done((bf16[384,256]{1,0:T(8,128)(2,1)S(1)}, bf16[384,256]{1,0:T(8,128)(2,1)S(1)}, u32[]{:S(2)}, u32[]{:S(2)}) %collective-permute-start.9) | collective-permute-done | bytes 196640 | tf_op jit(solution)/shard_map/ppermute | solution.py:263
  28.1 2.3 %attend_early.1 = (bf16[128,384]{1,0:T(8,128)(2,1)S(1)}, bf16[128,384]{1,0:T(8,128)(2,1)S(1)}) custom-call(bf16[784,256]{1,0:T(8,128)(2,1)S(1)} %get-tuple-element.22.refs_0_, bf16[784,256]{1,0:T(8,128)(2,1)S(1)} %collective-permute-done.refs_1_, bf16[784,256]{1,0:T(8,128)(2,1)S(1)} %collective-permute-done.1.refs_0_.refs_2_, ...), custom_call_target="tpu_custom_call" | custom-call | tf_op jit(solution)/shard_map/attend_early/pallas_call | solution.py:338
  30.4 2.9 %collective-permute-start.10 = (bf16[128,384]{1,0:T(8,128)(2,1)S(1)}, bf16[128,384]{1,0:T(8,128)(2,1)S(1)}, u32[]{:S(2)}, u32[]{:S(2)}) collective-permute-start(bf16[128,384]{1,0:T(8,128)(2,1)S(1)} %get-tuple-element.37), channel_id=1, source_target_pairs={{0,28},{4,24},{8,20},{12,16},{16,12},{20,8},{24,4},{28,0},{1,29},{... | collective-permute-start | bytes 294920 | tf_op jit(solution)/shard_map/ppermute | solution.py:263
  33.3 2.3 %attend_late.1 = (bf16[128,384]{1,0:T(8,128)(2,1)S(1)}, bf16[128,384]{1,0:T(8,128)(2,1)S(1)}) custom-call(bf16[784,256]{1,0:T(8,128)(2,1)S(1)} %get-tuple-element.22.refs_0_, bf16[784,256]{1,0:T(8,128)(2,1)S(1)} %collective-permute-done.refs_1_, bf16[784,256]{1,0:T(8,128)(2,1)S(1)} %collective-permute-done.1.refs_0_.refs_2_, ...), custom_call_target="tpu_custom_call" | custom-call | tf_op jit(solution)/shard_map/attend_late/pallas_call | solution.py:338
  35.6 1.0 %collective-permute-start.8 = (bf16[128,384]{1,0:T(8,128)(2,1)S(1)}, bf16[128,384]{1,0:T(8,128)(2,1)S(1)}, u32[]{:S(2)}, u32[]{:S(2)}) collective-permute-start(bf16[128,384]{1,0:T(8,128)(2,1)S(1)} %get-tuple-element.35), channel_id=1, source_target_pairs={{0,12},{4,16},{8,28},{12,0},{16,4},{20,24},{24,20},{28,8},{1,13},{... | collective-permute-start | bytes 294920 | tf_op jit(solution)/shard_map/ppermute | solution.py:263
  36.6 1.4 %collective-permute-start.7 = (bf16[128,384]{1,0:T(8,128)(2,1)S(1)}, bf16[128,384]{1,0:T(8,128)(2,1)S(1)}, u32[]{:S(2)}, u32[]{:S(2)}) collective-permute-start(bf16[128,384]{1,0:T(8,128)(2,1)S(1)} %get-tuple-element.33), channel_id=1, source_target_pairs={{0,20},{4,8},{8,4},{12,24},{16,28},{20,0},{24,12},{28,16},{1,21},{... | collective-permute-start | bytes 294920 | tf_op jit(solution)/shard_map/ppermute | solution.py:263
  38.0 0.6 %part0.1.refs_0_ = f32[128,3072]{1,0:T(8,128)S(1)} custom-call(bf16[128,384]{1,0:T(8,128)(2,1)S(1)} %get-tuple-element.38.ta_ref, bf16[1536,3072]{1,0:T(8,128)(2,1)S(1)} %get-tuple-element.34.w_ref), custom_call_target="tpu_custom_call" | custom-call | tf_op jit(solution)/shard_map/part0/pallas_call | solution.py:356
  38.6 0.6 %part1.1.refs_0_ = f32[128,3072]{1,0:T(8,128)S(1)} custom-call(bf16[128,384]{1,0:T(8,128)(2,1)S(1)} %collective-permute-done.10.ta_ref, bf16[1536,3072]{1,0:T(8,128)(2,1)S(1)} %get-tuple-element.34.w_ref, f32[128,3072]{1,0:T(8,128)S(1)} %part0.1.refs_0_), custom_call_target="tpu_custom_call" | custom-call | tf_op jit(solution)/shard_map/part1/pallas_call | solution.py:356
  39.7 0.6 %part2.1.begun_ref = f32[128,3072]{1,0:T(8,128)S(1)} custom-call(bf16[128,384]{1,0:T(8,128)(2,1)S(1)} %collective-permute-done.8.ta_ref, bf16[1536,3072]{1,0:T(8,128)(2,1)S(1)} %get-tuple-element.34.w_ref, f32[128,3072]{1,0:T(8,128)S(1)} %part1.1.refs_0_), custom_call_target="tpu_custom_call" | custom-call | tf_op jit(solution)/shard_map/part2/pallas_call | solution.py:356
  40.4 1.1 %collective-permute-done.7.ta_ref = bf16[128,384]{1,0:T(8,128)(2,1)S(1)} collective-permute-done((bf16[128,384]{1,0:T(8,128)(2,1)S(1)}, bf16[128,384]{1,0:T(8,128)(2,1)S(1)}, u32[]{:S(2)}, u32[]{:S(2)}) %collective-permute-start.7) | collective-permute-done | bytes 98336 | tf_op jit(solution)/shard_map/ppermute | solution.py:263
  41.4 0.6 %project.1 = (f32[128,3072]{1,0:T(8,128)S(1)}, f32[1,3072]{1,0:T(1,128)S(1)}) custom-call(bf16[128,384]{1,0:T(8,128)(2,1)S(1)} %collective-permute-done.7.ta_ref, bf16[1536,3072]{1,0:T(8,128)(2,1)S(1)} %get-tuple-element.34.w_ref, f32[128,3072]{1,0:T(8,128)S(1)} %part2.1.begun_ref, bf16[1,128,3072]{2,1,0:T(8,128)(2,1)S(1)} %get-tuple-element.39.cot_ref), custom_call_target="tpu_custom_call" | custom-call | tf_op jit(solution)/shard_map/project/pallas_call | solution.py:364
  42.1 0.5 collective-permute-start.11
  42.6 0.8 %collective-permute-done.11.refs_0_ = f32[1,3072]{1,0:T(1,128)S(1)} collective-permute-done((f32[1,3072]{1,0:T(1,128)S(1)}, f32[1,3072]{1,0:T(1,128)S(1)}, u32[]{:S(2)}, u32[]{:S(2)}) %collective-permute-start.11) | collective-permute-done | bytes 12320 | tf_op jit(solution)/shard_map/ppermute | solution.py:230
  43.5 1.8 %collective-permute-start.12 = (f32[1,3072]{1,0:T(1,128)S(1)}, f32[1,3072]{1,0:T(1,128)S(1)}, u32[]{:S(2)}, u32[]{:S(2)}) collective-permute-start(f32[1,3072]{1,0:T(1,128)S(1)} %sum.4.refs_3_), channel_id=1, source_target_pairs={{0,28},{1,29},{2,30},{3,31},{4,24},{5,25},{6,26},{7,27},{8,20},{9,... | collective-permute-start | bytes 36872 | tf_op jit(solution)/shard_map/ppermute | solution.py:230
  45.4 1.3 %collective-permute-start.14 = (f32[1,3072]{1,0:T(1,128)S(1)}, f32[1,3072]{1,0:T(1,128)S(1)}, u32[]{:S(2)}, u32[]{:S(2)}) collective-permute-start(f32[1,3072]{1,0:T(1,128)S(1)} %sum.4.refs_3_), channel_id=1, source_target_pairs={{0,12},{1,13},{2,14},{3,15},{4,8},{5,9},{6,10},{7,11},{8,4},{9,5},... | collective-permute-start | bytes 36872 | tf_op jit(solution)/shard_map/ppermute | solution.py:230
  46.6 0.9 %collective-permute-done.12.refs_0_ = f32[1,3072]{1,0:T(1,128)S(1)} collective-permute-done((f32[1,3072]{1,0:T(1,128)S(1)}, f32[1,3072]{1,0:T(1,128)S(1)}, u32[]{:S(2)}, u32[]{:S(2)}) %collective-permute-start.12) | collective-permute-done | bytes 12320 | tf_op jit(solution)/shard_map/ppermute | solution.py:230
  47.5 0.9 %collective-permute-done.13.refs_1_ = f32[1,3072]{1,0:T(1,128)S(1)} collective-permute-done((f32[1,3072]{1,0:T(1,128)S(1)}, f32[1,3072]{1,0:T(1,128)S(1)}, u32[]{:S(2)}, u32[]{:S(2)}) %collective-permute-start.13) | collective-permute-done | bytes 12320 | tf_op jit(solution)/shard_map/ppermute | solution.py:230
  48.5 1.4 %collective-permute-start.15 = (f32[1,3072]{1,0:T(1,128)S(1)}, f32[1,3072]{1,0:T(1,128)S(1)}, u32[]{:S(2)}, u32[]{:S(2)}) collective-permute-start(f32[1,3072]{1,0:T(1,128)S(1)} %sum.5.refs_1_), channel_id=1, source_target_pairs={{0,5},{1,4},{2,7},{3,6},{4,1},{5,0},{6,3},{7,2},{8,13},{9,12},{10,... | collective-permute-start | bytes 36872 | tf_op jit(solution)/shard_map/ppermute | solution.py:230
  49.8 1.8 %collective-permute-done.15.refs_0_ = f32[1,3072]{1,0:T(1,128)S(1)} collective-permute-done((f32[1,3072]{1,0:T(1,128)S(1)}, f32[1,3072]{1,0:T(1,128)S(1)}, u32[]{:S(2)}, u32[]{:S(2)}) %collective-permute-start.15) | collective-permute-done | bytes 12320 | tf_op jit(solution)/shard_map/ppermute | solution.py:230
  51.6 2.4 %collective-permute-start.16 = (f32[1,3072]{1,0:T(1,128)S(1)}, f32[1,3072]{1,0:T(1,128)S(1)}, u32[]{:S(2)}, u32[]{:S(2)}) collective-permute-start(f32[1,3072]{1,0:T(1,128)S(1)} %sum.6.refs_1_), channel_id=1, source_target_pairs={{0,6},{1,7},{2,4},{3,5},{4,2},{5,3},{6,0},{7,1},{8,14},{9,15},{10,... | collective-permute-start | bytes 36872 | tf_op jit(solution)/shard_map/ppermute | solution.py:230
  54.0 1.0 %branch.1 = bf16[1,128,3072]{2,1,0:T(8,128)(2,1)} custom-call(f32[128,3072]{1,0:T(8,128)S(1)} %get-tuple-element.40.projected_ref, f32[1,3072]{1,0:T(1,128)S(1)} %bitcast.2), custom_call_target="tpu_custom_call" | custom-call | tf_op jit(solution)/shard_map/branch/pallas_call | solution.py:372
  55.0 0.7 %collective-permute-done.16.refs_0_ = f32[1,3072]{1,0:T(1,128)S(1)} collective-permute-done((f32[1,3072]{1,0:T(1,128)S(1)}, f32[1,3072]{1,0:T(1,128)S(1)}, u32[]{:S(2)}, u32[]{:S(2)}) %collective-permute-start.16) | collective-permute-done | bytes 12320 | tf_op jit(solution)/shard_map/ppermute | solution.py:230
  55.6 0.6 %sum.7 = f32[1,3072]{1,0:T(1,128)} custom-call(f32[1,3072]{1,0:T(1,128)S(1)} %collective-permute-done.16.refs_0_, f32[1,3072]{1,0:T(1,128)S(1)} %sum.6.refs_1_), custom_call_target="tpu_custom_call" | custom-call | tf_op jit(solution)/shard_map/sum/pallas_call | solution.py:231
  (22 shorter events, 2.0 us)
Async XLA Ops:
  1.8 14.6 %collective-permute-start = (bf16[784,256]{1,0:T(8,128)(2,1)S(1)}, bf16[784,256]{1,0:T(8,128)(2,1)S(1)}, u32[]{:S(2)}, u32[]{:S(2)}) collective-permute-start(bf16[784,256]{1,0:T(8,128)(2,1)S(1)} %pack_far.1), channel_id=1, source_target_pairs={{0,28},{4,24},{8,20},{12,16},{16,12},{20,8},{24,4},{28,0},{1,29},{... | collective-permute-start | bytes 1204232 | tf_op jit(solution)/shard_map/ppermute | solution.py:263
  7.2 17.3 %collective-permute-start.1 = (bf16[784,256]{1,0:T(8,128)(2,1)S(1)}, bf16[784,256]{1,0:T(8,128)(2,1)S(1)}, u32[]{:S(2)}, u32[]{:S(2)}) collective-permute-start(bf16[784,256]{1,0:T(8,128)(2,1)S(1)} %get-tuple-element.23), channel_id=1, source_target_pairs={{0,12},{4,16},{8,28},{12,0},{16,4},{20,24},{24,20},{28,8},{1,13},{... | collective-permute-start | bytes 1204232 | tf_op jit(solution)/shard_map/ppermute | solution.py:263
  8.1 16.5 %collective-permute-start.2 = (bf16[784,256]{1,0:T(8,128)(2,1)S(1)}, bf16[784,256]{1,0:T(8,128)(2,1)S(1)}, u32[]{:S(2)}, u32[]{:S(2)}) collective-permute-start(bf16[784,256]{1,0:T(8,128)(2,1)S(1)} %get-tuple-element.24), channel_id=1, source_target_pairs={{0,20},{4,8},{8,4},{12,24},{16,28},{20,0},{24,12},{28,16},{1,21},{... | collective-permute-start | bytes 1204232 | tf_op jit(solution)/shard_map/ppermute | solution.py:263
  9.9 17.9 %collective-permute-start.9 = (bf16[384,256]{1,0:T(8,128)(2,1)S(1)}, bf16[384,256]{1,0:T(8,128)(2,1)S(1)}, u32[]{:S(2)}, u32[]{:S(2)}) collective-permute-start(bf16[384,256]{1,0:T(8,128)(2,1)S(1)} %get-tuple-element.36), channel_id=1, source_target_pairs={{0,28},{4,24},{8,20},{12,16},{16,12},{20,8},{24,4},{28,0},{1,29},{... | collective-permute-start | bytes 589832 | tf_op jit(solution)/shard_map/ppermute | solution.py:263
  12.6 20.7 %collective-permute-start.5 = (bf16[384,256]{1,0:T(8,128)(2,1)S(1)}, bf16[384,256]{1,0:T(8,128)(2,1)S(1)}, u32[]{:S(2)}, u32[]{:S(2)}) collective-permute-start(bf16[384,256]{1,0:T(8,128)(2,1)S(1)} %get-tuple-element.31), channel_id=1, source_target_pairs={{0,12},{4,16},{8,28},{12,0},{16,4},{20,24},{24,20},{28,8},{1,13},{... | collective-permute-start | bytes 589832 | tf_op jit(solution)/shard_map/ppermute | solution.py:263
  16.5 16.8 %collective-permute-start.6 = (bf16[384,256]{1,0:T(8,128)(2,1)S(1)}, bf16[384,256]{1,0:T(8,128)(2,1)S(1)}, u32[]{:S(2)}, u32[]{:S(2)}) collective-permute-start(bf16[384,256]{1,0:T(8,128)(2,1)S(1)} %get-tuple-element.32), channel_id=1, source_target_pairs={{0,20},{4,8},{8,4},{12,24},{16,28},{20,0},{24,12},{28,16},{1,21},{... | collective-permute-start | bytes 589832 | tf_op jit(solution)/shard_map/ppermute | solution.py:263
  24.5 3.3 %collective-permute-start.3 = (bf16[1664,256]{1,0:T(8,128)(2,1)S(1)}, bf16[1664,256]{1,0:T(8,128)(2,1)S(1)}, u32[]{:S(2)}, u32[]{:S(2)}) collective-permute-start(bf16[1664,256]{1,0:T(8,128)(2,1)S(1)} %get-tuple-element.29), channel_id=1, source_target_pairs={{0,4},{4,0},{8,12},{12,8},{16,20},{20,16},{24,28},{28,24},{1,5},{5... | collective-permute-start | bytes 2555912 | tf_op jit(solution)/shard_map/ppermute | solution.py:254
  24.7 3.4 %collective-permute-start.4 = (bf16[1664,256]{1,0:T(8,128)(2,1)S(1)}, bf16[1664,256]{1,0:T(8,128)(2,1)S(1)}, u32[]{:S(2)}, u32[]{:S(2)}) collective-permute-start(bf16[1664,256]{1,0:T(8,128)(2,1)S(1)} %get-tuple-element.30), channel_id=1, source_target_pairs={{0,4},{4,0},{8,12},{12,8},{16,20},{20,16},{24,28},{28,24},{1,5},{5... | collective-permute-start | bytes 2555912 | tf_op jit(solution)/shard_map/ppermute | solution.py:254
  30.4 8.1 %collective-permute-start.10 = (bf16[128,384]{1,0:T(8,128)(2,1)S(1)}, bf16[128,384]{1,0:T(8,128)(2,1)S(1)}, u32[]{:S(2)}, u32[]{:S(2)}) collective-permute-start(bf16[128,384]{1,0:T(8,128)(2,1)S(1)} %get-tuple-element.37), channel_id=1, source_target_pairs={{0,28},{4,24},{8,20},{12,16},{16,12},{20,8},{24,4},{28,0},{1,29},{... | collective-permute-start | bytes 294920 | tf_op jit(solution)/shard_map/ppermute | solution.py:263
  35.6 4.1 %collective-permute-start.8 = (bf16[128,384]{1,0:T(8,128)(2,1)S(1)}, bf16[128,384]{1,0:T(8,128)(2,1)S(1)}, u32[]{:S(2)}, u32[]{:S(2)}) collective-permute-start(bf16[128,384]{1,0:T(8,128)(2,1)S(1)} %get-tuple-element.35), channel_id=1, source_target_pairs={{0,12},{4,16},{8,28},{12,0},{16,4},{20,24},{24,20},{28,8},{1,13},{... | collective-permute-start | bytes 294920 | tf_op jit(solution)/shard_map/ppermute | solution.py:263
  36.6 4.8 %collective-permute-start.7 = (bf16[128,384]{1,0:T(8,128)(2,1)S(1)}, bf16[128,384]{1,0:T(8,128)(2,1)S(1)}, u32[]{:S(2)}, u32[]{:S(2)}) collective-permute-start(bf16[128,384]{1,0:T(8,128)(2,1)S(1)} %get-tuple-element.33), channel_id=1, source_target_pairs={{0,20},{4,8},{8,4},{12,24},{16,28},{20,0},{24,12},{28,16},{1,21},{... | collective-permute-start | bytes 294920 | tf_op jit(solution)/shard_map/ppermute | solution.py:263
  41.4 12.6 %copy-start = (f32[3072]{0:T(1024)S(1)}, f32[3072]{0:T(1024)}, u32[]{:S(2)}) copy-start(f32[3072]{0:T(1024)} %param.20) | copy-start | bytes 36868
  42.1 1.4 %collective-permute-start.11 = (f32[1,3072]{1,0:T(1,128)S(1)}, f32[1,3072]{1,0:T(1,128)S(1)}, u32[]{:S(2)}, u32[]{:S(2)}) collective-permute-start(f32[1,3072]{1,0:T(1,128)S(1)} %get-tuple-element.41.refs_1_), channel_id=1, source_target_pairs={{0,4},{1,5},{2,6},{3,7},{4,0},{5,1},{6,2},{7,3},{8,12},{9,13},{10,... | collective-permute-start | bytes 36872 | tf_op jit(solution)/shard_map/ppermute | solution.py:230
  43.5 4.0 %collective-permute-start.12 = (f32[1,3072]{1,0:T(1,128)S(1)}, f32[1,3072]{1,0:T(1,128)S(1)}, u32[]{:S(2)}, u32[]{:S(2)}) collective-permute-start(f32[1,3072]{1,0:T(1,128)S(1)} %sum.4.refs_3_), channel_id=1, source_target_pairs={{0,28},{1,29},{2,30},{3,31},{4,24},{5,25},{6,26},{7,27},{8,20},{9,... | collective-permute-start | bytes 36872 | tf_op jit(solution)/shard_map/ppermute | solution.py:230
  45.2 3.1 %collective-permute-start.13 = (f32[1,3072]{1,0:T(1,128)S(1)}, f32[1,3072]{1,0:T(1,128)S(1)}, u32[]{:S(2)}, u32[]{:S(2)}) collective-permute-start(f32[1,3072]{1,0:T(1,128)S(1)} %sum.4.refs_3_), channel_id=1, source_target_pairs={{0,20},{1,21},{2,22},{3,23},{4,16},{5,17},{6,18},{7,19},{8,28},{9,... | collective-permute-start | bytes 36872 | tf_op jit(solution)/shard_map/ppermute | solution.py:230
  45.4 3.1 %collective-permute-start.14 = (f32[1,3072]{1,0:T(1,128)S(1)}, f32[1,3072]{1,0:T(1,128)S(1)}, u32[]{:S(2)}, u32[]{:S(2)}) collective-permute-start(f32[1,3072]{1,0:T(1,128)S(1)} %sum.4.refs_3_), channel_id=1, source_target_pairs={{0,12},{1,13},{2,14},{3,15},{4,8},{5,9},{6,10},{7,11},{8,4},{9,5},... | collective-permute-start | bytes 36872 | tf_op jit(solution)/shard_map/ppermute | solution.py:230
  48.5 3.1 %collective-permute-start.15 = (f32[1,3072]{1,0:T(1,128)S(1)}, f32[1,3072]{1,0:T(1,128)S(1)}, u32[]{:S(2)}, u32[]{:S(2)}) collective-permute-start(f32[1,3072]{1,0:T(1,128)S(1)} %sum.5.refs_1_), channel_id=1, source_target_pairs={{0,5},{1,4},{2,7},{3,6},{4,1},{5,0},{6,3},{7,2},{8,13},{9,12},{10,... | collective-permute-start | bytes 36872 | tf_op jit(solution)/shard_map/ppermute | solution.py:230
  51.6 4.0 %collective-permute-start.16 = (f32[1,3072]{1,0:T(1,128)S(1)}, f32[1,3072]{1,0:T(1,128)S(1)}, u32[]{:S(2)}, u32[]{:S(2)}) collective-permute-start(f32[1,3072]{1,0:T(1,128)S(1)} %sum.6.refs_1_), channel_id=1, source_target_pairs={{0,6},{1,7},{2,4},{3,5},{4,2},{5,3},{6,0},{7,1},{8,14},{9,15},{10,... | collective-permute-start | bytes 36872 | tf_op jit(solution)/shard_map/ppermute | solution.py:230

commit v5 on v4

--- a/solution.py
+++ b/solution.py
@@ -86,6 +86,16 @@
             loads[t, p] = pltpu.make_async_copy(source.at[0, :, pl.ds(column, part)], scratch.at[t, p], in_sems.at[t, p])
             loads[t, p].start()
     cosines, sines = tables(order_ref.shape[0], rows, head_dim)
+    def store(t, change):
+        for p, out in enumerate(outs):
+            loads[t, p].wait()
+            for i in range(per_group):
+                at = (i * len(turns) + t // 2) * rows
+                out[at : at + rows, t % 2 * head_dim : (t % 2 + 1) * head_dim] = change(scratch[t, p, :, i * head_dim : (i + 1) * head_dim])
+
+    for t in range(n_in):
+        if not turns[t // 2]:
+            store(t, lambda x: x)
     small[0].wait()
     cosine, sine = rotation(order_ref[lax.axis_index("ctx")], rows, head_dim, cosines, sines)
 
@@ -93,19 +103,15 @@
         x = x.astype(jnp.float32)
         return (x * cosine + pltpu.roll(x, head_dim // 2, 1) * sine).astype(jnp.bfloat16)
 
+    for t in range(n_in):
+        if turns[t // 2]:
+            store(t, turned)
     small[1].wait()
     if with_ids:
         ids = jnp.broadcast_to(ids_ref[...].astype(jnp.float32), (ID_ROWS, rows)).astype(jnp.bfloat16)
         for out in outs:
             out[per_group * len(turns) * rows :, :head_dim] = ids
             out[per_group * len(turns) * rows :, head_dim:] = ids
-    for t in range(n_in):
-        for p, out in enumerate(outs):
-            loads[t, p].wait()
-            for i in range(per_group):
-                x = scratch[t, p, :, i * head_dim : (i + 1) * head_dim]
-                at = (i * len(turns) + t // 2) * rows
-                out[at : at + rows, t % 2 * head_dim : (t % 2 + 1) * head_dim] = turned(x) if turns[t // 2] else x
 
 
 def arrived_kernel(*refs):

time: 56.5 us -> 56.6 us (level)
  no operation moved by 1% of the time
where the time goes in v5:
time: 56.6 us; the launch traced here: 56.4 us
  starting transfers between devices  20.7 us (37%)
  Pallas kernels  18.1 us (32%)
  waiting for transfers between devices  16.8 us (30%)
  between operations  0.75 us (1%)
    ppermute x9, starting transfers between devices, send(): lax.ppermute(x, 'ctx', [(j, j ^ offset[j] * members + cross) for j in ran...  12.7 us
    ppermute x9, waiting for transfers between devices, send(): lax.ppermute(x, 'ctx', [(j, j ^ offset[j] * members + cross) for j in ran...  11.5 us
    ppermute x6, starting transfers between devices, exchange_sum(): lax.ppermute(x, ('ctx', 'dp'), [(j * n_dp + z, (j ^ own) * n_dp + (z ^ ot...  7.48 us
    pallas_call x3, Pallas kernels, pack(): pl.pallas_call(functools.partial(pack_kernel, [route[place] for place in...  5.32 us
    ppermute x6, waiting for transfers between devices, exchange_sum(): lax.ppermute(x, ('ctx', 'dp'), [(j * n_dp + z, (j ^ own) * n_dp + (z ^ ot...  5.09 us
    pallas_call x2, Pallas kernels, attend(): pl.pallas_call(functools.partial(attend_kernel, groups, members, places,...  4.63 us
    pallas_call x1, Pallas kernels, local(): pl.pallas_call(stage_kernel, out_shape=[pltpu.VMEM(out_weight.shape, bf16...  3.84 us
    pallas_call x3, Pallas kernels, local(): pl.pallas_call(functools.partial(part_kernel, members, route[place], 512)...  1.82 us
  transfers between devices with their start and end apart: 17, of which 11 were waited for; matrix products, arithmetic and copies ran while one was open for 0% of the time, Pallas kernels for 27%

profile of v5, /device:TPU:0, one launch (start us, length us, event | category | flops | bytes accessed | tf_op | source)
XLA Modules:
  0.0 56.4 jit_solution(7198630863458625097)
XLA Ops:
  0.6 1.4 %pack_far.1 = bf16[784,256]{1,0:T(8,128)(2,1)S(1)} custom-call(s32[8]{0:T(128)} %order_hbm.5, s32[1,128]{1,0:T(1,128)} %ids_hbm.5, bf16[1,128,1536]{2,1,0:T(8,128)(2,1)} %refs_0_.4, bf16[1,128,1536]{2,1,0:T(8,128)(2,1)} %refs_1_.4, bf16[1,128,1536]{2,1,0:T(8,128)(2,1)} %refs_2_.3, bf16[1,128,1536]{2,1,0:T(8,128)(2,1)} %refs_3_.3), custom_call_target="tpu_custom_call" | custom-call | tf_op jit(solution)/shard_map/pack_far/pallas_call | solution.py:278
  2.0 3.4 %collective-permute-start = (bf16[784,256]{1,0:T(8,128)(2,1)S(1)}, bf16[784,256]{1,0:T(8,128)(2,1)S(1)}, u32[]{:S(2)}, u32[]{:S(2)}) collective-permute-start(bf16[784,256]{1,0:T(8,128)(2,1)S(1)} %pack_far.1), channel_id=1, source_target_pairs={{0,28},{4,24},{8,20},{12,16},{16,12},{20,8},{24,4},{28,0},{1,29},{... | collective-permute-start | bytes 1204232 | tf_op jit(solution)/shard_map/ppermute | solution.py:269
  5.4 2.2 %pack_near.1 = (bf16[784,256]{1,0:T(8,128)(2,1)S(1)}, bf16[784,256]{1,0:T(8,128)(2,1)S(1)}, bf16[784,256]{1,0:T(8,128)(2,1)S(1)}) custom-call(s32[8]{0:T(128)} %order_hbm.5, s32[1,128]{1,0:T(1,128)} %ids_hbm.5, bf16[1,128,1536]{2,1,0:T(8,128)(2,1)} %refs_0_.4, bf16[1,128,1536]{2,1,0:T(8,128)(2,1)} %refs_1_.4, bf16[1,128,1536]{2,1,0:T(8,128)(2,1)} %refs_2_.3, ...), custom_call_target="tpu_custom_call" | custom-call | tf_op jit(solution)/shard_map/pack_near/pallas_call | solution.py:278
  7.6 0.9 %collective-permute-start.1 = (bf16[784,256]{1,0:T(8,128)(2,1)S(1)}, bf16[784,256]{1,0:T(8,128)(2,1)S(1)}, u32[]{:S(2)}, u32[]{:S(2)}) collective-permute-start(bf16[784,256]{1,0:T(8,128)(2,1)S(1)} %get-tuple-element.23), channel_id=1, source_target_pairs={{0,12},{4,16},{8,28},{12,0},{16,4},{20,24},{24,20},{28,8},{1,13},{... | collective-permute-start | bytes 1204232 | tf_op jit(solution)/shard_map/ppermute | solution.py:269
  8.5 1.8 %pack_queries.1 = (bf16[384,256]{1,0:T(8,128)(2,1)S(1)}, bf16[384,256]{1,0:T(8,128)(2,1)S(1)}, bf16[384,256]{1,0:T(8,128)(2,1)S(1)}, bf16[384,256]{1,0:T(8,128)(2,1)S(1)}) custom-call(s32[8]{0:T(128)} %order_hbm.5, s32[1,128]{1,0:T(1,128)} %ids_hbm.5, bf16[1,128,1536]{2,1,0:T(8,128)(2,1)} %refs_0_.5, bf16[1,128,1536]{2,1,0:T(8,128)(2,1)} %refs_1_.5), custom_call_target="tpu_custom_call" | custom-call | tf_op jit(solution)/shard_map/pack_queries/pallas_call | solution.py:278
  10.3 2.7 %collective-permute-start.9 = (bf16[384,256]{1,0:T(8,128)(2,1)S(1)}, bf16[384,256]{1,0:T(8,128)(2,1)S(1)}, u32[]{:S(2)}, u32[]{:S(2)}) collective-permute-start(bf16[384,256]{1,0:T(8,128)(2,1)S(1)} %get-tuple-element.36), channel_id=1, source_target_pairs={{0,28},{4,24},{8,20},{12,16},{16,12},{20,8},{24,4},{28,0},{1,29},{... | collective-permute-start | bytes 589832 | tf_op jit(solution)/shard_map/ppermute | solution.py:269
  13.0 3.8 %stage.1 = (bf16[1536,3072]{1,0:T(8,128)(2,1)S(1)}, bf16[1,128,3072]{2,1,0:T(8,128)(2,1)S(1)}, f32[8,128]{1,0:T(8,128)S(1)}) custom-call(bf16[1536,3072]{1,0:T(8,128)(2,1)} %w_hbm.1, bf16[1,128,3072]{2,1,0:T(8,128)(2,1)} %cot_hbm.1, bf16[384,256]{1,0:T(8,128)(2,1)S(1)} %get-tuple-element.25.refs_2_.after_ref.refs_0_.refs_8_), custom_call_target="tpu_custom_call" | custom-call | tf_op jit(solution)/shard_map/stage/pallas_call | solution.py:300
  17.4 7.3 %collective-permute-done.1.refs_0_.refs_2_ = bf16[784,256]{1,0:T(8,128)(2,1)S(1)} collective-permute-done((bf16[784,256]{1,0:T(8,128)(2,1)S(1)}, bf16[784,256]{1,0:T(8,128)(2,1)S(1)}, u32[]{:S(2)}, u32[]{:S(2)}) %collective-permute-start.1) | collective-permute-done | bytes 401440 | tf_op jit(solution)/shard_map/ppermute | solution.py:269
  24.9 0.5 collective-permute-start.4
  25.4 2.6 %collective-permute-done.9.refs_1_.refs_9_ = bf16[384,256]{1,0:T(8,128)(2,1)S(1)} collective-permute-done((bf16[384,256]{1,0:T(8,128)(2,1)S(1)}, bf16[384,256]{1,0:T(8,128)(2,1)S(1)}, u32[]{:S(2)}, u32[]{:S(2)}) %collective-permute-start.9) | collective-permute-done | bytes 196640 | tf_op jit(solution)/shard_map/ppermute | solution.py:269
  28.3 2.3 %attend_early.1 = (bf16[128,384]{1,0:T(8,128)(2,1)S(1)}, bf16[128,384]{1,0:T(8,128)(2,1)S(1)}) custom-call(bf16[784,256]{1,0:T(8,128)(2,1)S(1)} %get-tuple-element.22.refs_0_, bf16[784,256]{1,0:T(8,128)(2,1)S(1)} %collective-permute-done.refs_1_, bf16[784,256]{1,0:T(8,128)(2,1)S(1)} %collective-permute-done.1.refs_0_.refs_2_, ...), custom_call_target="tpu_custom_call" | custom-call | tf_op jit(solution)/shard_map/attend_early/pallas_call | solution.py:344
  30.6 2.8 %collective-permute-start.10 = (bf16[128,384]{1,0:T(8,128)(2,1)S(1)}, bf16[128,384]{1,0:T(8,128)(2,1)S(1)}, u32[]{:S(2)}, u32[]{:S(2)}) collective-permute-start(bf16[128,384]{1,0:T(8,128)(2,1)S(1)} %get-tuple-element.37), channel_id=1, source_target_pairs={{0,28},{4,24},{8,20},{12,16},{16,12},{20,8},{24,4},{28,0},{1,29},{... | collective-permute-start | bytes 294920 | tf_op jit(solution)/shard_map/ppermute | solution.py:269
  33.5 2.3 %attend_late.1 = (bf16[128,384]{1,0:T(8,128)(2,1)S(1)}, bf16[128,384]{1,0:T(8,128)(2,1)S(1)}) custom-call(bf16[784,256]{1,0:T(8,128)(2,1)S(1)} %get-tuple-element.22.refs_0_, bf16[784,256]{1,0:T(8,128)(2,1)S(1)} %collective-permute-done.refs_1_, bf16[784,256]{1,0:T(8,128)(2,1)S(1)} %collective-permute-done.1.refs_0_.refs_2_, ...), custom_call_target="tpu_custom_call" | custom-call | tf_op jit(solution)/shard_map/attend_late/pallas_call | solution.py:344
  35.8 1.0 %collective-permute-start.8 = (bf16[128,384]{1,0:T(8,128)(2,1)S(1)}, bf16[128,384]{1,0:T(8,128)(2,1)S(1)}, u32[]{:S(2)}, u32[]{:S(2)}) collective-permute-start(bf16[128,384]{1,0:T(8,128)(2,1)S(1)} %get-tuple-element.35), channel_id=1, source_target_pairs={{0,12},{4,16},{8,28},{12,0},{16,4},{20,24},{24,20},{28,8},{1,13},{... | collective-permute-start | bytes 294920 | tf_op jit(solution)/shard_map/ppermute | solution.py:269
  36.8 1.4 %collective-permute-start.7 = (bf16[128,384]{1,0:T(8,128)(2,1)S(1)}, bf16[128,384]{1,0:T(8,128)(2,1)S(1)}, u32[]{:S(2)}, u32[]{:S(2)}) collective-permute-start(bf16[128,384]{1,0:T(8,128)(2,1)S(1)} %get-tuple-element.33), channel_id=1, source_target_pairs={{0,20},{4,8},{8,4},{12,24},{16,28},{20,0},{24,12},{28,16},{1,21},{... | collective-permute-start | bytes 294920 | tf_op jit(solution)/shard_map/ppermute | solution.py:269
  38.2 0.6 %part0.1.refs_0_ = f32[128,3072]{1,0:T(8,128)S(1)} custom-call(bf16[128,384]{1,0:T(8,128)(2,1)S(1)} %get-tuple-element.38.ta_ref, bf16[1536,3072]{1,0:T(8,128)(2,1)S(1)} %get-tuple-element.34.w_ref), custom_call_target="tpu_custom_call" | custom-call | tf_op jit(solution)/shard_map/part0/pallas_call | solution.py:362
  38.8 0.6 %part1.1.refs_0_ = f32[128,3072]{1,0:T(8,128)S(1)} custom-call(bf16[128,384]{1,0:T(8,128)(2,1)S(1)} %collective-permute-done.10.ta_ref, bf16[1536,3072]{1,0:T(8,128)(2,1)S(1)} %get-tuple-element.34.w_ref, f32[128,3072]{1,0:T(8,128)S(1)} %part0.1.refs_0_), custom_call_target="tpu_custom_call" | custom-call | tf_op jit(solution)/shard_map/part1/pallas_call | solution.py:362
  39.9 0.6 %part2.1.begun_ref = f32[128,3072]{1,0:T(8,128)S(1)} custom-call(bf16[128,384]{1,0:T(8,128)(2,1)S(1)} %collective-permute-done.8.ta_ref, bf16[1536,3072]{1,0:T(8,128)(2,1)S(1)} %get-tuple-element.34.w_ref, f32[128,3072]{1,0:T(8,128)S(1)} %part1.1.refs_0_), custom_call_target="tpu_custom_call" | custom-call | tf_op jit(solution)/shard_map/part2/pallas_call | solution.py:362
  40.5 1.1 %collective-permute-done.7.ta_ref = bf16[128,384]{1,0:T(8,128)(2,1)S(1)} collective-permute-done((bf16[128,384]{1,0:T(8,128)(2,1)S(1)}, bf16[128,384]{1,0:T(8,128)(2,1)S(1)}, u32[]{:S(2)}, u32[]{:S(2)}) %collective-permute-start.7) | collective-permute-done | bytes 98336 | tf_op jit(solution)/shard_map/ppermute | solution.py:269
  41.6 0.6 %project.1 = (f32[128,3072]{1,0:T(8,128)S(1)}, f32[1,3072]{1,0:T(1,128)S(1)}) custom-call(bf16[128,384]{1,0:T(8,128)(2,1)S(1)} %collective-permute-done.7.ta_ref, bf16[1536,3072]{1,0:T(8,128)(2,1)S(1)} %get-tuple-element.34.w_ref, f32[128,3072]{1,0:T(8,128)S(1)} %part2.1.begun_ref, bf16[1,128,3072]{2,1,0:T(8,128)(2,1)S(1)} %get-tuple-element.39.cot_ref), custom_call_target="tpu_custom_call" | custom-call | tf_op jit(solution)/shard_map/project/pallas_call | solution.py:370
  42.2 0.5 collective-permute-start.11
  42.8 0.8 %collective-permute-done.11.refs_0_ = f32[1,3072]{1,0:T(1,128)S(1)} collective-permute-done((f32[1,3072]{1,0:T(1,128)S(1)}, f32[1,3072]{1,0:T(1,128)S(1)}, u32[]{:S(2)}, u32[]{:S(2)}) %collective-permute-start.11) | collective-permute-done | bytes 12320 | tf_op jit(solution)/shard_map/ppermute | solution.py:236
  43.6 1.8 %collective-permute-start.12 = (f32[1,3072]{1,0:T(1,128)S(1)}, f32[1,3072]{1,0:T(1,128)S(1)}, u32[]{:S(2)}, u32[]{:S(2)}) collective-permute-start(f32[1,3072]{1,0:T(1,128)S(1)} %sum.4.refs_3_), channel_id=1, source_target_pairs={{0,28},{1,29},{2,30},{3,31},{4,24},{5,25},{6,26},{7,27},{8,20},{9,... | collective-permute-start | bytes 36872 | tf_op jit(solution)/shard_map/ppermute | solution.py:236
  45.5 1.3 %collective-permute-start.14 = (f32[1,3072]{1,0:T(1,128)S(1)}, f32[1,3072]{1,0:T(1,128)S(1)}, u32[]{:S(2)}, u32[]{:S(2)}) collective-permute-start(f32[1,3072]{1,0:T(1,128)S(1)} %sum.4.refs_3_), channel_id=1, source_target_pairs={{0,12},{1,13},{2,14},{3,15},{4,8},{5,9},{6,10},{7,11},{8,4},{9,5},... | collective-permute-start | bytes 36872 | tf_op jit(solution)/shard_map/ppermute | solution.py:236
  46.8 0.9 %collective-permute-done.12.refs_0_ = f32[1,3072]{1,0:T(1,128)S(1)} collective-permute-done((f32[1,3072]{1,0:T(1,128)S(1)}, f32[1,3072]{1,0:T(1,128)S(1)}, u32[]{:S(2)}, u32[]{:S(2)}) %collective-permute-start.12) | collective-permute-done | bytes 12320 | tf_op jit(solution)/shard_map/ppermute | solution.py:236
  47.6 0.9 %collective-permute-done.13.refs_1_ = f32[1,3072]{1,0:T(1,128)S(1)} collective-permute-done((f32[1,3072]{1,0:T(1,128)S(1)}, f32[1,3072]{1,0:T(1,128)S(1)}, u32[]{:S(2)}, u32[]{:S(2)}) %collective-permute-start.13) | collective-permute-done | bytes 12320 | tf_op jit(solution)/shard_map/ppermute | solution.py:236
  48.6 1.4 %collective-permute-start.15 = (f32[1,3072]{1,0:T(1,128)S(1)}, f32[1,3072]{1,0:T(1,128)S(1)}, u32[]{:S(2)}, u32[]{:S(2)}) collective-permute-start(f32[1,3072]{1,0:T(1,128)S(1)} %sum.5.refs_1_), channel_id=1, source_target_pairs={{0,5},{1,4},{2,7},{3,6},{4,1},{5,0},{6,3},{7,2},{8,13},{9,12},{10,... | collective-permute-start | bytes 36872 | tf_op jit(solution)/shard_map/ppermute | solution.py:236
  50.0 1.8 %collective-permute-done.15.refs_0_ = f32[1,3072]{1,0:T(1,128)S(1)} collective-permute-done((f32[1,3072]{1,0:T(1,128)S(1)}, f32[1,3072]{1,0:T(1,128)S(1)}, u32[]{:S(2)}, u32[]{:S(2)}) %collective-permute-start.15) | collective-permute-done | bytes 12320 | tf_op jit(solution)/shard_map/ppermute | solution.py:236
  51.8 2.4 %collective-permute-start.16 = (f32[1,3072]{1,0:T(1,128)S(1)}, f32[1,3072]{1,0:T(1,128)S(1)}, u32[]{:S(2)}, u32[]{:S(2)}) collective-permute-start(f32[1,3072]{1,0:T(1,128)S(1)} %sum.6.refs_1_), channel_id=1, source_target_pairs={{0,6},{1,7},{2,4},{3,5},{4,2},{5,3},{6,0},{7,1},{8,14},{9,15},{10,... | collective-permute-start | bytes 36872 | tf_op jit(solution)/shard_map/ppermute | solution.py:236
  54.2 1.0 %branch.1 = bf16[1,128,3072]{2,1,0:T(8,128)(2,1)} custom-call(f32[128,3072]{1,0:T(8,128)S(1)} %get-tuple-element.40.projected_ref, f32[1,3072]{1,0:T(1,128)S(1)} %bitcast.2), custom_call_target="tpu_custom_call" | custom-call | tf_op jit(solution)/shard_map/branch/pallas_call | solution.py:378
  55.2 0.6 %collective-permute-done.16.refs_0_ = f32[1,3072]{1,0:T(1,128)S(1)} collective-permute-done((f32[1,3072]{1,0:T(1,128)S(1)}, f32[1,3072]{1,0:T(1,128)S(1)}, u32[]{:S(2)}, u32[]{:S(2)}) %collective-permute-start.16) | collective-permute-done | bytes 12320 | tf_op jit(solution)/shard_map/ppermute | solution.py:236
  55.8 0.6 %sum.7 = f32[1,3072]{1,0:T(1,128)} custom-call(f32[1,3072]{1,0:T(1,128)S(1)} %collective-permute-done.16.refs_0_, f32[1,3072]{1,0:T(1,128)S(1)} %sum.6.refs_1_), custom_call_target="tpu_custom_call" | custom-call | tf_op jit(solution)/shard_map/sum/pallas_call | solution.py:237
  (22 shorter events, 1.8 us)
Async XLA Ops:
  2.0 14.8 %collective-permute-start = (bf16[784,256]{1,0:T(8,128)(2,1)S(1)}, bf16[784,256]{1,0:T(8,128)(2,1)S(1)}, u32[]{:S(2)}, u32[]{:S(2)}) collective-permute-start(bf16[784,256]{1,0:T(8,128)(2,1)S(1)} %pack_far.1), channel_id=1, source_target_pairs={{0,28},{4,24},{8,20},{12,16},{16,12},{20,8},{24,4},{28,0},{1,29},{... | collective-permute-start | bytes 1204232 | tf_op jit(solution)/shard_map/ppermute | solution.py:269
  7.6 17.1 %collective-permute-start.1 = (bf16[784,256]{1,0:T(8,128)(2,1)S(1)}, bf16[784,256]{1,0:T(8,128)(2,1)S(1)}, u32[]{:S(2)}, u32[]{:S(2)}) collective-permute-start(bf16[784,256]{1,0:T(8,128)(2,1)S(1)} %get-tuple-element.23), channel_id=1, source_target_pairs={{0,12},{4,16},{8,28},{12,0},{16,4},{20,24},{24,20},{28,8},{1,13},{... | collective-permute-start | bytes 1204232 | tf_op jit(solution)/shard_map/ppermute | solution.py:269
  8.5 16.3 %collective-permute-start.2 = (bf16[784,256]{1,0:T(8,128)(2,1)S(1)}, bf16[784,256]{1,0:T(8,128)(2,1)S(1)}, u32[]{:S(2)}, u32[]{:S(2)}) collective-permute-start(bf16[784,256]{1,0:T(8,128)(2,1)S(1)} %get-tuple-element.24), channel_id=1, source_target_pairs={{0,20},{4,8},{8,4},{12,24},{16,28},{20,0},{24,12},{28,16},{1,21},{... | collective-permute-start | bytes 1204232 | tf_op jit(solution)/shard_map/ppermute | solution.py:269
  10.3 17.7 %collective-permute-start.9 = (bf16[384,256]{1,0:T(8,128)(2,1)S(1)}, bf16[384,256]{1,0:T(8,128)(2,1)S(1)}, u32[]{:S(2)}, u32[]{:S(2)}) collective-permute-start(bf16[384,256]{1,0:T(8,128)(2,1)S(1)} %get-tuple-element.36), channel_id=1, source_target_pairs={{0,28},{4,24},{8,20},{12,16},{16,12},{20,8},{24,4},{28,0},{1,29},{... | collective-permute-start | bytes 589832 | tf_op jit(solution)/shard_map/ppermute | solution.py:269
  13.0 20.5 %collective-permute-start.5 = (bf16[384,256]{1,0:T(8,128)(2,1)S(1)}, bf16[384,256]{1,0:T(8,128)(2,1)S(1)}, u32[]{:S(2)}, u32[]{:S(2)}) collective-permute-start(bf16[384,256]{1,0:T(8,128)(2,1)S(1)} %get-tuple-element.31), channel_id=1, source_target_pairs={{0,12},{4,16},{8,28},{12,0},{16,4},{20,24},{24,20},{28,8},{1,13},{... | collective-permute-start | bytes 589832 | tf_op jit(solution)/shard_map/ppermute | solution.py:269
  16.9 16.6 %collective-permute-start.6 = (bf16[384,256]{1,0:T(8,128)(2,1)S(1)}, bf16[384,256]{1,0:T(8,128)(2,1)S(1)}, u32[]{:S(2)}, u32[]{:S(2)}) collective-permute-start(bf16[384,256]{1,0:T(8,128)(2,1)S(1)} %get-tuple-element.32), channel_id=1, source_target_pairs={{0,20},{4,8},{8,4},{12,24},{16,28},{20,0},{24,12},{28,16},{1,21},{... | collective-permute-start | bytes 589832 | tf_op jit(solution)/shard_map/ppermute | solution.py:269
  24.7 3.3 %collective-permute-start.3 = (bf16[1664,256]{1,0:T(8,128)(2,1)S(1)}, bf16[1664,256]{1,0:T(8,128)(2,1)S(1)}, u32[]{:S(2)}, u32[]{:S(2)}) collective-permute-start(bf16[1664,256]{1,0:T(8,128)(2,1)S(1)} %get-tuple-element.29), channel_id=1, source_target_pairs={{0,4},{4,0},{8,12},{12,8},{16,20},{20,16},{24,28},{28,24},{1,5},{5... | collective-permute-start | bytes 2555912 | tf_op jit(solution)/shard_map/ppermute | solution.py:260
  24.9 3.4 %collective-permute-start.4 = (bf16[1664,256]{1,0:T(8,128)(2,1)S(1)}, bf16[1664,256]{1,0:T(8,128)(2,1)S(1)}, u32[]{:S(2)}, u32[]{:S(2)}) collective-permute-start(bf16[1664,256]{1,0:T(8,128)(2,1)S(1)} %get-tuple-element.30), channel_id=1, source_target_pairs={{0,4},{4,0},{8,12},{12,8},{16,20},{20,16},{24,28},{28,24},{1,5},{5... | collective-permute-start | bytes 2555912 | tf_op jit(solution)/shard_map/ppermute | solution.py:260
  30.6 8.1 %collective-permute-start.10 = (bf16[128,384]{1,0:T(8,128)(2,1)S(1)}, bf16[128,384]{1,0:T(8,128)(2,1)S(1)}, u32[]{:S(2)}, u32[]{:S(2)}) collective-permute-start(bf16[128,384]{1,0:T(8,128)(2,1)S(1)} %get-tuple-element.37), channel_id=1, source_target_pairs={{0,28},{4,24},{8,20},{12,16},{16,12},{20,8},{24,4},{28,0},{1,29},{... | collective-permute-start | bytes 294920 | tf_op jit(solution)/shard_map/ppermute | solution.py:269
  35.8 4.1 %collective-permute-start.8 = (bf16[128,384]{1,0:T(8,128)(2,1)S(1)}, bf16[128,384]{1,0:T(8,128)(2,1)S(1)}, u32[]{:S(2)}, u32[]{:S(2)}) collective-permute-start(bf16[128,384]{1,0:T(8,128)(2,1)S(1)} %get-tuple-element.35), channel_id=1, source_target_pairs={{0,12},{4,16},{8,28},{12,0},{16,4},{20,24},{24,20},{28,8},{1,13},{... | collective-permute-start | bytes 294920 | tf_op jit(solution)/shard_map/ppermute | solution.py:269
  36.8 4.8 %collective-permute-start.7 = (bf16[128,384]{1,0:T(8,128)(2,1)S(1)}, bf16[128,384]{1,0:T(8,128)(2,1)S(1)}, u32[]{:S(2)}, u32[]{:S(2)}) collective-permute-start(bf16[128,384]{1,0:T(8,128)(2,1)S(1)} %get-tuple-element.33), channel_id=1, source_target_pairs={{0,20},{4,8},{8,4},{12,24},{16,28},{20,0},{24,12},{28,16},{1,21},{... | collective-permute-start | bytes 294920 | tf_op jit(solution)/shard_map/ppermute | solution.py:269
  41.6 12.6 %copy-start = (f32[3072]{0:T(1024)S(1)}, f32[3072]{0:T(1024)}, u32[]{:S(2)}) copy-start(f32[3072]{0:T(1024)} %param.20) | copy-start | bytes 36868
  42.2 1.4 %collective-permute-start.11 = (f32[1,3072]{1,0:T(1,128)S(1)}, f32[1,3072]{1,0:T(1,128)S(1)}, u32[]{:S(2)}, u32[]{:S(2)}) collective-permute-start(f32[1,3072]{1,0:T(1,128)S(1)} %get-tuple-element.41.refs_1_), channel_id=1, source_target_pairs={{0,4},{1,5},{2,6},{3,7},{4,0},{5,1},{6,2},{7,3},{8,12},{9,13},{10,... | collective-permute-start | bytes 36872 | tf_op jit(solution)/shard_map/ppermute | solution.py:236
  43.6 4.0 %collective-permute-start.12 = (f32[1,3072]{1,0:T(1,128)S(1)}, f32[1,3072]{1,0:T(1,128)S(1)}, u32[]{:S(2)}, u32[]{:S(2)}) collective-permute-start(f32[1,3072]{1,0:T(1,128)S(1)} %sum.4.refs_3_), channel_id=1, source_target_pairs={{0,28},{1,29},{2,30},{3,31},{4,24},{5,25},{6,26},{7,27},{8,20},{9,... | collective-permute-start | bytes 36872 | tf_op jit(solution)/shard_map/ppermute | solution.py:236
  45.4 3.1 %collective-permute-start.13 = (f32[1,3072]{1,0:T(1,128)S(1)}, f32[1,3072]{1,0:T(1,128)S(1)}, u32[]{:S(2)}, u32[]{:S(2)}) collective-permute-start(f32[1,3072]{1,0:T(1,128)S(1)} %sum.4.refs_3_), channel_id=1, source_target_pairs={{0,20},{1,21},{2,22},{3,23},{4,16},{5,17},{6,18},{7,19},{8,28},{9,... | collective-permute-start | bytes 36872 | tf_op jit(solution)/shard_map/ppermute | solution.py:236
  45.5 3.1 %collective-permute-start.14 = (f32[1,3072]{1,0:T(1,128)S(1)}, f32[1,3072]{1,0:T(1,128)S(1)}, u32[]{:S(2)}, u32[]{:S(2)}) collective-permute-start(f32[1,3072]{1,0:T(1,128)S(1)} %sum.4.refs_3_), channel_id=1, source_target_pairs={{0,12},{1,13},{2,14},{3,15},{4,8},{5,9},{6,10},{7,11},{8,4},{9,5},... | collective-permute-start | bytes 36872 | tf_op jit(solution)/shard_map/ppermute | solution.py:236
  48.6 3.1 %collective-permute-start.15 = (f32[1,3072]{1,0:T(1,128)S(1)}, f32[1,3072]{1,0:T(1,128)S(1)}, u32[]{:S(2)}, u32[]{:S(2)}) collective-permute-start(f32[1,3072]{1,0:T(1,128)S(1)} %sum.5.refs_1_), channel_id=1, source_target_pairs={{0,5},{1,4},{2,7},{3,6},{4,1},{5,0},{6,3},{7,2},{8,13},{9,12},{10,... | collective-permute-start | bytes 36872 | tf_op jit(solution)/shard_map/ppermute | solution.py:236
  51.8 4.0 %collective-permute-start.16 = (f32[1,3072]{1,0:T(1,128)S(1)}, f32[1,3072]{1,0:T(1,128)S(1)}, u32[]{:S(2)}, u32[]{:S(2)}) collective-permute-start(f32[1,3072]{1,0:T(1,128)S(1)} %sum.6.refs_1_), channel_id=1, source_target_pairs={{0,6},{1,7},{2,4},{3,5},{4,2},{5,3},{6,0},{7,1},{8,14},{9,15},{10,... | collective-permute-start | bytes 36872 | tf_op jit(solution)/shard_map/ppermute | solution.py:236
